TPU v7x, 128 devices: a whole 4x4x4 slice. The times are simulated.
128 devices in a mesh: gx: 16 (over z, x), gy: 8 (over y, core).
Axes of the slice: x: 4, y: 4, z: 4, core: 2. Of those that a mesh axis runs over, the one named last changes fastest.
Arguments:
- pressure: float32 [262144, 512], P(('gx', 'gy')), may hold values from -3 to -0.05
- soil_class: int32 [262144], P(('gx', 'gy')), may hold values from 0 to 11
- levels: int32 [262144], P(('gx', 'gy')), may hold values from 0 to 2
- neighbors: int32 [262144, 6], P(('gx', 'gy')), may hold values from -1 to 262143, as said below
- neighbor_levels: int32 [262144, 6], P(('gx', 'gy')), may hold values from 0 to 2, as said below
- patch_of_block: int32 [262144], P(('gx', 'gy')), may hold values from -1 to 65535, as said below
- soil_params: float32 [5, 12], replicated, as said below
- water_depth: float32 [2048, 2048], P('gx', 'gy'), may hold values from 0.0001 to 0.3
- bed_height: float32 [2048, 2048], P('gx', 'gy'), may hold values from -1 to 1
- roughness: float32 [2048, 2048], P('gx', 'gy'), may hold values from 0.02 to 0.2
Outputs:
- new_pressure: float32 [262144, 512], P(('gx', 'gy'))
- new_depth: float32 [2048, 2048], P('gx', 'gy')
Inputs may be any that keep to these rules, and one draw needn't show every extreme that they name: `patch_of_block`: every surface patch lies over exactly one block. The blocks under the patches of device d belong to the devices d - 8 to d + 16 / 2 - 1 (flat index gx index * 8 + gy index, modulo the device count). Among the blocks of one device at most 64 lie under the patches of any one device, and every device has exactly 64 patches over the blocks of some one device. `neighbors`: symmetric face relation (b's +x neighbour has b as its -x neighbour, likewise y and z); neighbour numbers differ from the block's by at most 256, and by exactly 256 for some; neighbours' levels differ by at most one; blocks with a patch have no +z neighbour. `neighbor_levels`: the level of the neighbour across each face, 0 where there is none. `soil_params`: 0.02 <= theta_r <= 0.1, 0.35 <= theta_s <= 0.5, 0.5 <= alpha <= 5, 1.3 <= n <= 2.8, 0.02 <= Ks <= 1.
All inputs are finite; a program needn't handle non-finite values.
Results may differ from a plain program's by a relative error of at most 0.0003.
Values sent between devices are 32-bit elements; how exact they have to be, the bound alone decides.
No kernel may reach another device: no remote copies, remote signals or barrier semaphores. Data moves between devices by JAX's collectives and lax.ppermute only.
A program may use at most 192 MiB of HBM per device.

v0:
```python
import jax
import jax.numpy as jnp
from jax import lax
from jax.experimental import pallas as pl
from jax.experimental.pallas import tpu as pltpu
from jax.sharding import PartitionSpec as P

F32 = jnp.float32
BF16 = jnp.bfloat16
I32 = jnp.int32

HB = 256
TILE = 256
SLOTS = 64
GROUPS = 16
STORAGE = 0.05
SUB_STEP = 0.02
SURF_STEP = 0.003
SLOPE_FLOOR = 0.01
OPPOSITE = (1, 0, 3, 2, 5, 4)
GRAVITY = (0.0, 0.0, 0.0, 0.0, -1.0, 1.0)
MIB = 1024 * 1024

VMEM = pl.BlockSpec(memory_space=pltpu.VMEM)
SMEM = pl.BlockSpec(memory_space=pltpu.SMEM)


def split(value):
    high = value.astype(BF16)
    low = (value - high.astype(F32)).astype(BF16)
    return high, low


def iota(shape, dim):
    return lax.broadcasted_iota(I32, shape, dim)


def as_bf16(mask):
    return jnp.where(mask, 1.0, 0.0).astype(BF16)


def cell_width(levels):
    return jnp.where(levels == 0, 0.25, jnp.where(levels == 1, 0.5, 1.0)).astype(F32)


def soil_rows(soil_ref, classes):
    rows = []
    for row in range(5):
        value = jnp.full(classes.shape, soil_ref[row, 0], F32)
        for cls in range(1, soil_ref.shape[1]):
            value = jnp.where(classes == cls, soil_ref[row, cls], value)
        rows.append(value)
    residual, saturated, alpha, power, cond = rows
    exponent = 1.0 - 1.0 / power
    return alpha, power - 1.0, -0.5 * exponent, cond, (saturated - residual) * alpha * (exponent * power)


def curve(pressure, soil):
    alpha, lesser, half, _, _ = soil
    suction = alpha * jnp.maximum(-pressure, 0.0)
    powered = jnp.exp2(lesser * jnp.log2(suction))
    base = 1.0 + powered * suction
    root = jnp.exp2(half * jnp.log2(base))
    ratio = powered * (root * root)
    rest = 1.0 - ratio
    conductivity = soil[3] * root * (rest * rest)
    return conductivity, base, ratio


def face_rows(ref, half, face):
    if face < 2:
        return ref[half, pl.ds(7 * face, 64, stride=8), :]
    if face < 4:
        start = 56 * (face - 2)
        return jnp.concatenate([ref[half, 64 * k + start : 64 * k + start + 8, :] for k in range(8)], axis=0)
    start = 448 * (face - 4)
    return ref[half, start : start + 64, :]


def write_faces(head_ref, cond_ref, half, put):
    for face in range(6):
        head_high, head_low = split(face_rows(head_ref, half, face))
        cond_high, cond_low = split(face_rows(cond_ref, half, face))
        for part, value in enumerate((head_high, head_low, cond_high, cond_low)):
            put(256 * face + 64 * part, half, value)


def route_kernel(place_ref, meta_ref, top_ref, depth_ref, bed_ref, rough_ref,
                 send_ref, slot_ref, rows_ref, turned, packed, edges):
    own, gy = place_ref[0], place_ref[2]
    devices, width = place_ref[3], place_ref[4]
    blocks = meta_ref.shape[1]
    patch = meta_ref[2:3, :]
    is_top = patch >= 0
    safe = jnp.where(is_top, patch, 0)
    offset = lax.rem(lax.shift_right_logical(safe, 9) - own + (GROUPS // 2 - 1) + devices, devices) - (GROUPS // 2 - 1)
    column = gy + offset
    moved = (column < 0) | (column >= width)
    group = 2 * lax.rem(column + width, width) + moved.astype(I32)
    upper = as_bf16(iota((TILE, TILE), 0) < iota((TILE, TILE), 1))
    carry = jnp.zeros((GROUPS, 1), F32)
    for part in range(blocks // TILE):
        lanes = slice(part * TILE, (part + 1) * TILE)
        member = jnp.where(
            (iota((GROUPS, TILE), 0) == group[:, lanes]) & is_top[:, lanes], 1.0, 0.0
        )
        before = jnp.dot(member.astype(BF16), upper, preferred_element_type=F32) + carry
        rank = jnp.sum(member * before, axis=0, keepdims=True)
        carry = carry + jnp.sum(member, axis=1, keepdims=True)
        slot_ref[:, lanes] = jnp.where(
            is_top[:, lanes], group[:, lanes] * SLOTS + rank.astype(I32), -1
        )
        for half in (2 * part, 2 * part + 1):
            turned[half] = top_ref[128 * half : 128 * half + 128, :].T
    for half in range(blocks // 128):
        lanes = slice(128 * half, 128 * half + 128)
        heads = jnp.concatenate(
            [turned[half, pl.ds(64 + i, 8, stride=8), :] for i in range(8)], axis=0
        )
        high, low = split(heads)
        packed[0:64, lanes] = high
        packed[64:128, lanes] = low
    place = jnp.bitwise_and(safe, 511)
    row = iota((16, blocks), 0)
    tags = jnp.where(row == 0, jnp.bitwise_and(place, 255), 0)
    tags = jnp.where(row == 1, lax.shift_right_logical(place, 8), tags)
    tags = jnp.where(row == 2, 1, tags)
    tags = jnp.where(row == 3, meta_ref[0:1, :], tags)
    tags = jnp.where(row == 4, meta_ref[1:2, :], tags)
    packed[128:144, :] = tags.astype(F32).astype(BF16)
    for number, field in enumerate((depth_ref, bed_ref, rough_ref)):
        edges[0, 3 * number : 3 * number + 3, :] = field[:, 0:128].T[0:3, :]
        edges[1, 3 * number : 3 * number + 3, :] = field[:, 128:256].T[125:128, :]
        for half in range(2):
            at = 3 * (2 * number + half)
            lanes = slice(128 * half, 128 * half + 128)
            rows_ref[0, at : at + 3, :] = field[0:3, lanes]
            rows_ref[1, at : at + 3, :] = field[125:128, lanes]
    low_lane = iota((32, 128), 1) < 64
    slot = slot_ref[...]

    def chunk(number, _):
        wanted = as_bf16(iota((128, blocks), 0) + 128 * number == slot)
        out = lax.dot_general(packed[...], wanted, (((1,), (1,)), ((), ())), preferred_element_type=F32)
        first = out[0:32] + out[64:96]
        second = out[32:64] + out[96:128]
        send_ref[number, 0:32, :] = jnp.where(low_lane, first, pltpu.roll(second, 64, 1))
        send_ref[number, 32:64, :] = jnp.where(low_lane, pltpu.roll(first, 64, 1), second)
        label = out[130:131] * (out[128:129] + 256.0 * out[129:130] + 1.0) - 1.0
        row = iota((8, 128), 0)
        send_ref[number, 64:72, :] = jnp.where(
            row == 0, label, jnp.where(row == 1, out[131:132], out[132:133])
        )
        send_ref[number, 72:88, :] = jnp.where(number == gy + 1, edges[1], edges[0])
        return 0

    lax.fori_loop(0, send_ref.shape[0], chunk, 0)


def route(place, meta, pressure, water_depth, bed_height, roughness, width):
    blocks = meta.shape[1]
    return pl.pallas_call(
        route_kernel,
        grid=(1,),
        in_specs=[
            SMEM,
            pl.BlockSpec(meta.shape, lambda t: (0, 0)),
            pl.BlockSpec((blocks, 128), lambda t: (0, 3)),
            pl.BlockSpec(water_depth.shape, lambda t: (0, 0)),
            pl.BlockSpec(water_depth.shape, lambda t: (0, 0)),
            pl.BlockSpec(water_depth.shape, lambda t: (0, 0)),
        ],
        out_specs=[
            pl.BlockSpec((width, 88, 128), lambda t: (0, 0, 0)),
            pl.BlockSpec((1, blocks), lambda t: (0, 0)),
            pl.BlockSpec((2, 24, 128), lambda t: (0, 0, 0)),
        ],
        out_shape=[
            jax.ShapeDtypeStruct((width, 88, 128), F32),
            jax.ShapeDtypeStruct((1, blocks), I32),
            jax.ShapeDtypeStruct((2, 24, 128), F32),
        ],
        scratch_shapes=[
            pltpu.VMEM((blocks // 128, 128, 128), F32),
            pltpu.VMEM((144, blocks), BF16),
            pltpu.VMEM((2, 16, 128), F32),
        ],
        compiler_params=pltpu.CompilerParams(vmem_limit_bytes=40 * MIB),
        name="route",
    )(place, meta, pressure, water_depth, bed_height, roughness)


def surface_kernel(place_ref, soil_ref, got_ref, up_ref, down_ref, depth_ref,
                   stay_ref, back_ref, tile_ref, cols_ref, packed, labels, match):
    gy = place_ref[2]
    low_lane = iota((32, 128), 1) < 64
    tag_low = iota((8, 128), 1) < 64
    width = got_ref.shape[0]
    slots = width * 128
    patches = match.shape[0]
    for source in range(width):
        lanes = slice(128 * source, 128 * source + 128)
        at = 40 * source
        from_up = source >= gy
        stay = got_ref[source, 0:32, :]
        moved = jnp.where(from_up, up_ref[at : at + 32, :], down_ref[at : at + 32, :])
        high, low = split(jnp.where(low_lane, stay, pltpu.roll(moved, 64, 1)))
        packed[0:32, lanes] = high
        packed[64:96, lanes] = low
        high, low = split(jnp.where(low_lane, pltpu.roll(stay, 64, 1), moved))
        packed[32:64, lanes] = high
        packed[96:128, lanes] = low
        tags = jnp.where(
            tag_low,
            got_ref[source, 64:72, :],
            jnp.where(from_up, up_ref[at + 32 : at + 40, :], down_ref[at + 32 : at + 40, :]),
        )
        labels[:, lanes] = (tags[0:1, :] + 0.5).astype(I32) - jnp.where(tags[0:1, :] < 0, 1, 0)
        row = iota((16, 128), 0)
        packed[128:144, lanes] = jnp.where(row == 0, tags[1:2, :], tags[2:3, :]).astype(BF16)
    for part in range(patches // 128):
        match[128 * part : 128 * part + 128, :] = as_bf16(
            iota((128, slots), 0) + 128 * part == labels[...]
        )
    placed = lax.dot_general(
        packed[...], match[...], (((1,), (1,)), ((), ())), preferred_element_type=F32
    )
    classes = (placed[128:129] + 0.5).astype(I32)
    levels = (placed[129:130] + 0.5).astype(I32)
    soil = soil_rows(soil_ref, classes)
    half_cell = 0.5 * cell_width(levels)
    head = placed[0:64] + placed[64:128]
    conductivity, _, _ = curve(head, soil)
    row_of = lax.shift_right_logical(iota((128, patches), 0), 3)
    own_row = row_of == lax.shift_right_logical(iota((128, patches), 1), 5)
    depth_high, depth_low = split(depth_ref[...])
    depth_both = jnp.concatenate([depth_high, depth_low], axis=0)
    cols = depth_ref.shape[1]
    pieces = []
    for i in range(8):
        pick = as_bf16(iota((cols, patches), 0) == 8 * jnp.bitwise_and(iota((cols, patches), 1), 31) + i)
        spread = jnp.dot(depth_both, pick, preferred_element_type=F32)
        spread = jnp.where(own_row, spread[0:128] + spread[128:256], 0.0)
        pieces.append(jnp.sum(spread.reshape(16, 8, patches), axis=0))
    depth = jnp.concatenate(pieces, axis=0)
    infiltration = jnp.minimum(
        conductivity / half_cell * (depth - (head - half_cell)), depth / (3.0 * SURF_STEP)
    )
    high, low = split(infiltration)
    both = jnp.concatenate([high, low], axis=0)
    answer = jnp.dot(both, match[...], preferred_element_type=F32)
    answer = answer[0:64] + answer[64:128]
    for source in range(width):
        lanes = slice(128 * source, 128 * source + 128)
        first, second = answer[0:32, lanes], answer[32:64, lanes]
        stay_ref[source] = jnp.where(low_lane, first, pltpu.roll(second, 64, 1))
        moved = jnp.where(low_lane, pltpu.roll(first, 64, 1), second)
        back_ref[0, 32 * source : 32 * source + 32, :] = moved
        back_ref[1, 32 * source : 32 * source + 32, :] = moved
    total = jnp.zeros(depth_ref.shape, F32)
    for i in range(8):
        pick = as_bf16(iota((patches, cols), 1) == 8 * jnp.bitwise_and(iota((patches, cols), 0), 31) + i)
        rows = jnp.concatenate([infiltration[8 * i : 8 * i + 8]] * 16, axis=0)
        high, low = split(jnp.where(own_row, rows, 0.0))
        spread = jnp.dot(jnp.concatenate([high, low], axis=0), pick, preferred_element_type=F32)
        total = total + (spread[0:128] + spread[128:256])
    tile_ref[...] = total
    base = 32 * width
    for half in range(2):
        lanes = slice(128 * half, 128 * half + 128)
        back_ref[0, base + 2 * half : base + 2 * half + 2, :] = total[0:2, lanes]
        back_ref[1, base + 2 * half : base + 2 * half + 2, :] = total[126:128, lanes]
    cols_ref[0, 0:2, :] = total[:, 0:128].T[0:2, :]
    cols_ref[1, 0:2, :] = total[:, 128:256].T[126:128, :]


def surface(place, soil, got, up, down, water_depth, patches):
    width = got.shape[0]
    return pl.pallas_call(
        surface_kernel,
        in_specs=[SMEM, SMEM, VMEM, VMEM, VMEM, VMEM],
        out_specs=[VMEM, VMEM, VMEM, VMEM],
        out_shape=[
            jax.ShapeDtypeStruct((width, 32, 128), F32),
            jax.ShapeDtypeStruct((2, 32 * width + 8, 128), F32),
            jax.ShapeDtypeStruct(water_depth.shape, F32),
            jax.ShapeDtypeStruct((2, 8, 128), F32),
        ],
        scratch_shapes=[
            pltpu.VMEM((144, width * 128), BF16),
            pltpu.VMEM((1, width * 128), I32),
            pltpu.VMEM((patches, width * 128), BF16),
        ],
        compiler_params=pltpu.CompilerParams(vmem_limit_bytes=40 * MIB),
        name="surface",
    )(place, soil, got, up, down, water_depth)


def sweep_kernel(place_ref, depth_ref, bed_ref, rough_ref, left_ref, right_ref, up_ref, down_ref,
                 source_ref, above_ref, below_ref, west_ref, east_ref,
                 out_ref, depth_ext, bed_ext, rough_ext, source_ext, turn):
    gx, gy = place_ref[1], place_ref[2]
    rows_total, cols_total = place_ref[5], place_ref[6]
    shape = depth_ext.shape
    depth_ext[...] = jnp.zeros(shape, F32)
    bed_ext[...] = jnp.zeros(shape, F32)
    rough_ext[...] = jnp.ones(shape, F32)
    source_ext[...] = jnp.zeros(shape, F32)
    for number, (ext, field) in enumerate(
        ((depth_ext, depth_ref), (bed_ext, bed_ref), (rough_ext, rough_ref))
    ):
        ext[8:136, 128:384] = field[...]
        for half in range(2):
            at = 3 * (2 * number + half)
            lanes = slice(128 + 128 * half, 256 + 128 * half)
            ext[5:8, lanes] = up_ref[at : at + 3, :]
            ext[136:139, lanes] = down_ref[at : at + 3, :]
        col = 3 * number
        fill = 1.0 if number == 2 else 0.0
        for side, lanes in ((0, slice(0, 128)), (1, slice(384, 512))):
            to = slice(125, 128) if side == 0 else slice(0, 3)
            center_ref = left_ref if side == 0 else right_ref
            away = 24 + 16 * side + col
            turn[...] = jnp.full((128, 128), fill, F32)
            turn[to, :] = center_ref[col : col + 3, :]
            ext[8:136, lanes] = turn[...].T
            turn[to, :] = up_ref[away : away + 3, :]
            ext[0:8, lanes] = turn[...].T[120:128, :]
            turn[to, :] = down_ref[away : away + 3, :]
            ext[136:144, lanes] = turn[...].T[0:8, :]
    source_ext[8:136, 128:384] = source_ref[...]
    for half in range(2):
        lanes = slice(128 + 128 * half, 256 + 128 * half)
        source_ext[6:8, lanes] = above_ref[2 * half : 2 * half + 2, :]
        source_ext[136:138, lanes] = below_ref[2 * half : 2 * half + 2, :]
    for side, lanes in ((0, slice(0, 128)), (1, slice(384, 512))):
        to = slice(126, 128) if side == 0 else slice(0, 2)
        ref = west_ref if side == 0 else east_ref
        turn[...] = jnp.zeros((128, 128), F32)
        turn[to, :] = ref[0:2, :]
        source_ext[8:136, lanes] = turn[...].T
        source_ext[6:8, lanes] = ref[2:4, :]
        source_ext[136:138, lanes] = ref[4:6, :]
    row_id = gx * depth_ref.shape[0] - 8 + iota(shape, 0)
    col_id = gy * depth_ref.shape[1] - 128 + iota(shape, 1)
    row_open = (row_id >= 0) & (row_id + 1 < rows_total)
    col_open = (col_id >= 0) & (col_id + 1 < cols_total)
    bed = bed_ext[...]
    rough = rough_ext[...]
    inverse = {
        0: jnp.where(row_open, 2.0 / (rough + pltpu.roll(rough, shape[0] - 1, 0)), 0.0),
        1: jnp.where(col_open, 2.0 / (rough + pltpu.roll(rough, shape[1] - 1, 1)), 0.0),
    }
    head = depth_ext[...]
    source = source_ext[...]
    for _ in range(3):
        wet = jnp.maximum(head, 0.0)
        section = head + bed
        net = jnp.zeros(shape, F32) - source
        for axis in range(2):
            back = shape[axis] - 1
            slope = pltpu.roll(section, back, axis) - section
            mean = 0.5 * (wet + pltpu.roll(wet, back, axis))
            flux = (
                jnp.exp2((5.0 / 3.0) * jnp.log2(mean))
                * inverse[axis]
                * slope
                * lax.rsqrt(jnp.abs(slope) + SLOPE_FLOOR)
            )
            net = net + flux - pltpu.roll(flux, 1, axis)
        head = head + SURF_STEP * net
    out_ref[...] = head[8:136, 128:384]


def sweeps(place, water_depth, bed_height, roughness, left, right, up, down, source, above, below, west, east):
    shape = (144, 512)
    return pl.pallas_call(
        sweep_kernel,
        in_specs=[SMEM] + [VMEM] * 12,
        out_specs=VMEM,
        out_shape=jax.ShapeDtypeStruct(water_depth.shape, F32),
        scratch_shapes=[pltpu.VMEM(shape, F32)] * 4 + [pltpu.VMEM((128, 128), F32)],
        compiler_params=pltpu.CompilerParams(vmem_limit_bytes=40 * MIB),
        name="sweeps",
    )(place, water_depth, bed_height, roughness, left, right, up, down, source, above, below, west, east)


def inside_kernel(soil_ref, meta_ref, head_ref, base_ref, factor_ref, table_ref, turned, cond):
    open_i = iota((8, 8, 128), 1) < 7
    nothing = jnp.zeros((1, 8, 128), F32)
    for half in range(head_ref.shape[0] // 128):
        lanes = slice(128 * half, 128 * half + 128)
        turned[half] = head_ref[lanes, :].T
        soil = soil_rows(soil_ref, meta_ref[0:1, lanes])
        width = cell_width(meta_ref[1:2, lanes])
        half_over = 0.5 / width
        scaled = SUB_STEP / width
        for k in range(8):
            rows = slice(64 * k, 64 * k + 64)
            conductivity, base, ratio = curve(turned[half, rows, :], soil)
            cond[half, rows, :] = conductivity
            factor_ref[half, rows, :] = scaled / (soil[4] * ratio / base + STORAGE)
        below = None
        for k in range(8):
            rows = slice(64 * k, 64 * k + 64)
            head = turned[half, rows, :].reshape(8, 8, 128)
            cnd = cond[half, rows, :].reshape(8, 8, 128)
            flux = (cnd + pltpu.roll(cnd, 7, 1)) * (pltpu.roll(head, 7, 1) - head) * half_over
            flux = jnp.where(open_i, flux, 0.0)
            inflow = flux - pltpu.roll(flux, 1, 1)
            flux = (cnd[1:] + cnd[:-1]) * (head[1:] - head[:-1]) * half_over
            inflow = inflow + jnp.concatenate([flux, nothing], 0) - jnp.concatenate([nothing, flux], 0)
            if k < 7:
                above = slice(64 * k + 64, 64 * k + 128)
                head_up = turned[half, above, :].reshape(8, 8, 128)
                cnd_up = cond[half, above, :].reshape(8, 8, 128)
                flux = (cnd + cnd_up) * ((head_up - head) * half_over + 0.5)
                inflow = inflow + flux
            if below is not None:
                inflow = inflow - below
            below = flux
            base_ref[half, rows, :] = (
                turned[half, rows, :] + factor_ref[half, rows, :] * inflow.reshape(64, 128)
            )

    def put(row, half, value):
        table_ref[row : row + 64, 128 * half : 128 * half + 128] = value

    for half in range(head_ref.shape[0] // 128):
        write_faces(turned, cond, half, put)


def inside(soil, meta, pressure):
    blocks = pressure.shape[0]
    return pl.pallas_call(
        inside_kernel,
        grid=(blocks // TILE,),
        in_specs=[
            SMEM,
            pl.BlockSpec((16, TILE), lambda t: (0, t)),
            pl.BlockSpec((TILE, 512), lambda t: (t, 0)),
        ],
        out_specs=[
            pl.BlockSpec((TILE // 128, 512, 128), lambda t: (t, 0, 0)),
            pl.BlockSpec((TILE // 128, 512, 128), lambda t: (t, 0, 0)),
            pl.BlockSpec((1536, TILE), lambda t: (0, t)),
        ],
        out_shape=[
            jax.ShapeDtypeStruct((blocks // 128, 512, 128), F32),
            jax.ShapeDtypeStruct((blocks // 128, 512, 128), F32),
            jax.ShapeDtypeStruct((1536, blocks), BF16),
        ],
        scratch_shapes=[pltpu.VMEM((TILE // 128, 512, 128), F32)] * 2,
        compiler_params=pltpu.CompilerParams(vmem_limit_bytes=40 * MIB),
        name="inside",
    )(soil, meta, pressure)


def across_kernel(place_ref, soil_ref, meta_ref, low_ref, high_ref, base_ref, factor_ref, table_ref,
                  out_ref, table, turned, cond, arrived):
    step = pl.program_id(0)
    blocks = table_ref.shape[1]
    own_lanes = pl.ds(HB, blocks)

    @pl.when(step == 0)
    def _():
        copy = pltpu.make_async_copy(table_ref, table.at[:, own_lanes], arrived)
        copy.start()
        for number, ref in enumerate((low_ref, high_ref)):
            start = 0 if number == 0 else HB + blocks

            def put(row, half, value):
                table[row : row + 64, start + 128 * half : start + 128 * half + 128] = value

            for half in range(HB // 128):
                lanes = slice(128 * half, 128 * half + 128)
                turned[half] = ref[lanes, :].T
                classes = ref[HB : HB + 8, lanes][0:1, :].astype(I32)
                soil = soil_rows(soil_ref, classes)
                for k in range(8):
                    rows = slice(64 * k, 64 * k + 64)
                    cond[half, rows, :] = curve(turned[half, rows, :], soil)[0]
                write_faces(turned, cond, half, put)
        copy.wait()

    turned[...] = base_ref[...]
    window = pl.ds(pl.multiple_of(step * TILE, TILE), TILE + 2 * HB)
    own = pl.ds(pl.multiple_of(step * TILE + HB, TILE), TILE)
    width = cell_width(meta_ref[1:2, :])
    first_row = place_ref[0] * blocks - HB + step * TILE
    for face in range(6):
        neighbor = meta_ref[3 + face : 4 + face, :]
        far_width = cell_width(meta_ref[9 + face : 10 + face, :])
        over_gap = 2.0 / (width + far_width)
        half = jnp.where(neighbor >= 0, 0.5, 0.0)
        chosen = as_bf16(iota((TILE + 2 * HB, TILE), 0) == neighbor - first_row)
        there = 256 * OPPOSITE[face]
        far = jnp.dot(table[there : there + 256, window], chosen, preferred_element_type=F32)
        near = table[256 * face : 256 * face + 256, own].astype(F32)
        head_diff = (far[0:64] - near[0:64]) + (far[64:128] - near[64:128])
        conds = (far[128:192] + near[128:192]) + (far[192:256] + near[192:256])
        flux = conds * half * (head_diff * over_gap + GRAVITY[face])
        for part in range(TILE // 128):
            added = flux[:, 128 * part : 128 * part + 128]
            if face < 2:
                rows = pl.ds(7 * face, 64, stride=8)
                turned[part, rows, :] += factor_ref[part, rows, :] * added
            elif face < 4:
                for k in range(8):
                    at = slice(64 * k + 56 * (face - 2), 64 * k + 56 * (face - 2) + 8)
                    turned[part, at, :] += factor_ref[part, at, :] * added[8 * k : 8 * k + 8]
            else:
                at = slice(448 * (face - 4), 448 * (face - 4) + 64)
                turned[part, at, :] += factor_ref[part, at, :] * added
    for part in range(TILE // 128):
        out_ref[128 * part : 128 * part + 128, :] = turned[part].T


def across(place, soil, meta, low, high, base, factor, table):
    blocks = table.shape[1]
    return pl.pallas_call(
        across_kernel,
        grid=(blocks // TILE,),
        in_specs=[
            SMEM,
            SMEM,
            pl.BlockSpec((16, TILE), lambda t: (0, t)),
            pl.BlockSpec(low.shape, lambda t: (0, 0)),
            pl.BlockSpec(high.shape, lambda t: (0, 0)),
            pl.BlockSpec((TILE // 128, 512, 128), lambda t: (t, 0, 0)),
            pl.BlockSpec((TILE // 128, 512, 128), lambda t: (t, 0, 0)),
            pl.BlockSpec(memory_space=pl.ANY),
        ],
        out_specs=pl.BlockSpec((TILE, 512), lambda t: (t, 0)),
        out_shape=jax.ShapeDtypeStruct((blocks, 512), F32),
        scratch_shapes=[
            pltpu.VMEM((1536, blocks + 2 * HB), BF16),
            pltpu.VMEM((TILE // 128, 512, 128), F32),
            pltpu.VMEM((TILE // 128, 512, 128), F32),
            pltpu.SemaphoreType.DMA,
        ],
        compiler_params=pltpu.CompilerParams(vmem_limit_bytes=48 * MIB),
        name="across",
    )(place, soil, meta, low, high, base, factor, table)


def top_kernel(got_ref, slot_ref, factor_ref, head_ref, out_ref, packed, turned):
    low_lane = iota((32, 128), 1) < 64
    width = got_ref.shape[0]
    slots = width * 128

    @pl.when(pl.program_id(0) == 0)
    def _():
        for number in range(width):
            lanes = slice(128 * number, 128 * number + 128)
            stay, moved = got_ref[number, 0:32, :], got_ref[number, 32:64, :]
            high, low = split(jnp.where(low_lane, stay, pltpu.roll(moved, 64, 1)))
            packed[0:32, lanes] = high
            packed[64:96, lanes] = low
            high, low = split(jnp.where(low_lane, pltpu.roll(stay, 64, 1), moved))
            packed[32:64, lanes] = high
            packed[96:128, lanes] = low

    blocks = slot_ref.shape[1]
    wanted = as_bf16(iota((slots, blocks), 0) == slot_ref[...])
    flux = jnp.dot(packed[...], wanted, preferred_element_type=F32)
    flux = flux[0:64] + flux[64:128]
    for part in range(blocks // 128):
        lanes = slice(128 * part, 128 * part + 128)
        turned[part, 0:64, :] = jnp.zeros((64, 128), F32)
        for i in range(8):
            turned[part, pl.ds(64 + i, 8, stride=8), :] = flux[8 * i : 8 * i + 8, lanes]
        turned[part, 64:128, :] = turned[part, 64:128, :] * factor_ref[part]
        out_ref[lanes, :] = head_ref[lanes, :] + turned[part].T


def top(got, slot, factor, head):
    blocks = head.shape[0]
    part = 2 * TILE
    return pl.pallas_call(
        top_kernel,
        grid=(blocks // part,),
        in_specs=[
            pl.BlockSpec(got.shape, lambda t: (0, 0, 0)),
            pl.BlockSpec((1, part), lambda t: (0, t)),
            pl.BlockSpec((part // 128, 64, 128), lambda t: (t, 7, 0)),
            pl.BlockSpec((part, 128), lambda t: (t, 3)),
        ],
        out_specs=pl.BlockSpec((part, 128), lambda t: (t, 3)),
        out_shape=jax.ShapeDtypeStruct(head.shape, F32),
        input_output_aliases={3: 0},
        scratch_shapes=[
            pltpu.VMEM((128, got.shape[0] * 128), BF16),
            pltpu.VMEM((part // 128, 128, 128), F32),
        ],
        compiler_params=pltpu.CompilerParams(vmem_limit_bytes=40 * MIB),
        name="top",
    )(got, slot, factor, head)


def shifted(value, axis, steps, wrap=True):
    count = lax.axis_size(axis)
    pairs = [(i, (i + steps) % count) for i in range(count) if wrap or 0 <= i + steps < count]
    return lax.ppermute(value, axis, pairs)


def per_device(pressure, soil_class, levels, neighbors, neighbor_levels, patch_of_block, soil_params,
               water_depth, bed_height, roughness):
    blocks = pressure.shape[0]
    rows, cols = water_depth.shape
    patches = rows // 8 * (cols // 8)
    along, width = lax.axis_size("gx"), lax.axis_size("gy")
    gx, gy = lax.axis_index("gx"), lax.axis_index("gy")
    place = jnp.stack(
        [gx * width + gy, gx, gy]
        + [jnp.int32(v) for v in (along * width, width, rows * along, cols * width, 0)]
    ).astype(I32)
    meta = jnp.concatenate(
        [
            soil_class[None],
            levels[None],
            patch_of_block[None],
            neighbors.T,
            neighbor_levels.T,
            jnp.zeros((1, blocks), I32),
        ],
        axis=0,
    )

    def edge(part):
        classes = jnp.pad(soil_class[part].astype(F32)[None], ((0, 7), (0, 512 - HB)))
        return jnp.concatenate([pressure[part], classes], axis=0)

    low_edge = shifted(edge(slice(blocks - HB, blocks)), ("gx", "gy"), 1, wrap=False)
    high_edge = shifted(edge(slice(0, HB)), ("gx", "gy"), -1, wrap=False)

    send, slot, edge_rows = route(place, meta, pressure, water_depth, bed_height, roughness, width)
    got = lax.all_to_all(send, "gy", 0, 0)
    halos = got[:, 72:88]
    left = lax.dynamic_index_in_dim(halos, jnp.maximum(gy - 1, 0), 0, keepdims=False)
    right = lax.dynamic_index_in_dim(halos, jnp.minimum(gy + 1, width - 1), 0, keepdims=False)
    moving = got[:, 32:72].reshape(40 * width, 128)
    from_low = shifted(jnp.concatenate([moving, edge_rows[1], left, right], axis=0), "gx", 1)
    from_high = shifted(jnp.concatenate([moving, edge_rows[0], left, right], axis=0), "gx", -1)

    base, factor, table = inside(soil_params, meta, pressure)

    stay, back, tile, edge_cols = surface(
        place, soil_params, got, from_low, from_high, water_depth, patches
    )
    back_high = shifted(back[0], "gx", -1)
    back_low = shifted(back[1], "gx", 1)

    head = across(place, soil_params, meta, low_edge, high_edge, base, factor, table)

    number = jnp.arange(width, dtype=I32)[:, None, None]
    moved = jnp.where(
        number >= gy,
        back_high[: 32 * width].reshape(width, 32, 128),
        back_low[: 32 * width].reshape(width, 32, 128),
    )
    above, below = back_low[32 * width :], back_high[32 * width :]

    def side(kind):
        lines = slice(2 * kind, 2 * kind + 2)
        return jnp.concatenate(
            [edge_cols[kind, 0:2], above[lines], below[lines], jnp.zeros((2, 128), F32)], axis=0
        )

    sides = jnp.where(number == gy + 1, side(1)[None], side(0)[None])
    returned = lax.all_to_all(jnp.concatenate([stay, moved, sides], axis=1), "gy", 0, 0)
    ends = returned[:, 64:72]
    west = lax.dynamic_index_in_dim(ends, jnp.maximum(gy - 1, 0), 0, keepdims=False)
    east = lax.dynamic_index_in_dim(ends, jnp.minimum(gy + 1, width - 1), 0, keepdims=False)
    new_depth = sweeps(
        place, water_depth, bed_height, roughness, left, right,
        from_low[40 * width :], from_high[40 * width :], tile, above, below, west, east,
    )
    new_pressure = top(returned, slot, factor, head)
    return new_pressure, new_depth


def solution(mesh):
    blocks = P(("gx", "gy"))
    wide = P(("gx", "gy"), None)
    tile = P("gx", "gy")
    return jax.shard_map(
        per_device,
        mesh=mesh,
        in_specs=(wide, blocks, blocks, wide, wide, blocks, P(), tile, tile, tile),
        out_specs=(wide, tile),
        check_vma=False,
    )
```

profile of v0, /device:TPU:1, one launch (start us, length us, event | category | flops | bytes accessed | tf_op | source)
XLA Modules:
  0.0 101.5 jit_solution(15045609817089190986)
XLA Ops:
  0.6 2.6 %concatenate.24.meta_ref = s32[16,2048]{1,0:T(8,128)S(1)} concatenate(s32[1,2048]{1,0:T(1,128)} %bitcast.38, s32[1,2048]{1,0:T(1,128)} %bitcast.39, s32[1,2048]{1,0:T(1,128)} %bitcast.40, s32[6,2048]{1,0:T(8,128)} %bitcast.36, s32[6,2048]{1,0:T(8,128)} %bitcast.37, s32[1,2048]{1,0:T(1,128)S(1)} %broadcast_in_dim.56), dimensions={0} | concatenate | bytes 262144 | tf_op jit(solution)/shard_map/concatenate | solution.py:618
  3.3 0.1 stack.15.place_ref
  3.4 0.0 copy-start
  3.4 2.2 %copy-done = f32[2048,512]{1,0:T(8,128)S(1)} copy-done((f32[2048,512]{1,0:T(8,128)S(1)}, f32[2048,512]{1,0:T(8,128)}, u32[]{:S(2)}) %copy-start) | copy-done | bytes 4194328
  5.6 0.9 copy-done.4
  6.5 0.9 copy-done.6
  7.4 0.9 copy-done.8
  8.3 5.1 %route.1 = (f32[8,88,128]{2,1,0:T(8,128)}, s32[1,2048]{1,0:T(1,128)S(1)}, f32[2,24,128]{2,1,0:T(8,128)S(1)}) custom-call(s32[8]{0:T(128)S(1)} %stack.15.place_ref, s32[16,2048]{1,0:T(8,128)S(1)} %concatenate.24.meta_ref, f32[2048,512]{1,0:T(8,128)S(1)} %copy-done, f32[128,256]{1,0:T(8,128)S(1)} %copy-done.4, f32[128,256]{1,0:T(8,128)S(1)} %copy-done.6, ...), custom_call_target="tpu_custom_call" | custom-call | tf_op jit(solution)/shard_map/route/pallas_call | solution.py:162
  13.4 6.1 %all-to-all-start = ((f32[8,88,128]{2,1,0:T(8,128)}), f32[8,88,128]{2,1,0:T(8,128)S(1)}, u32[]{:S(2)}, u32[]{:S(2)}) async-start(f32[8,88,128]{2,1,0:T(8,128)} %get-tuple-element.12), calls=%async_computation | async-start | bytes 720896 | tf_op jit(solution)/shard_map/all_to_all | solution.py:638
  19.5 0.7 slice_convert_fusion
  20.2 1.3 %fusion = (f32[256,512]{1,0:T(8,128)S(1)}, f32[256,512]{1,0:T(8,128)S(1)}) fusion(f32[2048,512]{1,0:T(8,128)} %head_ref.1), kind=kLoop, calls=%fused_computation.28 | loop fusion | bytes 2097152 | tf_op jit(solution)/shard_map/slice | solution.py:632
  21.5 3.5 %collective-permute-start.4 = (f32[264,512]{1,0:T(8,128)S(1)}, f32[264,512]{1,0:T(8,128)S(1)}, u32[]{:S(2)}, u32[]{:S(2)}) collective-permute-start(f32[264,512]{1,0:T(8,128)S(1)} %select_maximum_fusion.1), channel_id=1, source_target_pairs={{0,1},{1,2},{2,3},{3,4},{4,5},{5,6},{6,7},{7,8},{8,9},{9,10},{10,1... | collective-permute-start | bytes 1622024 | tf_op jit(solution)/shard_map/ppermute | solution.py:604
  25.1 1.9 %collective-permute-start.5 = (f32[264,512]{1,0:T(8,128)S(1)}, f32[264,512]{1,0:T(8,128)S(1)}, u32[]{:S(2)}, u32[]{:S(2)}) collective-permute-start(f32[264,512]{1,0:T(8,128)S(1)} %select_maximum_fusion), channel_id=1, source_target_pairs={{1,0},{2,1},{3,2},{4,3},{5,4},{6,5},{7,6},{8,7},{9,8},{10,9},{11,1... | collective-permute-start | bytes 1622024 | tf_op jit(solution)/shard_map/ppermute | solution.py:604
  27.1 0.1 pad.23.clone
  27.1 0.1 all-to-all-done.got_ref
  27.3 6.0 %collective-permute-start.1 = (f32[376,128]{1,0:T(8,128)S(1)}, f32[376,128]{1,0:T(8,128)S(1)}, u32[]{:S(2)}, u32[]{:S(2)}) collective-permute-start(f32[376,128]{1,0:T(8,128)S(1)} %get-tuple-element.26), channel_id=1, source_target_pairs={{0,120},{8,0},{16,8},{24,16},{32,24},{40,32},{48,40},{56,48},{64,5... | collective-permute-start | bytes 577544 | tf_op jit(solution)/shard_map/ppermute | solution.py:604
  33.3 0.0 collective-permute-start
  33.3 2.6 %collective-permute-done.1.down_ref = f32[376,128]{1,0:T(8,128)S(1)} collective-permute-done((f32[376,128]{1,0:T(8,128)S(1)}, f32[376,128]{1,0:T(8,128)S(1)}, u32[]{:S(2)}, u32[]{:S(2)}) %collective-permute-start.1) | collective-permute-done | bytes 192544 | tf_op jit(solution)/shard_map/ppermute | solution.py:604
  35.9 5.2 %collective-permute-done.up_ref = f32[376,128]{1,0:T(8,128)S(1)} collective-permute-done((f32[376,128]{1,0:T(8,128)S(1)}, f32[376,128]{1,0:T(8,128)S(1)}, u32[]{:S(2)}, u32[]{:S(2)}) %collective-permute-start) | collective-permute-done | bytes 192544 | tf_op jit(solution)/shard_map/ppermute | solution.py:604
  41.1 0.0 copy-done.5
  41.1 0.0 copy-done.10
  41.1 3.6 %surface.1 = (f32[8,32,128]{2,1,0:T(8,128)S(1)}, f32[2,264,128]{2,1,0:T(8,128)S(1)}, f32[128,256]{1,0:T(8,128)S(1)}, f32[2,8,128]{2,1,0:T(8,128)S(1)}) custom-call(s32[8]{0:T(128)S(1)} %stack.15.place_ref, f32[5,12]{1,0:T(8,128)S(1)} %copy-done.10, f32[8,88,128]{2,1,0:T(8,128)S(1)} %all-to-all-done.got_ref, f32[376,128]{1,0:T(8,128)S(1)} %collective-permute-done.up_ref, ...), custom_call_target="tpu_custom_call" | custom-call | tf_op jit(solution)/shard_map/surface/pallas_call | solution.py:279
  44.8 0.1 collective-permute-start.3
  44.9 4.8 %collective-permute-start.2 = (f32[264,128]{1,0:T(8,128)S(1)}, f32[264,128]{1,0:T(8,128)S(1)}, u32[]{:S(2)}, u32[]{:S(2)}) collective-permute-start(f32[264,128]{1,0:T(8,128)S(1)} %get-tuple-element.25), channel_id=1, source_target_pairs={{0,120},{8,0},{16,8},{24,16},{32,24},{40,32},{48,40},{56,48},{64,5... | collective-permute-start | bytes 405512 | tf_op jit(solution)/shard_map/ppermute | solution.py:604
  49.6 2.4 %collective-permute-done.3 = f32[264,128]{1,0:T(8,128)S(1)} collective-permute-done((f32[264,128]{1,0:T(8,128)S(1)}, f32[264,128]{1,0:T(8,128)S(1)}, u32[]{:S(2)}, u32[]{:S(2)}) %collective-permute-start.3) | collective-permute-done | bytes 135200 | tf_op jit(solution)/shard_map/ppermute | solution.py:604
  52.0 0.0 collective-permute-done.2
  52.1 0.0 copy-start.11
  52.1 0.1 broadcast_select_fusion
  52.2 0.5 copy-done.11
  52.7 0.1 maximum_maximum_fusion
  52.8 0.1 broadcast_select_fusion.1
  52.9 0.7 pad_maximum_fusion
  53.6 8.1 %all-to-all-start.1 = ((f32[8,72,128]{2,1,0:T(8,128)}), f32[8,72,128]{2,1,0:T(8,128)S(1)}, u32[]{:S(2)}, u32[]{:S(2)}) async-start(f32[8,72,128]{2,1,0:T(8,128)} %pad_maximum_fusion), calls=%async_computation.1 | async-start | bytes 589824 | tf_op jit(solution)/shard_map/all_to_all | solution.py:671
  61.7 2.2 %copy-done.1 = f32[2048,512]{1,0:T(8,128)S(1)} copy-done((f32[2048,512]{1,0:T(8,128)S(1)}, f32[2048,512]{1,0:T(8,128)}, u32[]{:S(2)}) %copy-start.1) | copy-done | bytes 4194328
  63.9 10.6 %inside.1 = (f32[16,512,128]{2,1,0:T(8,128)S(1)}, f32[16,512,128]{2,1,0:T(8,128)S(1)}, bf16[1536,2048]{1,0:T(8,128)(2,1)}) custom-call(f32[5,12]{1,0:T(8,128)S(1)} %copy-done.10, s32[16,2048]{1,0:T(8,128)S(1)} %concatenate.24.meta_ref, f32[2048,512]{1,0:T(8,128)S(1)} %copy-done.1), custom_call_target="tpu_custom_call" | custom-call | tf_op jit(solution)/shard_map/inside/pallas_call | solution.py:435
  74.4 2.1 %copy-done.2 = f32[16,512,128]{2,1,0:T(8,128)} copy-done((f32[16,512,128]{2,1,0:T(8,128)}, f32[16,512,128]{2,1,0:T(8,128)S(1)}, u32[]{:S(2)}) %copy-start.2) | copy-done | bytes 4194328
  76.5 0.0 collective-permute-done.4.low_ref
  76.5 0.0 collective-permute-done.5.high_ref
  76.5 0.0 copy-start.7
  76.5 0.0 copy-start.9
  76.6 14.8 %across.1.head_ref = f32[2048,512]{1,0:T(8,128)} custom-call(s32[8]{0:T(128)S(1)} %stack.15.place_ref, f32[5,12]{1,0:T(8,128)S(1)} %copy-done.10, s32[16,2048]{1,0:T(8,128)S(1)} %concatenate.24.meta_ref, f32[264,512]{1,0:T(8,128)S(1)} %collective-permute-done.4.low_ref, f32[264,512]{1,0:T(8,128)S(1)} %collective-permute-done.5.high_ref, ...), custom_call_target="tpu_custom_call" | custom-call | tf_op jit(solution)/shard_map/across/pallas_call | solution.py:521
  91.3 0.7 slice.107.below_ref
  92.0 0.0 all-to-all-done.1.got_ref
  92.0 0.0 copy-done.7
  92.0 0.0 copy-done.9
  92.0 2.9 %sweeps.1 = f32[128,256]{1,0:T(8,128)} custom-call(s32[8]{0:T(128)S(1)} %stack.15.place_ref, f32[128,256]{1,0:T(8,128)S(1)} %copy-done.5, f32[128,256]{1,0:T(8,128)S(1)} %copy-done.7, f32[128,256]{1,0:T(8,128)S(1)} %copy-done.9, f32[16,128]{1,0:T(8,128)S(1)} %get-tuple-element.32.left_ref, f32[16,128]{1,0:T(8,128)S(1)} %get-tuple-element.33.right_ref, ...), custom_call_target="tpu_custom_call" | custom-call | tf_op jit(solution)/shard_map/sweeps/pallas_call | solution.py:377
  94.9 2.2 %copy-done.3 = f32[16,512,128]{2,1,0:T(8,128)S(1)} copy-done((f32[16,512,128]{2,1,0:T(8,128)S(1)}, f32[16,512,128]{2,1,0:T(8,128)}, u32[]{:S(2)}) %copy-start.3) | copy-done | bytes 4194328
  97.1 4.4 %top.1 = f32[2048,512]{1,0:T(8,128)} custom-call(f32[8,72,128]{2,1,0:T(8,128)S(1)} %all-to-all-done.1.got_ref, s32[1,2048]{1,0:T(1,128)S(1)} %get-tuple-element.17.slot_ref, f32[16,512,128]{2,1,0:T(8,128)S(1)} %copy-done.3, f32[2048,512]{1,0:T(8,128)} %across.1.head_ref), custom_call_target="tpu_custom_call", output_to_operand_aliasing={{}: (3, {})} | custom-call | tf_op jit(solution)/shard_map/top/pallas_call | solution.py:580
  (31 shorter events, 0.2 us)
Async XLA Ops:
  3.4 2.2 %copy-start = (f32[2048,512]{1,0:T(8,128)S(1)}, f32[2048,512]{1,0:T(8,128)}, u32[]{:S(2)}) copy-start(f32[2048,512]{1,0:T(8,128)} %head_ref.1) | copy-start | bytes 12582916
  5.5 0.9 copy-start.4
  6.5 0.9 copy-start.6
  7.4 0.9 copy-start.8
  13.4 27.7 %copy-start.5 = (f32[128,256]{1,0:T(8,128)S(1)}, f32[128,256]{1,0:T(8,128)}, u32[]{:S(2)}) copy-start(f32[128,256]{1,0:T(8,128)} %depth_ref.5) | copy-start | bytes 393220
  13.4 27.7 %copy-start.10 = (f32[5,12]{1,0:T(8,128)S(1)}, f32[5,12]{1,0:T(8,128)}, u32[]{:S(2)}) copy-start(f32[5,12]{1,0:T(8,128)} %soil_ref.5) | copy-start | bytes 724
  13.4 13.8 %all-to-all-start = ((f32[8,88,128]{2,1,0:T(8,128)}), f32[8,88,128]{2,1,0:T(8,128)S(1)}, u32[]{:S(2)}, u32[]{:S(2)}) async-start(f32[8,88,128]{2,1,0:T(8,128)} %get-tuple-element.12), calls=%async_computation | async-start | bytes 720896 | tf_op jit(solution)/shard_map/all_to_all | solution.py:638
  21.5 55.0 %collective-permute-start.4 = (f32[264,512]{1,0:T(8,128)S(1)}, f32[264,512]{1,0:T(8,128)S(1)}, u32[]{:S(2)}, u32[]{:S(2)}) collective-permute-start(f32[264,512]{1,0:T(8,128)S(1)} %select_maximum_fusion.1), channel_id=1, source_target_pairs={{0,1},{1,2},{2,3},{3,4},{4,5},{5,6},{6,7},{7,8},{8,9},{9,10},{10,1... | collective-permute-start | bytes 1622024 | tf_op jit(solution)/shard_map/ppermute | solution.py:604
  25.1 51.4 %collective-permute-start.5 = (f32[264,512]{1,0:T(8,128)S(1)}, f32[264,512]{1,0:T(8,128)S(1)}, u32[]{:S(2)}, u32[]{:S(2)}) collective-permute-start(f32[264,512]{1,0:T(8,128)S(1)} %select_maximum_fusion), channel_id=1, source_target_pairs={{1,0},{2,1},{3,2},{4,3},{5,4},{6,5},{7,6},{8,7},{9,8},{10,9},{11,1... | collective-permute-start | bytes 1622024 | tf_op jit(solution)/shard_map/ppermute | solution.py:604
  27.3 8.6 %collective-permute-start.1 = (f32[376,128]{1,0:T(8,128)S(1)}, f32[376,128]{1,0:T(8,128)S(1)}, u32[]{:S(2)}, u32[]{:S(2)}) collective-permute-start(f32[376,128]{1,0:T(8,128)S(1)} %get-tuple-element.26), channel_id=1, source_target_pairs={{0,120},{8,0},{16,8},{24,16},{32,24},{40,32},{48,40},{56,48},{64,5... | collective-permute-start | bytes 577544 | tf_op jit(solution)/shard_map/ppermute | solution.py:604
  33.3 7.8 %collective-permute-start = (f32[376,128]{1,0:T(8,128)S(1)}, f32[376,128]{1,0:T(8,128)S(1)}, u32[]{:S(2)}, u32[]{:S(2)}) collective-permute-start(f32[376,128]{1,0:T(8,128)S(1)} %get-tuple-element.27), channel_id=1, source_target_pairs={{0,8},{8,16},{16,24},{24,32},{32,40},{40,48},{48,56},{56,64},{64,7... | collective-permute-start | bytes 577544 | tf_op jit(solution)/shard_map/ppermute | solution.py:604
  44.8 7.3 %collective-permute-start.3 = (f32[264,128]{1,0:T(8,128)S(1)}, f32[264,128]{1,0:T(8,128)S(1)}, u32[]{:S(2)}, u32[]{:S(2)}) collective-permute-start(f32[264,128]{1,0:T(8,128)S(1)} %get-tuple-element.24), channel_id=1, source_target_pairs={{0,8},{8,16},{16,24},{24,32},{32,40},{40,48},{48,56},{56,64},{64,7... | collective-permute-start | bytes 405512 | tf_op jit(solution)/shard_map/ppermute | solution.py:604
  44.9 7.2 %collective-permute-start.2 = (f32[264,128]{1,0:T(8,128)S(1)}, f32[264,128]{1,0:T(8,128)S(1)}, u32[]{:S(2)}, u32[]{:S(2)}) collective-permute-start(f32[264,128]{1,0:T(8,128)S(1)} %get-tuple-element.25), channel_id=1, source_target_pairs={{0,120},{8,0},{16,8},{24,16},{32,24},{40,32},{48,40},{56,48},{64,5... | collective-permute-start | bytes 405512 | tf_op jit(solution)/shard_map/ppermute | solution.py:604
  52.1 0.7 copy-start.11
  53.6 38.4 %all-to-all-start.1 = ((f32[8,72,128]{2,1,0:T(8,128)}), f32[8,72,128]{2,1,0:T(8,128)S(1)}, u32[]{:S(2)}, u32[]{:S(2)}) async-start(f32[8,72,128]{2,1,0:T(8,128)} %pad_maximum_fusion), calls=%async_computation.1 | async-start | bytes 589824 | tf_op jit(solution)/shard_map/all_to_all | solution.py:671
  61.7 2.2 %copy-start.1 = (f32[2048,512]{1,0:T(8,128)S(1)}, f32[2048,512]{1,0:T(8,128)}, u32[]{:S(2)}) copy-start(f32[2048,512]{1,0:T(8,128)} %head_ref.1) | copy-start | bytes 12582916
  74.4 2.1 %copy-start.2 = (f32[16,512,128]{2,1,0:T(8,128)}, f32[16,512,128]{2,1,0:T(8,128)S(1)}, u32[]{:S(2)}) copy-start(f32[16,512,128]{2,1,0:T(8,128)S(1)} %get-tuple-element.18.factor_ref) | copy-start | bytes 12582916
  76.5 15.5 %copy-start.7 = (f32[128,256]{1,0:T(8,128)S(1)}, f32[128,256]{1,0:T(8,128)}, u32[]{:S(2)}) copy-start(f32[128,256]{1,0:T(8,128)} %bed_ref.3) | copy-start | bytes 393220
  76.5 15.5 %copy-start.9 = (f32[128,256]{1,0:T(8,128)S(1)}, f32[128,256]{1,0:T(8,128)}, u32[]{:S(2)}) copy-start(f32[128,256]{1,0:T(8,128)} %rough_ref.3) | copy-start | bytes 393220
  94.9 2.2 %copy-start.3 = (f32[16,512,128]{2,1,0:T(8,128)S(1)}, f32[16,512,128]{2,1,0:T(8,128)}, u32[]{:S(2)}) copy-start(f32[16,512,128]{2,1,0:T(8,128)} %copy-done.2) | copy-start | bytes 12582916
where the time goes:
time: 102 us; the launch traced here: 101 us
  Pallas kernels  41.3 us (40%)
  starting transfers between devices  30.5 us (30%)
  local copies, waits for them, and re-layouts  16.7 us (16%)
  waiting for transfers between devices  10.3 us (10%)
  other arithmetic  1.79 us (2%)
    ppermute x6, starting transfers between devices, shifted(): return lax.ppermute(value, axis, pairs)  16.3 us
    pallas_call x1, Pallas kernels, across(): pl.pallas_call(across_kernel, grid=(blocks // TILE,), in_specs=[SMEM, SME...  14.8 us
    unnamed x24, local copies, waits for them, and re-layouts  11.9 us
    pallas_call x1, Pallas kernels, inside(): pl.pallas_call(inside_kernel, grid=(blocks // TILE,), in_specs=[SMEM, pl....  10.6 us
    ppermute x6, waiting for transfers between devices, shifted(): return lax.ppermute(value, axis, pairs)  10.2 us
    all_to_all x1, starting transfers between devices, per_device(): lax.all_to_all(jnp.concatenate([stay, moved, sides], axis=1), 'gy', 0, 0)  8.06 us
    all_to_all x1, starting transfers between devices, per_device(): got = lax.all_to_all(send, 'gy', 0, 0)  6.1 us
    pallas_call x1, Pallas kernels, route(): pl.pallas_call(route_kernel, grid=(1,), in_specs=[SMEM, pl.BlockSpec(meta...  5.13 us
  transfers between devices with their start and end apart: 8, of which 4 were waited for; matrix products, arithmetic and copies ran while one was open for 4% of the time, Pallas kernels for 29%

commit v1 on v0

--- a/solution.py
+++ b/solution.py
@@ -1,3 +1,5 @@
+import functools
+
 import jax
 import jax.numpy as jnp
 from jax import lax
@@ -19,10 +21,11 @@
 SLOPE_FLOOR = 0.01
 OPPOSITE = (1, 0, 3, 2, 5, 4)
 GRAVITY = (0.0, 0.0, 0.0, 0.0, -1.0, 1.0)
-MIB = 1024 * 1024
+VMEM_LIMIT = 60 * 1024 * 1024
 
 VMEM = pl.BlockSpec(memory_space=pltpu.VMEM)
 SMEM = pl.BlockSpec(memory_space=pltpu.SMEM)
+ANY = pl.BlockSpec(memory_space=pl.ANY)
 
 
 def split(value):
@@ -86,7 +89,32 @@
 
 
 def route_kernel(place_ref, meta_ref, top_ref, depth_ref, bed_ref, rough_ref,
-                 send_ref, slot_ref, rows_ref, turned, packed, edges):
+                 send_ref, slot_ref, rows_ref, match_ref, turned, packed, edges):
+    number = pl.program_id(0)
+    gy = place_ref[2]
+
+    @pl.when(number == 0)
+    def _():
+        route_once(place_ref, meta_ref, top_ref, depth_ref, bed_ref, rough_ref,
+                   slot_ref, rows_ref, turned, packed, edges)
+
+    blocks = meta_ref.shape[1]
+    low_lane = iota((32, 128), 1) < 64
+    wanted = as_bf16(iota((128, blocks), 0) + 128 * number == slot_ref[...])
+    match_ref[...] = wanted
+    out = lax.dot_general(packed[...], wanted, (((1,), (1,)), ((), ())), preferred_element_type=F32)
+    first = out[0:32] + out[64:96]
+    second = out[32:64] + out[96:128]
+    send_ref[0, 0:32, :] = jnp.where(low_lane, first, pltpu.roll(second, 64, 1))
+    send_ref[0, 32:64, :] = jnp.where(low_lane, pltpu.roll(first, 64, 1), second)
+    label = out[130:131] * (out[128:129] + 256.0 * out[129:130] + 1.0) - 1.0
+    row = iota((8, 128), 0)
+    send_ref[0, 64:72, :] = jnp.where(row == 0, label, jnp.where(row == 1, out[131:132], out[132:133]))
+    send_ref[0, 72:88, :] = jnp.where(number == gy + 1, edges[1], edges[0])
+
+
+def route_once(place_ref, meta_ref, top_ref, depth_ref, bed_ref, rough_ref,
+               slot_ref, rows_ref, turned, packed, edges):
     own, gy = place_ref[0], place_ref[2]
     devices, width = place_ref[3], place_ref[4]
     blocks = meta_ref.shape[1]
@@ -136,32 +164,13 @@
             lanes = slice(128 * half, 128 * half + 128)
             rows_ref[0, at : at + 3, :] = field[0:3, lanes]
             rows_ref[1, at : at + 3, :] = field[125:128, lanes]
-    low_lane = iota((32, 128), 1) < 64
-    slot = slot_ref[...]
-
-    def chunk(number, _):
-        wanted = as_bf16(iota((128, blocks), 0) + 128 * number == slot)
-        out = lax.dot_general(packed[...], wanted, (((1,), (1,)), ((), ())), preferred_element_type=F32)
-        first = out[0:32] + out[64:96]
-        second = out[32:64] + out[96:128]
-        send_ref[number, 0:32, :] = jnp.where(low_lane, first, pltpu.roll(second, 64, 1))
-        send_ref[number, 32:64, :] = jnp.where(low_lane, pltpu.roll(first, 64, 1), second)
-        label = out[130:131] * (out[128:129] + 256.0 * out[129:130] + 1.0) - 1.0
-        row = iota((8, 128), 0)
-        send_ref[number, 64:72, :] = jnp.where(
-            row == 0, label, jnp.where(row == 1, out[131:132], out[132:133])
-        )
-        send_ref[number, 72:88, :] = jnp.where(number == gy + 1, edges[1], edges[0])
-        return 0
-
-    lax.fori_loop(0, send_ref.shape[0], chunk, 0)
 
 
 def route(place, meta, pressure, water_depth, bed_height, roughness, width):
     blocks = meta.shape[1]
     return pl.pallas_call(
         route_kernel,
-        grid=(1,),
+        grid=(width,),
         in_specs=[
             SMEM,
             pl.BlockSpec(meta.shape, lambda t: (0, 0)),
@@ -171,26 +180,28 @@
             pl.BlockSpec(water_depth.shape, lambda t: (0, 0)),
         ],
         out_specs=[
-            pl.BlockSpec((width, 88, 128), lambda t: (0, 0, 0)),
+            pl.BlockSpec((1, 88, 128), lambda t: (t, 0, 0)),
             pl.BlockSpec((1, blocks), lambda t: (0, 0)),
             pl.BlockSpec((2, 24, 128), lambda t: (0, 0, 0)),
+            pl.BlockSpec((128, blocks), lambda t: (t, 0)),
         ],
         out_shape=[
             jax.ShapeDtypeStruct((width, 88, 128), F32),
             jax.ShapeDtypeStruct((1, blocks), I32),
             jax.ShapeDtypeStruct((2, 24, 128), F32),
+            jax.ShapeDtypeStruct((128 * width, blocks), BF16),
         ],
         scratch_shapes=[
             pltpu.VMEM((blocks // 128, 128, 128), F32),
             pltpu.VMEM((144, blocks), BF16),
             pltpu.VMEM((2, 16, 128), F32),
         ],
-        compiler_params=pltpu.CompilerParams(vmem_limit_bytes=40 * MIB),
+        compiler_params=pltpu.CompilerParams(vmem_limit_bytes=VMEM_LIMIT),
         name="route",
     )(place, meta, pressure, water_depth, bed_height, roughness)
 
 
-def surface_kernel(place_ref, soil_ref, got_ref, up_ref, down_ref, depth_ref,
+def surface_kernel(place_ref, soil_ref, got_ref, up_ref, down_ref, depth_ref, after_ref,
                    stay_ref, back_ref, tile_ref, cols_ref, packed, labels, match):
     gy = place_ref[2]
     low_lane = iota((32, 128), 1) < 64
@@ -274,11 +285,11 @@
     cols_ref[1, 0:2, :] = total[:, 128:256].T[126:128, :]
 
 
-def surface(place, soil, got, up, down, water_depth, patches):
+def surface(place, soil, got, up, down, water_depth, patches, after):
     width = got.shape[0]
     return pl.pallas_call(
         surface_kernel,
-        in_specs=[SMEM, SMEM, VMEM, VMEM, VMEM, VMEM],
+        in_specs=[SMEM, SMEM, VMEM, VMEM, VMEM, VMEM, ANY],
         out_specs=[VMEM, VMEM, VMEM, VMEM],
         out_shape=[
             jax.ShapeDtypeStruct((width, 32, 128), F32),
@@ -291,17 +302,20 @@
             pltpu.VMEM((1, width * 128), I32),
             pltpu.VMEM((patches, width * 128), BF16),
         ],
-        compiler_params=pltpu.CompilerParams(vmem_limit_bytes=40 * MIB),
+        compiler_params=pltpu.CompilerParams(vmem_limit_bytes=VMEM_LIMIT),
         name="surface",
-    )(place, soil, got, up, down, water_depth)
-
-
-def sweep_kernel(place_ref, depth_ref, bed_ref, rough_ref, left_ref, right_ref, up_ref, down_ref,
-                 source_ref, above_ref, below_ref, west_ref, east_ref,
+    )(place, soil, got, up, down, water_depth, after)
+
+
+def sweep_kernel(place_ref, depth_ref, bed_ref, rough_ref, got_ref, up_ref, down_ref,
+                 source_ref, low_ref, high_ref, back_ref, after_ref,
                  out_ref, depth_ext, bed_ext, rough_ext, source_ext, turn):
     gx, gy = place_ref[1], place_ref[2]
+    left_at, right_at = jnp.maximum(gy - 1, 0), jnp.minimum(gy + 1, place_ref[4] - 1)
     rows_total, cols_total = place_ref[5], place_ref[6]
     shape = depth_ext.shape
+    halo = 40 * got_ref.shape[0]
+    edge = 32 * got_ref.shape[0]
     depth_ext[...] = jnp.zeros(shape, F32)
     bed_ext[...] = jnp.zeros(shape, F32)
     rough_ext[...] = jnp.ones(shape, F32)
@@ -313,16 +327,16 @@
         for half in range(2):
             at = 3 * (2 * number + half)
             lanes = slice(128 + 128 * half, 256 + 128 * half)
-            ext[5:8, lanes] = up_ref[at : at + 3, :]
-            ext[136:139, lanes] = down_ref[at : at + 3, :]
+            ext[5:8, lanes] = up_ref[halo + at : halo + at + 3, :]
+            ext[136:139, lanes] = down_ref[halo + at : halo + at + 3, :]
         col = 3 * number
         fill = 1.0 if number == 2 else 0.0
         for side, lanes in ((0, slice(0, 128)), (1, slice(384, 512))):
             to = slice(125, 128) if side == 0 else slice(0, 3)
-            center_ref = left_ref if side == 0 else right_ref
-            away = 24 + 16 * side + col
+            beside = left_at if side == 0 else right_at
+            away = halo + 24 + 16 * side + col
             turn[...] = jnp.full((128, 128), fill, F32)
-            turn[to, :] = center_ref[col : col + 3, :]
+            turn[to, :] = got_ref[beside, 72:88, :][col : col + 3, :]
             ext[8:136, lanes] = turn[...].T
             turn[to, :] = up_ref[away : away + 3, :]
             ext[0:8, lanes] = turn[...].T[120:128, :]
@@ -331,16 +345,16 @@
     source_ext[8:136, 128:384] = source_ref[...]
     for half in range(2):
         lanes = slice(128 + 128 * half, 256 + 128 * half)
-        source_ext[6:8, lanes] = above_ref[2 * half : 2 * half + 2, :]
-        source_ext[136:138, lanes] = below_ref[2 * half : 2 * half + 2, :]
+        source_ext[6:8, lanes] = low_ref[edge + 2 * half : edge + 2 * half + 2, :]
+        source_ext[136:138, lanes] = high_ref[edge + 2 * half : edge + 2 * half + 2, :]
     for side, lanes in ((0, slice(0, 128)), (1, slice(384, 512))):
         to = slice(126, 128) if side == 0 else slice(0, 2)
-        ref = west_ref if side == 0 else east_ref
+        ends = back_ref[left_at if side == 0 else right_at, 64:72, :]
         turn[...] = jnp.zeros((128, 128), F32)
-        turn[to, :] = ref[0:2, :]
+        turn[to, :] = ends[0:2, :]
         source_ext[8:136, lanes] = turn[...].T
-        source_ext[6:8, lanes] = ref[2:4, :]
-        source_ext[136:138, lanes] = ref[4:6, :]
+        source_ext[6:8, lanes] = ends[2:4, :]
+        source_ext[136:138, lanes] = ends[4:6, :]
     row_id = gx * depth_ref.shape[0] - 8 + iota(shape, 0)
     col_id = gy * depth_ref.shape[1] - 128 + iota(shape, 1)
     row_open = (row_id >= 0) & (row_id + 1 < rows_total)
@@ -372,20 +386,20 @@
     out_ref[...] = head[8:136, 128:384]
 
 
-def sweeps(place, water_depth, bed_height, roughness, left, right, up, down, source, above, below, west, east):
+def sweeps(place, water_depth, *rest):
     shape = (144, 512)
     return pl.pallas_call(
         sweep_kernel,
-        in_specs=[SMEM] + [VMEM] * 12,
+        in_specs=[SMEM] + [VMEM] * 10 + [ANY],
         out_specs=VMEM,
         out_shape=jax.ShapeDtypeStruct(water_depth.shape, F32),
         scratch_shapes=[pltpu.VMEM(shape, F32)] * 4 + [pltpu.VMEM((128, 128), F32)],
-        compiler_params=pltpu.CompilerParams(vmem_limit_bytes=40 * MIB),
+        compiler_params=pltpu.CompilerParams(vmem_limit_bytes=VMEM_LIMIT),
         name="sweeps",
-    )(place, water_depth, bed_height, roughness, left, right, up, down, source, above, below, west, east)
-
-
-def inside_kernel(soil_ref, meta_ref, head_ref, base_ref, factor_ref, table_ref, turned, cond):
+    )(place, water_depth, *rest)
+
+
+def inside_kernel(soil_ref, meta_ref, head_ref, after_ref, base_ref, factor_ref, table_ref, turned, cond):
     open_i = iota((8, 8, 128), 1) < 7
     nothing = jnp.zeros((1, 8, 128), F32)
     for half in range(head_ref.shape[0] // 128):
@@ -399,7 +413,7 @@
             rows = slice(64 * k, 64 * k + 64)
             conductivity, base, ratio = curve(turned[half, rows, :], soil)
             cond[half, rows, :] = conductivity
-            factor_ref[half, rows, :] = scaled / (soil[4] * ratio / base + STORAGE)
+            factor_ref[half, rows, :] = scaled * base / (soil[4] * ratio + STORAGE * base)
         below = None
         for k in range(8):
             rows = slice(64 * k, 64 * k + 64)
@@ -430,15 +444,17 @@
         write_faces(turned, cond, half, put)
 
 
-def inside(soil, meta, pressure):
-    blocks = pressure.shape[0]
+def inside(soil, meta, pressure, after, part):
+    blocks = pressure.shape[0] // 2
+    steps = blocks // TILE
     return pl.pallas_call(
         inside_kernel,
-        grid=(blocks // TILE,),
+        grid=(steps,),
         in_specs=[
             SMEM,
-            pl.BlockSpec((16, TILE), lambda t: (0, t)),
-            pl.BlockSpec((TILE, 512), lambda t: (t, 0)),
+            pl.BlockSpec((meta.shape[0], TILE), lambda t: (0, t + part * steps)),
+            pl.BlockSpec((TILE, 512), lambda t: (t + part * steps, 0)),
+            ANY,
         ],
         out_specs=[
             pl.BlockSpec((TILE // 128, 512, 128), lambda t: (t, 0, 0)),
@@ -451,46 +467,52 @@
             jax.ShapeDtypeStruct((1536, blocks), BF16),
         ],
         scratch_shapes=[pltpu.VMEM((TILE // 128, 512, 128), F32)] * 2,
-        compiler_params=pltpu.CompilerParams(vmem_limit_bytes=40 * MIB),
+        compiler_params=pltpu.CompilerParams(vmem_limit_bytes=VMEM_LIMIT),
+        cost_estimate=pl.CostEstimate(flops=blocks * 512 * 60, bytes_accessed=blocks * 512 * 18, transcendentals=blocks * 512 * 5),
         name="inside",
-    )(soil, meta, pressure)
-
-
-def across_kernel(place_ref, soil_ref, meta_ref, low_ref, high_ref, base_ref, factor_ref, table_ref,
-                  out_ref, table, turned, cond, arrived):
+    )(soil, meta, pressure, after)
+
+
+def across_kernel(part, place_ref, soil_ref, meta_ref, near_ref, edge_ref, base_ref, factor_ref, table_ref,
+                  other_ref, after_ref, out_ref, table, turned, cond, arrived):
     step = pl.program_id(0)
     blocks = table_ref.shape[1]
-    own_lanes = pl.ds(HB, blocks)
+    start = (0, HB + blocks)[part]
 
     @pl.when(step == 0)
     def _():
-        copy = pltpu.make_async_copy(table_ref, table.at[:, own_lanes], arrived)
-        copy.start()
-        for number, ref in enumerate((low_ref, high_ref)):
-            start = 0 if number == 0 else HB + blocks
-
-            def put(row, half, value):
-                table[row : row + 64, start + 128 * half : start + 128 * half + 128] = value
-
-            for half in range(HB // 128):
-                lanes = slice(128 * half, 128 * half + 128)
-                turned[half] = ref[lanes, :].T
-                classes = ref[HB : HB + 8, lanes][0:1, :].astype(I32)
-                soil = soil_rows(soil_ref, classes)
-                for k in range(8):
-                    rows = slice(64 * k, 64 * k + 64)
-                    cond[half, rows, :] = curve(turned[half, rows, :], soil)[0]
-                write_faces(turned, cond, half, put)
-        copy.wait()
+        own_copy = pltpu.make_async_copy(table_ref, table.at[:, pl.ds(HB, blocks)], arrived.at[0])
+        own_copy.start()
+        next_copy = pltpu.make_async_copy(
+            other_ref.at[:, pl.ds((0, blocks - HB)[part], HB)],
+            table.at[:, pl.ds((HB + blocks, 0)[part], HB)],
+            arrived.at[1],
+        )
+        next_copy.start()
+
+        def put(row, half, value):
+            table[row : row + 64, start + 128 * half : start + 128 * half + 128] = value
+
+        for half in range(HB // 128):
+            lanes = slice(128 * half, 128 * half + 128)
+            turned[half] = edge_ref[lanes, :].T
+            classes = edge_ref[HB : HB + 8, lanes][0:1, :].astype(I32)
+            soil = soil_rows(soil_ref, classes)
+            for k in range(8):
+                rows = slice(64 * k, 64 * k + 64)
+                cond[half, rows, :] = curve(turned[half, rows, :], soil)[0]
+            write_faces(turned, cond, half, put)
+        own_copy.wait()
+        next_copy.wait()
 
     turned[...] = base_ref[...]
     window = pl.ds(pl.multiple_of(step * TILE, TILE), TILE + 2 * HB)
     own = pl.ds(pl.multiple_of(step * TILE + HB, TILE), TILE)
     width = cell_width(meta_ref[1:2, :])
-    first_row = place_ref[0] * blocks - HB + step * TILE
+    first_row = (2 * place_ref[0] + part) * blocks - HB + step * TILE
     for face in range(6):
-        neighbor = meta_ref[3 + face : 4 + face, :]
-        far_width = cell_width(meta_ref[9 + face : 10 + face, :])
+        neighbor = near_ref[face : face + 1, :]
+        far_width = cell_width(near_ref[6 + face : 7 + face, :])
         over_gap = 2.0 / (width + far_width)
         half = jnp.where(neighbor >= 0, 0.5, 0.0)
         chosen = as_bf16(iota((TILE + 2 * HB, TILE), 0) == neighbor - first_row)
@@ -516,38 +538,54 @@
         out_ref[128 * part : 128 * part + 128, :] = turned[part].T
 
 
-def across(place, soil, meta, low, high, base, factor, table):
+def across(place, soil, meta, near, edge, inner, other, after, part, head):
+    base, factor, table = inner
     blocks = table.shape[1]
+    steps = blocks // TILE
+    kernel = functools.partial(across_kernel, part)
+    kernel_in = kernel
+    aliases = {}
+    extra, extra_specs = [], []
+    if head is not None:
+        def kernel_in(*refs):
+            kernel(*refs[:10], *refs[11:])
+
+        aliases = {10: 0}
+        extra, extra_specs = [head], [ANY]
     return pl.pallas_call(
-        across_kernel,
-        grid=(blocks // TILE,),
+        kernel_in,
+        grid=(steps,),
         in_specs=[
             SMEM,
             SMEM,
-            pl.BlockSpec((16, TILE), lambda t: (0, t)),
-            pl.BlockSpec(low.shape, lambda t: (0, 0)),
-            pl.BlockSpec(high.shape, lambda t: (0, 0)),
+            pl.BlockSpec((meta.shape[0], TILE), lambda t: (0, t + part * steps)),
+            pl.BlockSpec((near.shape[0], TILE), lambda t: (0, t + part * steps)),
+            pl.BlockSpec(edge.shape, lambda t: (0, 0)),
             pl.BlockSpec((TILE // 128, 512, 128), lambda t: (t, 0, 0)),
             pl.BlockSpec((TILE // 128, 512, 128), lambda t: (t, 0, 0)),
-            pl.BlockSpec(memory_space=pl.ANY),
-        ],
-        out_specs=pl.BlockSpec((TILE, 512), lambda t: (t, 0)),
-        out_shape=jax.ShapeDtypeStruct((blocks, 512), F32),
+            ANY,
+            ANY,
+            ANY,
+        ]
+        + extra_specs,
+        out_specs=pl.BlockSpec((TILE, 512), lambda t: (t + part * steps, 0)),
+        out_shape=jax.ShapeDtypeStruct((2 * blocks, 512), F32),
+        input_output_aliases=aliases,
         scratch_shapes=[
             pltpu.VMEM((1536, blocks + 2 * HB), BF16),
             pltpu.VMEM((TILE // 128, 512, 128), F32),
             pltpu.VMEM((TILE // 128, 512, 128), F32),
-            pltpu.SemaphoreType.DMA,
-        ],
-        compiler_params=pltpu.CompilerParams(vmem_limit_bytes=48 * MIB),
+            pltpu.SemaphoreType.DMA((2,)),
+        ],
+        compiler_params=pltpu.CompilerParams(vmem_limit_bytes=VMEM_LIMIT),
+        cost_estimate=pl.CostEstimate(flops=steps * 6 * 2 * 256 * 256 * 768, bytes_accessed=blocks * 512 * 18, transcendentals=0),
         name="across",
-    )(place, soil, meta, low, high, base, factor, table)
-
-
-def top_kernel(got_ref, slot_ref, factor_ref, head_ref, out_ref, packed, turned):
+    )(place, soil, meta, near, edge, base, factor, table, other, after, *extra)
+
+
+def top_kernel(got_ref, match_ref, factor_ref, head_ref, out_ref, packed, turned):
     low_lane = iota((32, 128), 1) < 64
     width = got_ref.shape[0]
-    slots = width * 128
 
     @pl.when(pl.program_id(0) == 0)
     def _():
@@ -561,9 +599,8 @@
             packed[32:64, lanes] = high
             packed[96:128, lanes] = low
 
-    blocks = slot_ref.shape[1]
-    wanted = as_bf16(iota((slots, blocks), 0) == slot_ref[...])
-    flux = jnp.dot(packed[...], wanted, preferred_element_type=F32)
+    blocks = match_ref.shape[1]
+    flux = jnp.dot(packed[...], match_ref[...], preferred_element_type=F32)
     flux = flux[0:64] + flux[64:128]
     for part in range(blocks // 128):
         lanes = slice(128 * part, 128 * part + 128)
@@ -574,28 +611,100 @@
         out_ref[lanes, :] = head_ref[lanes, :] + turned[part].T
 
 
-def top(got, slot, factor, head):
+def top(got, match, factors, head):
     blocks = head.shape[0]
     part = 2 * TILE
+    steps = blocks // part
+    half = steps // 2
+
+    def kernel(got_ref, match_ref, first_ref, second_ref, head_ref, out_ref, packed, turned):
+        step = pl.program_id(0)
+
+        @pl.when(step < half)
+        def _():
+            top_kernel(got_ref, match_ref, first_ref, head_ref, out_ref, packed, turned)
+
+        @pl.when(step >= half)
+        def _():
+            top_kernel(got_ref, match_ref, second_ref, head_ref, out_ref, packed, turned)
+
     return pl.pallas_call(
-        top_kernel,
-        grid=(blocks // part,),
+        kernel,
+        grid=(steps,),
         in_specs=[
             pl.BlockSpec(got.shape, lambda t: (0, 0, 0)),
-            pl.BlockSpec((1, part), lambda t: (0, t)),
-            pl.BlockSpec((part // 128, 64, 128), lambda t: (t, 7, 0)),
+            pl.BlockSpec((match.shape[0], part), lambda t: (0, t)),
+            pl.BlockSpec((part // 128, 64, 128), lambda t: (jnp.minimum(t, half - 1), 7, 0)),
+            pl.BlockSpec((part // 128, 64, 128), lambda t: (jnp.maximum(t - half, 0), 7, 0)),
             pl.BlockSpec((part, 128), lambda t: (t, 3)),
         ],
         out_specs=pl.BlockSpec((part, 128), lambda t: (t, 3)),
         out_shape=jax.ShapeDtypeStruct(head.shape, F32),
-        input_output_aliases={3: 0},
+        input_output_aliases={4: 0},
         scratch_shapes=[
             pltpu.VMEM((128, got.shape[0] * 128), BF16),
             pltpu.VMEM((part // 128, 128, 128), F32),
         ],
-        compiler_params=pltpu.CompilerParams(vmem_limit_bytes=40 * MIB),
+        compiler_params=pltpu.CompilerParams(vmem_limit_bytes=VMEM_LIMIT),
         name="top",
-    )(got, slot, factor, head)
+    )(got, match, *factors, head)
+
+
+def forward_kernel(place_ref, got_ref, rows_ref, after_ref, up_ref, down_ref):
+    gy, width = place_ref[2], got_ref.shape[0]
+    west = jnp.maximum(gy - 1, 0)
+    east = jnp.minimum(gy + 1, width - 1)
+    base = 40 * width
+    for number, ref in ((1, up_ref), (0, down_ref)):
+        for source in range(width):
+            ref[40 * source : 40 * source + 40, :] = got_ref[source, 32:72, :]
+        ref[base : base + 24, :] = rows_ref[number]
+        ref[base + 24 : base + 40, :] = got_ref[west, 72:88, :]
+        ref[base + 40 : base + 56, :] = got_ref[east, 72:88, :]
+
+
+def forward(place, got, rows, after):
+    width = got.shape[0]
+    shape = jax.ShapeDtypeStruct((40 * width + 56, 128), F32)
+    return pl.pallas_call(
+        forward_kernel,
+        in_specs=[SMEM, VMEM, VMEM, ANY],
+        out_specs=[VMEM, VMEM],
+        out_shape=[shape, shape],
+        compiler_params=pltpu.CompilerParams(vmem_limit_bytes=VMEM_LIMIT),
+        name="forward",
+    )(place, got, rows, after)
+
+
+def backward_kernel(place_ref, stay_ref, low_ref, high_ref, cols_ref, after_ref, send_ref):
+    gy, width = place_ref[2], stay_ref.shape[0]
+    base = 32 * width
+    sides = []
+    for kind in range(2):
+        lines = slice(base + 2 * kind, base + 2 * kind + 2)
+        sides.append(
+            jnp.concatenate(
+                [cols_ref[kind, 0:2, :], low_ref[lines, :], high_ref[lines, :], jnp.zeros((2, 128), F32)],
+                axis=0,
+            )
+        )
+    for number in range(width):
+        rows = slice(32 * number, 32 * number + 32)
+        send_ref[number, 0:32, :] = stay_ref[number]
+        send_ref[number, 32:64, :] = jnp.where(number >= gy, high_ref[rows, :], low_ref[rows, :])
+        send_ref[number, 64:72, :] = jnp.where(number == gy + 1, sides[1], sides[0])
+
+
+def backward(place, stay, low, high, cols, after):
+    width = stay.shape[0]
+    return pl.pallas_call(
+        backward_kernel,
+        in_specs=[SMEM, VMEM, VMEM, VMEM, VMEM, ANY],
+        out_specs=VMEM,
+        out_shape=jax.ShapeDtypeStruct((width, 72, 128), F32),
+        compiler_params=pltpu.CompilerParams(vmem_limit_bytes=VMEM_LIMIT),
+        name="backward",
+    )(place, stay, low, high, cols, after)
 
 
 def shifted(value, axis, steps, wrap=True):
@@ -615,17 +724,8 @@
         [gx * width + gy, gx, gy]
         + [jnp.int32(v) for v in (along * width, width, rows * along, cols * width, 0)]
     ).astype(I32)
-    meta = jnp.concatenate(
-        [
-            soil_class[None],
-            levels[None],
-            patch_of_block[None],
-            neighbors.T,
-            neighbor_levels.T,
-            jnp.zeros((1, blocks), I32),
-        ],
-        axis=0,
-    )
+    meta = jnp.stack([soil_class, levels, patch_of_block])
+    near = jnp.concatenate([neighbors.T, neighbor_levels.T], axis=0)
 
     def edge(part):
         classes = jnp.pad(soil_class[part].astype(F32)[None], ((0, 7), (0, 512 - HB)))
@@ -634,49 +734,29 @@
     low_edge = shifted(edge(slice(blocks - HB, blocks)), ("gx", "gy"), 1, wrap=False)
     high_edge = shifted(edge(slice(0, HB)), ("gx", "gy"), -1, wrap=False)
 
-    send, slot, edge_rows = route(place, meta, pressure, water_depth, bed_height, roughness, width)
+    send, slot, edge_rows, match = route(
+        place, meta, pressure, water_depth, bed_height, roughness, width
+    )
     got = lax.all_to_all(send, "gy", 0, 0)
-    halos = got[:, 72:88]
-    left = lax.dynamic_index_in_dim(halos, jnp.maximum(gy - 1, 0), 0, keepdims=False)
-    right = lax.dynamic_index_in_dim(halos, jnp.minimum(gy + 1, width - 1), 0, keepdims=False)
-    moving = got[:, 32:72].reshape(40 * width, 128)
-    from_low = shifted(jnp.concatenate([moving, edge_rows[1], left, right], axis=0), "gx", 1)
-    from_high = shifted(jnp.concatenate([moving, edge_rows[0], left, right], axis=0), "gx", -1)
-
-    base, factor, table = inside(soil_params, meta, pressure)
-
+    first = inside(soil_params, meta, pressure, slot, 0)
+    up, down = forward(place, got, edge_rows, first[0])
+    from_low = shifted(up, "gx", 1)
+    from_high = shifted(down, "gx", -1)
+    second = inside(soil_params, meta, pressure, up, 1)
     stay, back, tile, edge_cols = surface(
-        place, soil_params, got, from_low, from_high, water_depth, patches
+        place, soil_params, got, from_low, from_high, water_depth, patches, second[0]
     )
     back_high = shifted(back[0], "gx", -1)
     back_low = shifted(back[1], "gx", 1)
-
-    head = across(place, soil_params, meta, low_edge, high_edge, base, factor, table)
-
-    number = jnp.arange(width, dtype=I32)[:, None, None]
-    moved = jnp.where(
-        number >= gy,
-        back_high[: 32 * width].reshape(width, 32, 128),
-        back_low[: 32 * width].reshape(width, 32, 128),
+    head = across(place, soil_params, meta, near, low_edge, first, second[2], stay, 0, None)
+    reply = backward(place, stay, back_low, back_high, edge_cols, head)
+    returned = lax.all_to_all(reply, "gy", 0, 0)
+    head = across(place, soil_params, meta, near, high_edge, second, first[2], reply, 1, head)
+    new_depth = sweeps(
+        place, water_depth, bed_height, roughness, got, from_low, from_high, tile,
+        back_low, back_high, returned, head,
     )
-    above, below = back_low[32 * width :], back_high[32 * width :]
-
-    def side(kind):
-        lines = slice(2 * kind, 2 * kind + 2)
-        return jnp.concatenate(
-            [edge_cols[kind, 0:2], above[lines], below[lines], jnp.zeros((2, 128), F32)], axis=0
-        )
-
-    sides = jnp.where(number == gy + 1, side(1)[None], side(0)[None])
-    returned = lax.all_to_all(jnp.concatenate([stay, moved, sides], axis=1), "gy", 0, 0)
-    ends = returned[:, 64:72]
-    west = lax.dynamic_index_in_dim(ends, jnp.maximum(gy - 1, 0), 0, keepdims=False)
-    east = lax.dynamic_index_in_dim(ends, jnp.minimum(gy + 1, width - 1), 0, keepdims=False)
-    new_depth = sweeps(
-        place, water_depth, bed_height, roughness, left, right,
-        from_low[40 * width :], from_high[40 * width :], tile, above, below, west, east,
-    )
-    new_pressure = top(returned, slot, factor, head)
+    new_pressure = top(returned, match, (first[1], second[1]), head)
     return new_pressure, new_depth
 
 

time: 102 us -> 98.5 us (0.966)
  Pallas kernels: 41.3 us -> 57.8 us
  waiting for transfers between devices: 10.3 us -> 0.08 us
  local copies, waits for them, and re-layouts: 16.7 us -> 7.33 us
  starting transfers between devices: 30.5 us -> 28.6 us
  other arithmetic: 1.79 us -> 2.82 us
    pallas_call x5 -> x9, Pallas kernels: 37.7 us -> 52.9 us  [the longest x2 19 us: across(): pl.pallas_call(kernel_in, grid=(steps,), in_specs=[SMEM, SMEM, pl.BlockSp...]
    ppermute x6, waiting for transfers between devices: 10.2 us -> 0.07 us  [shifted(): return lax.ppermute(value, axis, pairs)]
    unnamed x24 -> x20, local copies, waits for them, and re-layouts: 11.9 us -> 4.47 us
    concatenate x2 -> x0, local copies, waits for them, and re-layouts: 2.68 us -> none  [the longest x1 2.61 us: per_device(): jnp.concatenate([soil_class[None], levels[None], patch_of_block[None], ne...]
    all_to_all x1, starting transfers between devices: 8.06 us -> 6.39 us  [per_device(): returned = lax.all_to_all(reply, 'gy', 0, 0)]
    another operation x0 -> x1, other arithmetic: none -> 1.36 us  [per_device(): meta = jnp.stack([soil_class, levels, patch_of_block])]
    pallas_call x1, Pallas kernels: 3.6 us -> 4.9 us  [surface(): pl.pallas_call(surface_kernel, in_specs=[SMEM, SMEM, VMEM, VMEM, VMEM, VM...]
  transfers between devices with their start and end apart: 8 -> 8, of which waited for: 4 -> 1; matrix products, arithmetic and copies ran while one was open for 4% -> 4% of each run, Pallas kernels for 29% -> 43%
where the time goes in v1:
time: 98.5 us; the launch traced here: 97.4 us
  Pallas kernels  57.8 us (59%)
  starting transfers between devices  28.6 us (29%)
  local copies, waits for them, and re-layouts  7.33 us (7%)
  other arithmetic  2.82 us (3%)
    pallas_call x2, Pallas kernels, across(): pl.pallas_call(kernel_in, grid=(steps,), in_specs=[SMEM, SMEM, pl.BlockSp...  19 us
    ppermute x6, starting transfers between devices, shifted(): return lax.ppermute(value, axis, pairs)  16.3 us
    pallas_call x2, Pallas kernels, inside(): pl.pallas_call(inside_kernel, grid=(steps,), in_specs=[SMEM, pl.BlockSpec...  14.5 us
    pallas_call x1, Pallas kernels, route(): pl.pallas_call(route_kernel, grid=(width,), in_specs=[SMEM, pl.BlockSpec(...  6.68 us
    all_to_all x1, starting transfers between devices, per_device(): returned = lax.all_to_all(reply, 'gy', 0, 0)  6.39 us
    all_to_all x1, starting transfers between devices, per_device(): got = lax.all_to_all(send, 'gy', 0, 0)  5.97 us
    pallas_call x1, Pallas kernels, top(): pl.pallas_call(kernel, grid=(steps,), in_specs=[pl.BlockSpec(got.shape, l...  5.35 us
    pallas_call x1, Pallas kernels, surface(): pl.pallas_call(surface_kernel, in_specs=[SMEM, SMEM, VMEM, VMEM, VMEM, VM...  4.9 us
  transfers between devices with their start and end apart: 8, of which 1 were waited for; matrix products, arithmetic and copies ran while one was open for 4% of the time, Pallas kernels for 43%

profile of v1, /device:TPU:1, one launch (start us, length us, event | category | flops | bytes accessed | tf_op | source)
XLA Modules:
  0.0 97.4 jit_solution(11478484307292645250)
XLA Ops:
  0.6 1.4 %pad_add_fusion.1.meta_ref.refs_2_ = s32[3,2048]{1,0:T(4,128)} fusion(s32[1,2048]{1,0:T(1,128)} %bitcast.17, s32[1,2048]{1,0:T(1,128)} %bitcast.18, s32[1,2048]{1,0:T(1,128)} %bitcast.16), kind=kLoop, calls=%fused_computation.6 | loop fusion | flops 12288 | bytes 49152 | tf_op jit(solution)/shard_map/stack | solution.py:727
  2.0 0.6 stack.27.place_ref.refs_0_
  2.6 6.7 %route.1 = (f32[8,88,128]{2,1,0:T(8,128)}, s32[1,2048]{1,0:T(1,128)}, f32[2,24,128]{2,1,0:T(8,128)}, bf16[1024,2048]{1,0:T(8,128)(2,1)}) custom-call(s32[8]{0:T(128)} %stack.27.place_ref.refs_0_, s32[3,2048]{1,0:T(4,128)} %pad_add_fusion.1.meta_ref.refs_2_, f32[2048,512]{1,0:T(8,128)} %head_ref.3, f32[128,256]{1,0:T(8,128)} %depth_ref.5, ...), custom_call_target="tpu_custom_call" | custom-call | tf_op jit(solution)/shard_map/route/pallas_call | solution.py:171
  9.3 6.0 %all-to-all-start = ((f32[8,88,128]{2,1,0:T(8,128)}), f32[8,88,128]{2,1,0:T(8,128)S(1)}, u32[]{:S(2)}, u32[]{:S(2)}) async-start(f32[8,88,128]{2,1,0:T(8,128)} %get-tuple-element.18), calls=%async_computation | async-start | bytes 720896 | tf_op jit(solution)/shard_map/all_to_all | solution.py:740
  15.3 1.3 %fusion = (f32[256,512]{1,0:T(8,128)S(1)}, f32[256,512]{1,0:T(8,128)S(1)}) fusion(f32[2048,512]{1,0:T(8,128)} %head_ref.3), kind=kLoop, calls=%fused_computation.9 | loop fusion | bytes 2097152 | tf_op jit(solution)/shard_map/slice | solution.py:732
  16.5 0.7 slice_convert_fusion
  17.3 3.5 %collective-permute-start.4 = (f32[264,512]{1,0:T(8,128)S(1)}, f32[264,512]{1,0:T(8,128)S(1)}, u32[]{:S(2)}, u32[]{:S(2)}) collective-permute-start(f32[264,512]{1,0:T(8,128)S(1)} %select_maximum_fusion.1), channel_id=1, source_target_pairs={{0,1},{1,2},{2,3},{3,4},{4,5},{5,6},{6,7},{7,8},{8,9},{9,10},{10,1... | collective-permute-start | bytes 1622024 | tf_op jit(solution)/shard_map/ppermute | solution.py:713
  20.8 0.0 copy-start.8
  20.8 0.0 copy-start.9
  20.9 1.9 %collective-permute-start.5 = (f32[264,512]{1,0:T(8,128)S(1)}, f32[264,512]{1,0:T(8,128)S(1)}, u32[]{:S(2)}, u32[]{:S(2)}) collective-permute-start(f32[264,512]{1,0:T(8,128)S(1)} %select_maximum_fusion), channel_id=1, source_target_pairs={{1,0},{2,1},{3,2},{4,3},{5,4},{6,5},{7,6},{8,7},{9,8},{10,9},{11,1... | collective-permute-start | bytes 1622024 | tf_op jit(solution)/shard_map/ppermute | solution.py:713
  22.8 7.3 %inside.2 = (f32[8,512,128]{2,1,0:T(8,128)}, f32[8,512,128]{2,1,0:T(8,128)}, bf16[1536,1024]{1,0:T(8,128)(2,1)}) custom-call(f32[5,12]{1,0:T(8,128)} %refs_1_.1, s32[3,2048]{1,0:T(4,128)} %pad_add_fusion.1.meta_ref.refs_2_, f32[2048,512]{1,0:T(8,128)} %head_ref.3, s32[1,2048]{1,0:T(1,128)} %get-tuple-element.20.after_ref), custom_call_target="tpu_custom_call" | custom-call | flops 31457280 | bytes 9437184 | tf_op jit(solution)/shard_map/inside/pallas_call | solution.py:450
  30.1 0.0 all-to-all-done.got_ref
  30.1 0.0 copy-start
  30.1 0.7 copy-done
  30.8 1.8 %forward.1 = (f32[376,128]{1,0:T(8,128)}, f32[376,128]{1,0:T(8,128)}) custom-call(s32[8]{0:T(128)} %stack.27.place_ref.refs_0_, f32[8,88,128]{2,1,0:T(8,128)} %copy-done, f32[2,24,128]{2,1,0:T(8,128)} %get-tuple-element.19.rows_ref, f32[8,512,128]{2,1,0:T(8,128)} %get-tuple-element.21.after_ref.base_ref), custom_call_target="tpu_custom_call" | custom-call | tf_op jit(solution)/shard_map/forward/pallas_call | solution.py:669
  32.6 6.0 %collective-permute-start.1 = (f32[376,128]{1,0:T(8,128)}, f32[376,128]{1,0:T(8,128)S(1)}, u32[]{:S(2)}, u32[]{:S(2)}) collective-permute-start(f32[376,128]{1,0:T(8,128)} %get-tuple-element.23), channel_id=1, source_target_pairs={{0,120},{8,0},{16,8},{24,16},{32,24},{40,32},{48,40},{56,48},{64,5... | collective-permute-start | bytes 577544 | tf_op jit(solution)/shard_map/ppermute | solution.py:713
  38.6 0.0 collective-permute-start
  38.6 0.0 copy-done.8
  38.6 0.0 copy-done.9
  38.6 0.7 pad_add_fusion.near_ref.refs_3_
  39.2 7.2 %inside.3 = (f32[8,512,128]{2,1,0:T(8,128)}, f32[8,512,128]{2,1,0:T(8,128)}, bf16[1536,1024]{1,0:T(8,128)(2,1)}) custom-call(f32[5,12]{1,0:T(8,128)} %refs_1_.1, s32[3,2048]{1,0:T(4,128)} %pad_add_fusion.1.meta_ref.refs_2_, f32[2048,512]{1,0:T(8,128)} %head_ref.3, f32[376,128]{1,0:T(8,128)} %get-tuple-element.22.after_ref), custom_call_target="tpu_custom_call" | custom-call | flops 31457280 | bytes 9437184 | tf_op jit(solution)/shard_map/inside/pallas_call | solution.py:450
  46.5 0.0 collective-permute-done.1.down_ref
  46.5 0.0 copy-start.2
  46.5 0.1 collective-permute-done.up_ref
  46.6 0.6 copy-done.2
  47.2 0.1 copy-done.3
  47.3 4.9 %surface.1 = (f32[8,32,128]{2,1,0:T(8,128)}, f32[2,264,128]{2,1,0:T(8,128)}, f32[128,256]{1,0:T(8,128)}, f32[2,8,128]{2,1,0:T(8,128)}) custom-call(s32[8]{0:T(128)} %stack.27.place_ref.refs_0_, f32[5,12]{1,0:T(8,128)} %refs_1_.1, f32[8,88,128]{2,1,0:T(8,128)} %copy-done, f32[376,128]{1,0:T(8,128)} %copy-done.3, f32[376,128]{1,0:T(8,128)} %copy-done.2, ...), custom_call_target="tpu_custom_call" | custom-call | tf_op jit(solution)/shard_map/surface/pallas_call | solution.py:290
  52.1 1.0 %slice_bitcast_fusion = (f32[264,128]{1,0:T(8,128)S(1)}, f32[264,128]{1,0:T(8,128)S(1)}) fusion(f32[2,264,128]{2,1,0:T(8,128)} %get-tuple-element.26), kind=kLoop, calls=%fused_computation.3 | loop fusion | bytes 540672 | tf_op jit(solution)/shard_map/squeeze | solution.py:749
  53.1 4.8 %collective-permute-start.3 = (f32[264,128]{1,0:T(8,128)S(1)}, f32[264,128]{1,0:T(8,128)S(1)}, u32[]{:S(2)}, u32[]{:S(2)}) collective-permute-start(f32[264,128]{1,0:T(8,128)S(1)} %get-tuple-element.36), channel_id=1, source_target_pairs={{0,120},{8,0},{16,8},{24,16},{32,24},{40,32},{48,40},{56,48},{64,5... | collective-permute-start | bytes 405512 | tf_op jit(solution)/shard_map/ppermute | solution.py:713
  58.0 0.0 collective-permute-start.2
  58.0 0.0 collective-permute-done.4.edge_ref
  58.0 0.8 copy-done.7
  58.8 9.5 %across.2.after_ref.refs_10_ = f32[2048,512]{1,0:T(8,128)} custom-call(s32[8]{0:T(128)} %stack.27.place_ref.refs_0_, f32[5,12]{1,0:T(8,128)} %refs_1_.1, s32[3,2048]{1,0:T(4,128)} %pad_add_fusion.1.meta_ref.refs_2_, s32[12,2048]{1,0:T(8,128)} %pad_add_fusion.near_ref.refs_3_, f32[264,512]{1,0:T(8,128)} %copy-done.7, ...), custom_call_target="tpu_custom_call" | custom-call | flops 2415919104 | bytes 9437184 | tf_op jit(solution)/shard_map/across/pallas_call | solution.py:555
  68.3 0.0 collective-permute-done.3.high_ref
  68.3 0.0 copy-start.4
  68.3 0.0 collective-permute-done.2.low_ref
  68.3 0.0 copy-start.5
  68.3 0.6 copy-done.4
  69.0 0.1 copy-done.5
  69.0 1.8 %backward.1.refs_9_ = f32[8,72,128]{2,1,0:T(8,128)} custom-call(s32[8]{0:T(128)} %stack.27.place_ref.refs_0_, f32[8,32,128]{2,1,0:T(8,128)} %get-tuple-element.25.after_ref.stay_ref, f32[264,128]{1,0:T(8,128)} %copy-done.5, f32[264,128]{1,0:T(8,128)} %copy-done.4, f32[2,8,128]{2,1,0:T(8,128)} %get-tuple-element.27.cols_ref, f32[2048,512]{1,0:T(8,128)} %across.2.after_ref.refs_10_), custom_call_target="tpu_custom_call" | custom-call | tf_op jit(solution)/shard_map/backward/pallas_call | solution.py:700
  70.8 6.4 %all-to-all-start.1 = ((f32[8,72,128]{2,1,0:T(8,128)}), f32[8,72,128]{2,1,0:T(8,128)S(1)}, u32[]{:S(2)}, u32[]{:S(2)}) async-start(f32[8,72,128]{2,1,0:T(8,128)} %backward.1.refs_9_), calls=%async_computation.1 | async-start | bytes 589824 | tf_op jit(solution)/shard_map/all_to_all | solution.py:753
  77.2 0.0 collective-permute-done.5.refs_4_
  77.2 0.8 copy-done.6
  78.0 9.5 %across.3.head_ref.after_ref = f32[2048,512]{1,0:T(8,128)} custom-call(s32[8]{0:T(128)} %stack.27.place_ref.refs_0_, f32[5,12]{1,0:T(8,128)} %refs_1_.1, s32[3,2048]{1,0:T(4,128)} %pad_add_fusion.1.meta_ref.refs_2_, s32[12,2048]{1,0:T(8,128)} %pad_add_fusion.near_ref.refs_3_, f32[264,512]{1,0:T(8,128)} %copy-done.6, ...), custom_call_target="tpu_custom_call", output_to_operand_aliasing={{}: (10, {})} | custom-call | flops 2415919104 | bytes 9437184 | tf_op jit(solution)/shard_map/across/pallas_call | solution.py:555
  87.5 0.0 all-to-all-done.1.got_ref.back_ref
  87.5 0.7 copy-done.1
  88.2 3.8 %sweeps.1 = f32[128,256]{1,0:T(8,128)} custom-call(s32[8]{0:T(128)} %stack.27.place_ref.refs_0_, f32[128,256]{1,0:T(8,128)} %depth_ref.5, f32[128,256]{1,0:T(8,128)} %bed_ref.3, f32[128,256]{1,0:T(8,128)} %rough_ref.3, f32[8,88,128]{2,1,0:T(8,128)} %copy-done, f32[376,128]{1,0:T(8,128)} %copy-done.3, f32[376,128]{1,0:T(8,128)} %copy-done.2, ...), custom_call_target="tpu_custom_call" | custom-call | tf_op jit(solution)/shard_map/sweeps/pallas_call | solution.py:391
  92.1 5.4 %top.1 = f32[2048,512]{1,0:T(8,128)} custom-call(f32[8,72,128]{2,1,0:T(8,128)} %copy-done.1, bf16[1024,2048]{1,0:T(8,128)(2,1)} %get-tuple-element.31.match_ref, f32[8,512,128]{2,1,0:T(8,128)} %get-tuple-element.28.factor_ref.first_ref, f32[8,512,128]{2,1,0:T(8,128)} %get-tuple-element.32.refs_6_.second_ref, ...), custom_call_target="tpu_custom_call", output_to_operand_aliasing={{}: (4, {})} | custom-call | tf_op jit(solution)/shard_map/top/pallas_call | solution.py:631
  (7 shorter events, 0.1 us)
Async XLA Ops:
  9.3 20.8 %all-to-all-start = ((f32[8,88,128]{2,1,0:T(8,128)}), f32[8,88,128]{2,1,0:T(8,128)S(1)}, u32[]{:S(2)}, u32[]{:S(2)}) async-start(f32[8,88,128]{2,1,0:T(8,128)} %get-tuple-element.18), calls=%async_computation | async-start | bytes 720896 | tf_op jit(solution)/shard_map/all_to_all | solution.py:740
  17.3 40.7 %collective-permute-start.4 = (f32[264,512]{1,0:T(8,128)S(1)}, f32[264,512]{1,0:T(8,128)S(1)}, u32[]{:S(2)}, u32[]{:S(2)}) collective-permute-start(f32[264,512]{1,0:T(8,128)S(1)} %select_maximum_fusion.1), channel_id=1, source_target_pairs={{0,1},{1,2},{2,3},{3,4},{4,5},{5,6},{6,7},{7,8},{8,9},{9,10},{10,1... | collective-permute-start | bytes 1622024 | tf_op jit(solution)/shard_map/ppermute | solution.py:713
  20.8 17.7 %copy-start.8 = (s32[2048,6]{0,1:T(8,128)S(1)}, s32[2048,6]{0,1:T(8,128)}, u32[]{:S(2)}) copy-start(s32[2048,6]{0,1:T(8,128)} %param.14) | copy-start | bytes 147460
  20.8 17.7 %copy-start.9 = (s32[2048,6]{0,1:T(8,128)S(1)}, s32[2048,6]{0,1:T(8,128)}, u32[]{:S(2)}) copy-start(s32[2048,6]{0,1:T(8,128)} %param.13) | copy-start | bytes 147460
  20.9 56.3 %collective-permute-start.5 = (f32[264,512]{1,0:T(8,128)S(1)}, f32[264,512]{1,0:T(8,128)S(1)}, u32[]{:S(2)}, u32[]{:S(2)}) collective-permute-start(f32[264,512]{1,0:T(8,128)S(1)} %select_maximum_fusion), channel_id=1, source_target_pairs={{1,0},{2,1},{3,2},{4,3},{5,4},{6,5},{7,6},{8,7},{9,8},{10,9},{11,1... | collective-permute-start | bytes 1622024 | tf_op jit(solution)/shard_map/ppermute | solution.py:713
  30.1 0.8 copy-start
  32.6 13.9 %collective-permute-start.1 = (f32[376,128]{1,0:T(8,128)}, f32[376,128]{1,0:T(8,128)S(1)}, u32[]{:S(2)}, u32[]{:S(2)}) collective-permute-start(f32[376,128]{1,0:T(8,128)} %get-tuple-element.23), channel_id=1, source_target_pairs={{0,120},{8,0},{16,8},{24,16},{32,24},{40,32},{48,40},{56,48},{64,5... | collective-permute-start | bytes 577544 | tf_op jit(solution)/shard_map/ppermute | solution.py:713
  38.6 8.0 %collective-permute-start = (f32[376,128]{1,0:T(8,128)}, f32[376,128]{1,0:T(8,128)S(1)}, u32[]{:S(2)}, u32[]{:S(2)}) collective-permute-start(f32[376,128]{1,0:T(8,128)} %get-tuple-element.22.after_ref), channel_id=1, source_target_pairs={{0,8},{8,16},{16,24},{24,32},{32,40},{40,48},{48,56},{56,64},{64,7... | collective-permute-start | bytes 577544 | tf_op jit(solution)/shard_map/ppermute | solution.py:713
  46.5 0.7 copy-start.2
  46.6 0.7 copy-start.3
  53.1 15.2 %collective-permute-start.3 = (f32[264,128]{1,0:T(8,128)S(1)}, f32[264,128]{1,0:T(8,128)S(1)}, u32[]{:S(2)}, u32[]{:S(2)}) collective-permute-start(f32[264,128]{1,0:T(8,128)S(1)} %get-tuple-element.36), channel_id=1, source_target_pairs={{0,120},{8,0},{16,8},{24,16},{32,24},{40,32},{48,40},{56,48},{64,5... | collective-permute-start | bytes 405512 | tf_op jit(solution)/shard_map/ppermute | solution.py:713
  58.0 10.3 %collective-permute-start.2 = (f32[264,128]{1,0:T(8,128)S(1)}, f32[264,128]{1,0:T(8,128)S(1)}, u32[]{:S(2)}, u32[]{:S(2)}) collective-permute-start(f32[264,128]{1,0:T(8,128)S(1)} %get-tuple-element.37), channel_id=1, source_target_pairs={{0,8},{8,16},{16,24},{24,32},{32,40},{40,48},{48,56},{56,64},{64,7... | collective-permute-start | bytes 405512 | tf_op jit(solution)/shard_map/ppermute | solution.py:713
  58.0 0.8 copy-start.7
  68.3 0.7 copy-start.4
  68.3 0.7 copy-start.5
  70.8 16.7 %all-to-all-start.1 = ((f32[8,72,128]{2,1,0:T(8,128)}), f32[8,72,128]{2,1,0:T(8,128)S(1)}, u32[]{:S(2)}, u32[]{:S(2)}) async-start(f32[8,72,128]{2,1,0:T(8,128)} %backward.1.refs_9_), calls=%async_computation.1 | async-start | bytes 589824 | tf_op jit(solution)/shard_map/all_to_all | solution.py:753
  77.2 0.8 copy-start.6
  87.5 0.7 copy-start.1

commit v2 on v1

--- a/solution.py
+++ b/solution.py
@@ -80,12 +80,14 @@
     return ref[half, start : start + 64, :]
 
 
-def write_faces(head_ref, cond_ref, half, put):
+def write_faces(head_ref, cond_ref, half, slot, table):
+    lanes = pl.ds(pl.multiple_of(slot * TILE, TILE) + 128 * half, 128)
     for face in range(6):
         head_high, head_low = split(face_rows(head_ref, half, face))
         cond_high, cond_low = split(face_rows(cond_ref, half, face))
         for part, value in enumerate((head_high, head_low, cond_high, cond_low)):
-            put(256 * face + 64 * part, half, value)
+            row = 256 * face + 64 * part
+            table[row : row + 64, lanes] = value
 
 
 def route_kernel(place_ref, meta_ref, top_ref, depth_ref, bed_ref, rough_ref,
@@ -399,23 +401,43 @@
     )(place, water_depth, *rest)
 
 
-def inside_kernel(soil_ref, meta_ref, head_ref, after_ref, base_ref, factor_ref, table_ref, turned, cond):
+def halo_tile(soil_ref, classes, source, slot, table, turned, cond):
+    for half in range(TILE // 128):
+        lanes = slice(128 * half, 128 * half + 128)
+        turned[half] = source(lanes).T
+        soil = soil_rows(soil_ref, classes(lanes))
+        for k in range(8):
+            rows = slice(64 * k, 64 * k + 64)
+            cond[half, rows, :] = curve(turned[half, rows, :], soil)[0]
+        write_faces(turned, cond, half, slot, table)
+
+
+def inner_tile(soil_ref, meta_ref, head_ref, slot, table, turned, cond, base_sc, factor_sc, top_ref):
     open_i = iota((8, 8, 128), 1) < 7
     nothing = jnp.zeros((1, 8, 128), F32)
-    for half in range(head_ref.shape[0] // 128):
+    for half in range(TILE // 128):
         lanes = slice(128 * half, 128 * half + 128)
+        at = 2 * (slot - 1) + half
         turned[half] = head_ref[lanes, :].T
         soil = soil_rows(soil_ref, meta_ref[0:1, lanes])
         width = cell_width(meta_ref[1:2, lanes])
         half_over = 0.5 / width
         scaled = SUB_STEP / width
-        for k in range(8):
+
+        def conduct(k):
             rows = slice(64 * k, 64 * k + 64)
             conductivity, base, ratio = curve(turned[half, rows, :], soil)
             cond[half, rows, :] = conductivity
-            factor_ref[half, rows, :] = scaled * base / (soil[4] * ratio + STORAGE * base)
+            factor = scaled * base / (soil[4] * ratio + STORAGE * base)
+            factor_sc[at, rows, :] = factor
+            if k == 7:
+                top_ref[half] = factor
+
+        conduct(0)
         below = None
         for k in range(8):
+            if k < 7:
+                conduct(k + 1)
             rows = slice(64 * k, 64 * k + 64)
             head = turned[half, rows, :].reshape(8, 8, 128)
             cnd = cond[half, rows, :].reshape(8, 8, 128)
@@ -433,89 +455,22 @@
             if below is not None:
                 inflow = inflow - below
             below = flux
-            base_ref[half, rows, :] = (
-                turned[half, rows, :] + factor_ref[half, rows, :] * inflow.reshape(64, 128)
+            base_sc[at, rows, :] = (
+                turned[half, rows, :] + factor_sc[at, rows, :] * inflow.reshape(64, 128)
             )
-
-    def put(row, half, value):
-        table_ref[row : row + 64, 128 * half : 128 * half + 128] = value
-
-    for half in range(head_ref.shape[0] // 128):
-        write_faces(turned, cond, half, put)
-
-
-def inside(soil, meta, pressure, after, part):
-    blocks = pressure.shape[0] // 2
-    steps = blocks // TILE
-    return pl.pallas_call(
-        inside_kernel,
-        grid=(steps,),
-        in_specs=[
-            SMEM,
-            pl.BlockSpec((meta.shape[0], TILE), lambda t: (0, t + part * steps)),
-            pl.BlockSpec((TILE, 512), lambda t: (t + part * steps, 0)),
-            ANY,
-        ],
-        out_specs=[
-            pl.BlockSpec((TILE // 128, 512, 128), lambda t: (t, 0, 0)),
-            pl.BlockSpec((TILE // 128, 512, 128), lambda t: (t, 0, 0)),
-            pl.BlockSpec((1536, TILE), lambda t: (0, t)),
-        ],
-        out_shape=[
-            jax.ShapeDtypeStruct((blocks // 128, 512, 128), F32),
-            jax.ShapeDtypeStruct((blocks // 128, 512, 128), F32),
-            jax.ShapeDtypeStruct((1536, blocks), BF16),
-        ],
-        scratch_shapes=[pltpu.VMEM((TILE // 128, 512, 128), F32)] * 2,
-        compiler_params=pltpu.CompilerParams(vmem_limit_bytes=VMEM_LIMIT),
-        cost_estimate=pl.CostEstimate(flops=blocks * 512 * 60, bytes_accessed=blocks * 512 * 18, transcendentals=blocks * 512 * 5),
-        name="inside",
-    )(soil, meta, pressure, after)
-
-
-def across_kernel(part, place_ref, soil_ref, meta_ref, near_ref, edge_ref, base_ref, factor_ref, table_ref,
-                  other_ref, after_ref, out_ref, table, turned, cond, arrived):
-    step = pl.program_id(0)
-    blocks = table_ref.shape[1]
-    start = (0, HB + blocks)[part]
-
-    @pl.when(step == 0)
-    def _():
-        own_copy = pltpu.make_async_copy(table_ref, table.at[:, pl.ds(HB, blocks)], arrived.at[0])
-        own_copy.start()
-        next_copy = pltpu.make_async_copy(
-            other_ref.at[:, pl.ds((0, blocks - HB)[part], HB)],
-            table.at[:, pl.ds((HB + blocks, 0)[part], HB)],
-            arrived.at[1],
-        )
-        next_copy.start()
-
-        def put(row, half, value):
-            table[row : row + 64, start + 128 * half : start + 128 * half + 128] = value
-
-        for half in range(HB // 128):
-            lanes = slice(128 * half, 128 * half + 128)
-            turned[half] = edge_ref[lanes, :].T
-            classes = edge_ref[HB : HB + 8, lanes][0:1, :].astype(I32)
-            soil = soil_rows(soil_ref, classes)
-            for k in range(8):
-                rows = slice(64 * k, 64 * k + 64)
-                cond[half, rows, :] = curve(turned[half, rows, :], soil)[0]
-            write_faces(turned, cond, half, put)
-        own_copy.wait()
-        next_copy.wait()
-
-    turned[...] = base_ref[...]
-    window = pl.ds(pl.multiple_of(step * TILE, TILE), TILE + 2 * HB)
-    own = pl.ds(pl.multiple_of(step * TILE + HB, TILE), TILE)
-    width = cell_width(meta_ref[1:2, :])
-    first_row = (2 * place_ref[0] + part) * blocks - HB + step * TILE
+        write_faces(turned, cond, half, slot, table)
+
+
+def face_tile(first_row, levels, near_ref, slot, table, base_sc, factor_sc, out_ref):
+    width = cell_width(levels)
+    window = pl.ds(pl.multiple_of((slot - 1) * TILE, TILE), 3 * TILE)
+    own = pl.ds(pl.multiple_of(slot * TILE, TILE), TILE)
     for face in range(6):
         neighbor = near_ref[face : face + 1, :]
         far_width = cell_width(near_ref[6 + face : 7 + face, :])
         over_gap = 2.0 / (width + far_width)
         half = jnp.where(neighbor >= 0, 0.5, 0.0)
-        chosen = as_bf16(iota((TILE + 2 * HB, TILE), 0) == neighbor - first_row)
+        chosen = as_bf16(iota((3 * TILE, TILE), 0) == neighbor - first_row)
         there = 256 * OPPOSITE[face]
         far = jnp.dot(table[there : there + 256, window], chosen, preferred_element_type=F32)
         near = table[256 * face : 256 * face + 256, own].astype(F32)
@@ -523,64 +478,135 @@
         conds = (far[128:192] + near[128:192]) + (far[192:256] + near[192:256])
         flux = conds * half * (head_diff * over_gap + GRAVITY[face])
         for part in range(TILE // 128):
+            at = 2 * (slot - 1) + part
             added = flux[:, 128 * part : 128 * part + 128]
             if face < 2:
                 rows = pl.ds(7 * face, 64, stride=8)
-                turned[part, rows, :] += factor_ref[part, rows, :] * added
+                base_sc[at, rows, :] += factor_sc[at, rows, :] * added
             elif face < 4:
                 for k in range(8):
-                    at = slice(64 * k + 56 * (face - 2), 64 * k + 56 * (face - 2) + 8)
-                    turned[part, at, :] += factor_ref[part, at, :] * added[8 * k : 8 * k + 8]
+                    rows = slice(64 * k + 56 * (face - 2), 64 * k + 56 * (face - 2) + 8)
+                    base_sc[at, rows, :] += factor_sc[at, rows, :] * added[8 * k : 8 * k + 8]
             else:
-                at = slice(448 * (face - 4), 448 * (face - 4) + 64)
-                turned[part, at, :] += factor_ref[part, at, :] * added
+                rows = slice(448 * (face - 4), 448 * (face - 4) + 64)
+                base_sc[at, rows, :] += factor_sc[at, rows, :] * added
     for part in range(TILE // 128):
-        out_ref[128 * part : 128 * part + 128, :] = turned[part].T
-
-
-def across(place, soil, meta, near, edge, inner, other, after, part, head):
-    base, factor, table = inner
-    blocks = table.shape[1]
-    steps = blocks // TILE
-    kernel = functools.partial(across_kernel, part)
+        out_ref[128 * part : 128 * part + 128, :] = base_sc[2 * (slot - 1) + part].T
+
+
+def cells_kernel(part, inner, place_ref, soil_ref, meta_ref, head_ref, edge_ref, own_ref, near_ref, after_ref,
+                 out_ref, top_ref, table, turned, cond, base_sc, factor_sc):
+    step = pl.program_id(0)
+    last = inner + 1
+    blocks = inner * TILE
+
+    def at_edge():
+        halo_tile(
+            soil_ref,
+            lambda lanes: edge_ref[HB : HB + 8, lanes][0:1, :].astype(I32),
+            lambda lanes: edge_ref[lanes, :],
+            step, table, turned, cond,
+        )
+
+    def beside():
+        halo_tile(
+            soil_ref,
+            lambda lanes: meta_ref[0:1, lanes],
+            lambda lanes: head_ref[lanes, :],
+            step, table, turned, cond,
+        )
+
+    def within():
+        inner_tile(
+            soil_ref, meta_ref, head_ref, step, table, turned, cond, base_sc, factor_sc, top_ref
+        )
+
+    def faces():
+        slot = step - 2
+        first_row = (2 * place_ref[0] + part) * blocks + (slot - 2) * TILE
+        face_tile(
+            first_row, own_ref[1:2, :], near_ref, slot, table, base_sc, factor_sc, out_ref
+        )
+
+    first, final = (at_edge, beside) if part == 0 else (beside, at_edge)
+
+    @pl.when(step == 0)
+    def _():
+        first()
+
+    @pl.when((step > 0) & (step < 3))
+    def _():
+        within()
+
+    @pl.when((step >= 3) & (step < last))
+    def _():
+        faces()
+        within()
+
+    @pl.when(step == last)
+    def _():
+        faces()
+        final()
+
+    @pl.when(step == last + 1)
+    def _():
+        faces()
+
+
+def cells(place, soil, meta, near, pressure, edge, after, part, head):
+    inner = pressure.shape[0] // TILE // 2
+    tiles = 2 * inner
+    kernel = functools.partial(cells_kernel, part, inner)
     kernel_in = kernel
     aliases = {}
     extra, extra_specs = [], []
     if head is not None:
         def kernel_in(*refs):
-            kernel(*refs[:10], *refs[11:])
-
-        aliases = {10: 0}
+            kernel(*refs[:8], *refs[9:])
+
+        aliases = {8: 0}
         extra, extra_specs = [head], [ANY]
+    low = part * inner
+    seen = lambda t: jnp.clip(t + low - 1, max(low - 1, 0), min(low + inner, tiles - 1))
+    done = lambda t: jnp.clip(t + low - 3, low, low + inner - 1)
     return pl.pallas_call(
         kernel_in,
-        grid=(steps,),
+        grid=(inner + 3,),
         in_specs=[
             SMEM,
             SMEM,
-            pl.BlockSpec((meta.shape[0], TILE), lambda t: (0, t + part * steps)),
-            pl.BlockSpec((near.shape[0], TILE), lambda t: (0, t + part * steps)),
+            pl.BlockSpec((meta.shape[0], TILE), lambda t: (0, seen(t))),
+            pl.BlockSpec((TILE, 512), lambda t: (seen(t), 0)),
             pl.BlockSpec(edge.shape, lambda t: (0, 0)),
-            pl.BlockSpec((TILE // 128, 512, 128), lambda t: (t, 0, 0)),
-            pl.BlockSpec((TILE // 128, 512, 128), lambda t: (t, 0, 0)),
-            ANY,
-            ANY,
+            pl.BlockSpec((meta.shape[0], TILE), lambda t: (0, done(t))),
+            pl.BlockSpec((near.shape[0], TILE), lambda t: (0, done(t))),
             ANY,
         ]
         + extra_specs,
-        out_specs=pl.BlockSpec((TILE, 512), lambda t: (t + part * steps, 0)),
-        out_shape=jax.ShapeDtypeStruct((2 * blocks, 512), F32),
+        out_specs=[
+            pl.BlockSpec((TILE, 512), lambda t: (done(t), 0)),
+            pl.BlockSpec((TILE // 128, 64, 128), lambda t: (jnp.clip(t - 1, 0, inner - 1), 0, 0)),
+        ],
+        out_shape=[
+            jax.ShapeDtypeStruct(pressure.shape, F32),
+            jax.ShapeDtypeStruct((2 * inner, 64, 128), F32),
+        ],
         input_output_aliases=aliases,
         scratch_shapes=[
-            pltpu.VMEM((1536, blocks + 2 * HB), BF16),
+            pltpu.VMEM((1536, (inner + 2) * TILE), BF16),
             pltpu.VMEM((TILE // 128, 512, 128), F32),
             pltpu.VMEM((TILE // 128, 512, 128), F32),
-            pltpu.SemaphoreType.DMA((2,)),
+            pltpu.VMEM((2 * inner, 512, 128), F32),
+            pltpu.VMEM((2 * inner, 512, 128), F32),
         ],
         compiler_params=pltpu.CompilerParams(vmem_limit_bytes=VMEM_LIMIT),
-        cost_estimate=pl.CostEstimate(flops=steps * 6 * 2 * 256 * 256 * 768, bytes_accessed=blocks * 512 * 18, transcendentals=0),
-        name="across",
-    )(place, soil, meta, near, edge, base, factor, table, other, after, *extra)
+        cost_estimate=pl.CostEstimate(
+            flops=inner * 6 * 2 * 256 * 256 * 768,
+            bytes_accessed=inner * TILE * 512 * 16,
+            transcendentals=inner * TILE * 512 * 8,
+        ),
+        name="cells",
+    )(place, soil, meta, pressure, edge, meta, near, after, *extra)
 
 
 def top_kernel(got_ref, match_ref, factor_ref, head_ref, out_ref, packed, turned):
@@ -634,8 +660,8 @@
         in_specs=[
             pl.BlockSpec(got.shape, lambda t: (0, 0, 0)),
             pl.BlockSpec((match.shape[0], part), lambda t: (0, t)),
-            pl.BlockSpec((part // 128, 64, 128), lambda t: (jnp.minimum(t, half - 1), 7, 0)),
-            pl.BlockSpec((part // 128, 64, 128), lambda t: (jnp.maximum(t - half, 0), 7, 0)),
+            pl.BlockSpec((part // 128, 64, 128), lambda t: (jnp.minimum(t, half - 1), 0, 0)),
+            pl.BlockSpec((part // 128, 64, 128), lambda t: (jnp.maximum(t - half, 0), 0, 0)),
             pl.BlockSpec((part, 128), lambda t: (t, 3)),
         ],
         out_specs=pl.BlockSpec((part, 128), lambda t: (t, 3)),
@@ -738,25 +764,23 @@
         place, meta, pressure, water_depth, bed_height, roughness, width
     )
     got = lax.all_to_all(send, "gy", 0, 0)
-    first = inside(soil_params, meta, pressure, slot, 0)
-    up, down = forward(place, got, edge_rows, first[0])
+    up, down = forward(place, got, edge_rows, slot)
     from_low = shifted(up, "gx", 1)
     from_high = shifted(down, "gx", -1)
-    second = inside(soil_params, meta, pressure, up, 1)
+    head, first = cells(place, soil_params, meta, near, pressure, low_edge, up, 0, None)
     stay, back, tile, edge_cols = surface(
-        place, soil_params, got, from_low, from_high, water_depth, patches, second[0]
+        place, soil_params, got, from_low, from_high, water_depth, patches, first
     )
     back_high = shifted(back[0], "gx", -1)
     back_low = shifted(back[1], "gx", 1)
-    head = across(place, soil_params, meta, near, low_edge, first, second[2], stay, 0, None)
-    reply = backward(place, stay, back_low, back_high, edge_cols, head)
+    head, second = cells(place, soil_params, meta, near, pressure, high_edge, stay, 1, head)
+    reply = backward(place, stay, back_low, back_high, edge_cols, second)
     returned = lax.all_to_all(reply, "gy", 0, 0)
-    head = across(place, soil_params, meta, near, high_edge, second, first[2], reply, 1, head)
     new_depth = sweeps(
         place, water_depth, bed_height, roughness, got, from_low, from_high, tile,
         back_low, back_high, returned, head,
     )
-    new_pressure = top(returned, match, (first[1], second[1]), head)
+    new_pressure = top(returned, match, (first, second), head)
     return new_pressure, new_depth
 
 

time: 98.5 us -> 99.8 us (1.013)
  blocking collectives: 0 us -> 13.1 us
  Pallas kernels: 57.8 us -> 49 us
  starting transfers between devices: 28.6 us -> 21.6 us
  waiting for transfers between devices: 0.08 us -> 5.08 us
    all_to_all x0 -> x1, blocking collectives: none -> 13.1 us  [per_device(): returned = lax.all_to_all(reply, 'gy', 0, 0)]
    pallas_call x4 -> x2, Pallas kernels: 33.5 us -> 24.6 us  [cells(): pl.pallas_call(kernel_in, grid=(inner + 3,), in_specs=[SMEM, SMEM, pl.Blo...]
    all_to_all x1 -> x0, starting transfers between devices: 6.39 us -> none  [per_device(): returned = lax.all_to_all(reply, 'gy', 0, 0)]
    all_to_all x1, waiting for transfers between devices: 0.01 us -> 5.06 us  [per_device(): got = lax.all_to_all(send, 'gy', 0, 0)]
    all_to_all x1, starting transfers between devices: 5.97 us -> 4.28 us  [per_device(): got = lax.all_to_all(send, 'gy', 0, 0)]
    ppermute x6, starting transfers between devices: 16.3 us -> 17.3 us  [shifted(): return lax.ppermute(value, axis, pairs)]
    unnamed x20 -> x18, local copies, waits for them, and re-layouts: 4.47 us -> 3.79 us
  transfers between devices with their start and end apart: 8 -> 7, of which waited for: 1 -> 1; matrix products, arithmetic and copies ran while one was open for 4% -> 4% of each run, Pallas kernels for 43% -> 38%
where the time goes in v2:
time: 99.8 us; the launch traced here: 99.1 us
  Pallas kernels  49 us (49%)
  starting transfers between devices  21.6 us (22%)
  blocking collectives  13.1 us (13%)
  local copies, waits for them, and re-layouts  6.72 us (7%)
  waiting for transfers between devices  5.08 us (5%)
  other arithmetic  2.81 us (3%)
    pallas_call x2, Pallas kernels, cells(): pl.pallas_call(kernel_in, grid=(inner + 3,), in_specs=[SMEM, SMEM, pl.Blo...  24.6 us
    ppermute x6, starting transfers between devices, shifted(): return lax.ppermute(value, axis, pairs)  17.3 us
    all_to_all x1, blocking collectives, per_device(): returned = lax.all_to_all(reply, 'gy', 0, 0)  13.1 us
    pallas_call x1, Pallas kernels, route(): pl.pallas_call(route_kernel, grid=(width,), in_specs=[SMEM, pl.BlockSpec(...  6.68 us
    pallas_call x1, Pallas kernels, top(): pl.pallas_call(kernel, grid=(steps,), in_specs=[pl.BlockSpec(got.shape, l...  5.41 us
    all_to_all x1, waiting for transfers between devices, per_device(): got = lax.all_to_all(send, 'gy', 0, 0)  5.06 us
    pallas_call x1, Pallas kernels, surface(): pl.pallas_call(surface_kernel, in_specs=[SMEM, SMEM, VMEM, VMEM, VMEM, VM...  4.94 us
    all_to_all x1, starting transfers between devices, per_device(): got = lax.all_to_all(send, 'gy', 0, 0)  4.28 us
  transfers between devices with their start and end apart: 7, of which 1 were waited for; matrix products, arithmetic and copies ran while one was open for 4% of the time, Pallas kernels for 38%

profile of v2, /device:TPU:1, one launch (start us, length us, event | category | flops | bytes accessed | tf_op | source)
XLA Modules:
  0.0 99.1 jit_solution(18145682231654145186)
XLA Ops:
  0.6 0.7 slice_convert_fusion
  1.3 1.3 %fusion = (f32[256,512]{1,0:T(8,128)S(1)}, f32[256,512]{1,0:T(8,128)S(1)}) fusion(f32[2048,512]{1,0:T(8,128)} %refs_3_.1), kind=kLoop, calls=%fused_computation.9 | loop fusion | bytes 2097152 | tf_op jit(solution)/shard_map/slice | solution.py:758
  2.6 0.0 copy-start.6
  2.6 0.0 copy-start.7
  2.7 4.6 %collective-permute-start.2 = (f32[264,512]{1,0:T(8,128)S(1)}, f32[264,512]{1,0:T(8,128)S(1)}, u32[]{:S(2)}, u32[]{:S(2)}) collective-permute-start(f32[264,512]{1,0:T(8,128)S(1)} %select_maximum_fusion.1), channel_id=1, source_target_pairs={{0,1},{1,2},{2,3},{3,4},{4,5},{5,6},{6,7},{7,8},{8,9},{9,10},{10,1... | collective-permute-start | bytes 1622024 | tf_op jit(solution)/shard_map/ppermute | solution.py:739
  7.3 0.7 stack.27.place_ref.refs_0_
  8.0 1.4 %pad_add_fusion.1.meta_ref.own_ref.refs_2_.refs_5_ = s32[3,2048]{1,0:T(4,128)} fusion(s32[1,2048]{1,0:T(1,128)} %bitcast.17, s32[1,2048]{1,0:T(1,128)} %bitcast.18, s32[1,2048]{1,0:T(1,128)} %bitcast.16), kind=kLoop, calls=%fused_computation.6 | loop fusion | flops 12288 | bytes 49152 | tf_op jit(solution)/shard_map/stack | solution.py:753
  9.3 6.7 %route.1 = (f32[8,88,128]{2,1,0:T(8,128)}, s32[1,2048]{1,0:T(1,128)}, f32[2,24,128]{2,1,0:T(8,128)}, bf16[1024,2048]{1,0:T(8,128)(2,1)}) custom-call(s32[8]{0:T(128)} %stack.27.place_ref.refs_0_, s32[3,2048]{1,0:T(4,128)} %pad_add_fusion.1.meta_ref.own_ref.refs_2_.refs_5_, f32[2048,512]{1,0:T(8,128)} %refs_3_.1, f32[128,256]{1,0:T(8,128)} %depth_ref.5, ...), custom_call_target="tpu_custom_call" | custom-call | tf_op jit(solution)/shard_map/route/pallas_call | solution.py:173
  16.0 4.3 %all-to-all-start = ((f32[8,88,128]{2,1,0:T(8,128)}), f32[8,88,128]{2,1,0:T(8,128)S(1)}, u32[]{:S(2)}, u32[]{:S(2)}) async-start(f32[8,88,128]{2,1,0:T(8,128)} %get-tuple-element.16), calls=%async_computation | async-start | bytes 720896 | tf_op jit(solution)/shard_map/all_to_all | solution.py:766
  20.3 1.9 %collective-permute-start.5 = (f32[264,512]{1,0:T(8,128)S(1)}, f32[264,512]{1,0:T(8,128)S(1)}, u32[]{:S(2)}, u32[]{:S(2)}) collective-permute-start(f32[264,512]{1,0:T(8,128)S(1)} %select_maximum_fusion), channel_id=1, source_target_pairs={{1,0},{2,1},{3,2},{4,3},{5,4},{6,5},{7,6},{8,7},{9,8},{10,9},{11,1... | collective-permute-start | bytes 1622024 | tf_op jit(solution)/shard_map/ppermute | solution.py:739
  22.3 0.0 copy-done.6
  22.3 0.0 copy-done.7
  22.3 0.7 pad_add_fusion.near_ref.refs_6_
  23.0 5.1 %all-to-all-done.got_ref = f32[8,88,128]{2,1,0:T(8,128)S(1)} async-done(((f32[8,88,128]{2,1,0:T(8,128)}), f32[8,88,128]{2,1,0:T(8,128)S(1)}, u32[]{:S(2)}, u32[]{:S(2)}) %all-to-all-start) | async-done | bytes 360480 | tf_op jit(solution)/shard_map/all_to_all | solution.py:766
  28.0 0.0 copy-start
  28.0 0.8 copy-done
  28.8 1.8 %forward.1 = (f32[376,128]{1,0:T(8,128)}, f32[376,128]{1,0:T(8,128)}) custom-call(s32[8]{0:T(128)} %stack.27.place_ref.refs_0_, f32[8,88,128]{2,1,0:T(8,128)} %copy-done, f32[2,24,128]{2,1,0:T(8,128)} %get-tuple-element.17.rows_ref, s32[1,2048]{1,0:T(1,128)} %get-tuple-element.18.after_ref), custom_call_target="tpu_custom_call" | custom-call | tf_op jit(solution)/shard_map/forward/pallas_call | solution.py:695
  30.6 6.0 %collective-permute-start.1 = (f32[376,128]{1,0:T(8,128)}, f32[376,128]{1,0:T(8,128)S(1)}, u32[]{:S(2)}, u32[]{:S(2)}) collective-permute-start(f32[376,128]{1,0:T(8,128)} %get-tuple-element.20), channel_id=1, source_target_pairs={{0,120},{8,0},{16,8},{24,16},{32,24},{40,32},{48,40},{56,48},{64,5... | collective-permute-start | bytes 577544 | tf_op jit(solution)/shard_map/ppermute | solution.py:739
  36.5 0.0 collective-permute-start
  36.5 0.0 collective-permute-done.2.edge_ref
  36.5 0.0 copy-start.8
  36.5 0.8 copy-done.8
  37.3 12.2 %cells.2 = (f32[2048,512]{1,0:T(8,128)}, f32[8,64,128]{2,1,0:T(8,128)}) custom-call(s32[8]{0:T(128)} %stack.27.place_ref.refs_0_, f32[5,12]{1,0:T(8,128)} %refs_1_.1, s32[3,2048]{1,0:T(4,128)} %pad_add_fusion.1.meta_ref.own_ref.refs_2_.refs_5_, f32[2048,512]{1,0:T(8,128)} %refs_3_.1, f32[264,512]{1,0:T(8,128)} %copy-done.8, ...), custom_call_target="tpu_custom_call" | custom-call | flops 2415919104 | bytes 8388608 | tf_op jit(solution)/shard_map/cells/pallas_call | solution.py:572
  49.5 0.0 collective-permute-done.1.down_ref
  49.5 0.0 copy-start.1
  49.5 0.0 collective-permute-done.up_ref
  49.6 0.0 copy-start.2
  49.6 0.6 copy-done.1
  50.2 0.1 copy-done.2
  50.3 4.9 %surface.1 = (f32[8,32,128]{2,1,0:T(8,128)}, f32[2,264,128]{2,1,0:T(8,128)}, f32[128,256]{1,0:T(8,128)}, f32[2,8,128]{2,1,0:T(8,128)}) custom-call(s32[8]{0:T(128)} %stack.27.place_ref.refs_0_, f32[5,12]{1,0:T(8,128)} %refs_1_.1, f32[8,88,128]{2,1,0:T(8,128)} %copy-done, f32[376,128]{1,0:T(8,128)} %copy-done.2, f32[376,128]{1,0:T(8,128)} %copy-done.1, ...), custom_call_target="tpu_custom_call" | custom-call | tf_op jit(solution)/shard_map/surface/pallas_call | solution.py:292
  55.2 1.0 slice_bitcast_fusion
  56.2 4.8 %collective-permute-start.4 = (f32[264,128]{1,0:T(8,128)S(1)}, f32[264,128]{1,0:T(8,128)S(1)}, u32[]{:S(2)}, u32[]{:S(2)}) collective-permute-start(f32[264,128]{1,0:T(8,128)S(1)} %get-tuple-element.32), channel_id=1, source_target_pairs={{0,120},{8,0},{16,8},{24,16},{32,24},{40,32},{48,40},{56,48},{64,5... | collective-permute-start | bytes 405512 | tf_op jit(solution)/shard_map/ppermute | solution.py:739
  61.1 0.0 collective-permute-start.3
  61.1 0.0 collective-permute-done.5.refs_4_
  61.1 0.0 copy-start.5
  61.1 0.8 copy-done.5
  61.9 12.4 %cells.3 = (f32[2048,512]{1,0:T(8,128)}, f32[8,64,128]{2,1,0:T(8,128)}) custom-call(s32[8]{0:T(128)} %stack.27.place_ref.refs_0_, f32[5,12]{1,0:T(8,128)} %refs_1_.1, s32[3,2048]{1,0:T(4,128)} %pad_add_fusion.1.meta_ref.own_ref.refs_2_.refs_5_, f32[2048,512]{1,0:T(8,128)} %refs_3_.1, f32[264,512]{1,0:T(8,128)} %copy-done.5, ...), custom_call_target="tpu_custom_call", output_to_operand_aliasing={{0}: (8, {})} | custom-call | flops 2415919104 | bytes 8388608 | tf_op jit(solution)/shard_map/cells/pallas_call | solution.py:572
  74.2 0.0 collective-permute-done.4.high_ref
  74.3 0.0 copy-start.3
  74.3 0.0 collective-permute-done.3.low_ref
  74.3 0.0 copy-start.4
  74.3 0.6 copy-done.3
  74.9 0.1 copy-done.4
  75.0 1.8 %backward.1 = f32[8,72,128]{2,1,0:T(8,128)} custom-call(s32[8]{0:T(128)} %stack.27.place_ref.refs_0_, f32[8,32,128]{2,1,0:T(8,128)} %get-tuple-element.22.refs_7_.stay_ref, f32[264,128]{1,0:T(8,128)} %copy-done.4, f32[264,128]{1,0:T(8,128)} %copy-done.3, f32[2,8,128]{2,1,0:T(8,128)} %get-tuple-element.24.cols_ref, ...), custom_call_target="tpu_custom_call" | custom-call | tf_op jit(solution)/shard_map/backward/pallas_call | solution.py:726
  76.8 13.1 %all_to_all.10.got_ref.back_ref = f32[8,72,128]{2,1,0:T(8,128)} all-to-all(f32[8,72,128]{2,1,0:T(8,128)} %backward.1), channel_id=1, replica_groups=mesh['gx'=16,'gy'=8] {'gy'}, dimensions={0} | all-to-all | bytes 589824 | tf_op jit(solution)/shard_map/all_to_all | solution.py:778
  89.8 3.8 %sweeps.1 = f32[128,256]{1,0:T(8,128)} custom-call(s32[8]{0:T(128)} %stack.27.place_ref.refs_0_, f32[128,256]{1,0:T(8,128)} %depth_ref.5, f32[128,256]{1,0:T(8,128)} %bed_ref.3, f32[128,256]{1,0:T(8,128)} %rough_ref.3, f32[8,88,128]{2,1,0:T(8,128)} %copy-done, f32[376,128]{1,0:T(8,128)} %copy-done.2, f32[376,128]{1,0:T(8,128)} %copy-done.1, ...), custom_call_target="tpu_custom_call" | custom-call | tf_op jit(solution)/shard_map/sweeps/pallas_call | solution.py:393
  93.6 5.4 %top.1 = f32[2048,512]{1,0:T(8,128)} custom-call(f32[8,72,128]{2,1,0:T(8,128)} %all_to_all.10.got_ref.back_ref, bf16[1024,2048]{1,0:T(8,128)(2,1)} %get-tuple-element.27.match_ref, f32[8,64,128]{2,1,0:T(8,128)} %get-tuple-element.21.after_ref.first_ref, f32[8,64,128]{2,1,0:T(8,128)} %get-tuple-element.26.after_ref.second_ref, ...), custom_call_target="tpu_custom_call", output_to_operand_aliasing={{}: (4, {})} | custom-call | tf_op jit(solution)/shard_map/top/pallas_call | solution.py:657
  (3 shorter events, 0.1 us)
Async XLA Ops:
  2.6 19.7 %copy-start.6 = (s32[2048,6]{0,1:T(8,128)S(1)}, s32[2048,6]{0,1:T(8,128)}, u32[]{:S(2)}) copy-start(s32[2048,6]{0,1:T(8,128)} %param.14) | copy-start | bytes 147460
  2.6 19.6 %copy-start.7 = (s32[2048,6]{0,1:T(8,128)S(1)}, s32[2048,6]{0,1:T(8,128)}, u32[]{:S(2)}) copy-start(s32[2048,6]{0,1:T(8,128)} %param.13) | copy-start | bytes 147460
  2.7 33.8 %collective-permute-start.2 = (f32[264,512]{1,0:T(8,128)S(1)}, f32[264,512]{1,0:T(8,128)S(1)}, u32[]{:S(2)}, u32[]{:S(2)}) collective-permute-start(f32[264,512]{1,0:T(8,128)S(1)} %select_maximum_fusion.1), channel_id=1, source_target_pairs={{0,1},{1,2},{2,3},{3,4},{4,5},{5,6},{6,7},{7,8},{8,9},{9,10},{10,1... | collective-permute-start | bytes 1622024 | tf_op jit(solution)/shard_map/ppermute | solution.py:739
  16.0 12.0 %all-to-all-start = ((f32[8,88,128]{2,1,0:T(8,128)}), f32[8,88,128]{2,1,0:T(8,128)S(1)}, u32[]{:S(2)}, u32[]{:S(2)}) async-start(f32[8,88,128]{2,1,0:T(8,128)} %get-tuple-element.16), calls=%async_computation | async-start | bytes 720896 | tf_op jit(solution)/shard_map/all_to_all | solution.py:766
  20.3 40.8 %collective-permute-start.5 = (f32[264,512]{1,0:T(8,128)S(1)}, f32[264,512]{1,0:T(8,128)S(1)}, u32[]{:S(2)}, u32[]{:S(2)}) collective-permute-start(f32[264,512]{1,0:T(8,128)S(1)} %select_maximum_fusion), channel_id=1, source_target_pairs={{1,0},{2,1},{3,2},{4,3},{5,4},{6,5},{7,6},{8,7},{9,8},{10,9},{11,1... | collective-permute-start | bytes 1622024 | tf_op jit(solution)/shard_map/ppermute | solution.py:739
  28.0 0.8 copy-start
  30.6 19.0 %collective-permute-start.1 = (f32[376,128]{1,0:T(8,128)}, f32[376,128]{1,0:T(8,128)S(1)}, u32[]{:S(2)}, u32[]{:S(2)}) collective-permute-start(f32[376,128]{1,0:T(8,128)} %get-tuple-element.20), channel_id=1, source_target_pairs={{0,120},{8,0},{16,8},{24,16},{32,24},{40,32},{48,40},{56,48},{64,5... | collective-permute-start | bytes 577544 | tf_op jit(solution)/shard_map/ppermute | solution.py:739
  36.5 13.0 %collective-permute-start = (f32[376,128]{1,0:T(8,128)}, f32[376,128]{1,0:T(8,128)S(1)}, u32[]{:S(2)}, u32[]{:S(2)}) collective-permute-start(f32[376,128]{1,0:T(8,128)} %get-tuple-element.19.after_ref), channel_id=1, source_target_pairs={{0,8},{8,16},{16,24},{24,32},{32,40},{40,48},{48,56},{56,64},{64,7... | collective-permute-start | bytes 577544 | tf_op jit(solution)/shard_map/ppermute | solution.py:739
  36.5 0.8 copy-start.8
  49.5 0.7 copy-start.1
  49.6 0.7 copy-start.2
  56.2 18.0 %collective-permute-start.4 = (f32[264,128]{1,0:T(8,128)S(1)}, f32[264,128]{1,0:T(8,128)S(1)}, u32[]{:S(2)}, u32[]{:S(2)}) collective-permute-start(f32[264,128]{1,0:T(8,128)S(1)} %get-tuple-element.32), channel_id=1, source_target_pairs={{0,120},{8,0},{16,8},{24,16},{32,24},{40,32},{48,40},{56,48},{64,5... | collective-permute-start | bytes 405512 | tf_op jit(solution)/shard_map/ppermute | solution.py:739
  61.1 13.2 %collective-permute-start.3 = (f32[264,128]{1,0:T(8,128)S(1)}, f32[264,128]{1,0:T(8,128)S(1)}, u32[]{:S(2)}, u32[]{:S(2)}) collective-permute-start(f32[264,128]{1,0:T(8,128)S(1)} %get-tuple-element.33), channel_id=1, source_target_pairs={{0,8},{8,16},{16,24},{24,32},{32,40},{40,48},{48,56},{56,64},{64,7... | collective-permute-start | bytes 405512 | tf_op jit(solution)/shard_map/ppermute | solution.py:739
  61.1 0.8 copy-start.5
  74.3 0.6 copy-start.3
  74.3 0.7 copy-start.4

commit v3 on v2

--- a/solution.py
+++ b/solution.py
@@ -13,6 +13,7 @@
 
 HB = 256
 TILE = 256
+PARTS = 4
 SLOTS = 64
 GROUPS = 16
 STORAGE = 0.05
@@ -26,6 +27,11 @@
 VMEM = pl.BlockSpec(memory_space=pltpu.VMEM)
 SMEM = pl.BlockSpec(memory_space=pltpu.SMEM)
 ANY = pl.BlockSpec(memory_space=pl.ANY)
+
+
+def position(width):
+    gx, gy = lax.axis_index("gx"), lax.axis_index("gy")
+    return gx * width + gy, gx, gy
 
 
 def split(value):
@@ -90,17 +96,17 @@
             table[row : row + 64, lanes] = value
 
 
-def route_kernel(place_ref, meta_ref, top_ref, depth_ref, bed_ref, rough_ref,
+def route_kernel(shape, class_ref, level_ref, patch_ref, top_ref, depth_ref, bed_ref, rough_ref,
                  send_ref, slot_ref, rows_ref, match_ref, turned, packed, edges):
     number = pl.program_id(0)
-    gy = place_ref[2]
+    own, _, gy = position(shape[1])
 
     @pl.when(number == 0)
     def _():
-        route_once(place_ref, meta_ref, top_ref, depth_ref, bed_ref, rough_ref,
+        route_once(own, gy, shape, class_ref, level_ref, patch_ref, top_ref, depth_ref, bed_ref, rough_ref,
                    slot_ref, rows_ref, turned, packed, edges)
 
-    blocks = meta_ref.shape[1]
+    blocks = patch_ref.shape[1]
     low_lane = iota((32, 128), 1) < 64
     wanted = as_bf16(iota((128, blocks), 0) + 128 * number == slot_ref[...])
     match_ref[...] = wanted
@@ -115,12 +121,11 @@
     send_ref[0, 72:88, :] = jnp.where(number == gy + 1, edges[1], edges[0])
 
 
-def route_once(place_ref, meta_ref, top_ref, depth_ref, bed_ref, rough_ref,
+def route_once(own, gy, shape, class_ref, level_ref, patch_ref, top_ref, depth_ref, bed_ref, rough_ref,
                slot_ref, rows_ref, turned, packed, edges):
-    own, gy = place_ref[0], place_ref[2]
-    devices, width = place_ref[3], place_ref[4]
-    blocks = meta_ref.shape[1]
-    patch = meta_ref[2:3, :]
+    devices, width = shape[0] * shape[1], shape[1]
+    blocks = patch_ref.shape[1]
+    patch = patch_ref[...]
     is_top = patch >= 0
     safe = jnp.where(is_top, patch, 0)
     offset = lax.rem(lax.shift_right_logical(safe, 9) - own + (GROUPS // 2 - 1) + devices, devices) - (GROUPS // 2 - 1)
@@ -155,8 +160,8 @@
     tags = jnp.where(row == 0, jnp.bitwise_and(place, 255), 0)
     tags = jnp.where(row == 1, lax.shift_right_logical(place, 8), tags)
     tags = jnp.where(row == 2, 1, tags)
-    tags = jnp.where(row == 3, meta_ref[0:1, :], tags)
-    tags = jnp.where(row == 4, meta_ref[1:2, :], tags)
+    tags = jnp.where(row == 3, class_ref[...], tags)
+    tags = jnp.where(row == 4, level_ref[...], tags)
     packed[128:144, :] = tags.astype(F32).astype(BF16)
     for number, field in enumerate((depth_ref, bed_ref, rough_ref)):
         edges[0, 3 * number : 3 * number + 3, :] = field[:, 0:128].T[0:3, :]
@@ -168,14 +173,17 @@
             rows_ref[1, at : at + 3, :] = field[125:128, lanes]
 
 
-def route(place, meta, pressure, water_depth, bed_height, roughness, width):
-    blocks = meta.shape[1]
+def route(shape, kinds, pressure, water_depth, bed_height, roughness):
+    blocks = pressure.shape[0]
+    width = shape[1]
+    row = pl.BlockSpec((1, blocks), lambda t: (0, 0))
     return pl.pallas_call(
-        route_kernel,
+        functools.partial(route_kernel, shape),
         grid=(width,),
         in_specs=[
-            SMEM,
-            pl.BlockSpec(meta.shape, lambda t: (0, 0)),
+            row,
+            row,
+            row,
             pl.BlockSpec((blocks, 128), lambda t: (0, 3)),
             pl.BlockSpec(water_depth.shape, lambda t: (0, 0)),
             pl.BlockSpec(water_depth.shape, lambda t: (0, 0)),
@@ -200,12 +208,12 @@
         ],
         compiler_params=pltpu.CompilerParams(vmem_limit_bytes=VMEM_LIMIT),
         name="route",
-    )(place, meta, pressure, water_depth, bed_height, roughness)
-
-
-def surface_kernel(place_ref, soil_ref, got_ref, up_ref, down_ref, depth_ref, after_ref,
-                   stay_ref, back_ref, tile_ref, cols_ref, packed, labels, match):
-    gy = place_ref[2]
+    )(*kinds, pressure, water_depth, bed_height, roughness)
+
+
+def surface_kernel(shape, soil_ref, got_ref, up_ref, down_ref, depth_ref, after_ref,
+                   stay_ref, back_high_ref, back_low_ref, tile_ref, cols_ref, packed, labels, match):
+    _, _, gy = position(shape[1])
     low_lane = iota((32, 128), 1) < 64
     tag_low = iota((8, 128), 1) < 64
     width = got_ref.shape[0]
@@ -268,8 +276,8 @@
         first, second = answer[0:32, lanes], answer[32:64, lanes]
         stay_ref[source] = jnp.where(low_lane, first, pltpu.roll(second, 64, 1))
         moved = jnp.where(low_lane, pltpu.roll(first, 64, 1), second)
-        back_ref[0, 32 * source : 32 * source + 32, :] = moved
-        back_ref[1, 32 * source : 32 * source + 32, :] = moved
+        back_high_ref[32 * source : 32 * source + 32, :] = moved
+        back_low_ref[32 * source : 32 * source + 32, :] = moved
     total = jnp.zeros(depth_ref.shape, F32)
     for i in range(8):
         pick = as_bf16(iota((patches, cols), 1) == 8 * jnp.bitwise_and(iota((patches, cols), 0), 31) + i)
@@ -281,21 +289,22 @@
     base = 32 * width
     for half in range(2):
         lanes = slice(128 * half, 128 * half + 128)
-        back_ref[0, base + 2 * half : base + 2 * half + 2, :] = total[0:2, lanes]
-        back_ref[1, base + 2 * half : base + 2 * half + 2, :] = total[126:128, lanes]
+        back_high_ref[base + 2 * half : base + 2 * half + 2, :] = total[0:2, lanes]
+        back_low_ref[base + 2 * half : base + 2 * half + 2, :] = total[126:128, lanes]
     cols_ref[0, 0:2, :] = total[:, 0:128].T[0:2, :]
     cols_ref[1, 0:2, :] = total[:, 128:256].T[126:128, :]
 
 
-def surface(place, soil, got, up, down, water_depth, patches, after):
+def surface(shape, soil, got, up, down, water_depth, patches, after):
     width = got.shape[0]
     return pl.pallas_call(
-        surface_kernel,
-        in_specs=[SMEM, SMEM, VMEM, VMEM, VMEM, VMEM, ANY],
-        out_specs=[VMEM, VMEM, VMEM, VMEM],
+        functools.partial(surface_kernel, shape),
+        in_specs=[SMEM, VMEM, VMEM, VMEM, VMEM, ANY],
+        out_specs=[VMEM] * 5,
         out_shape=[
             jax.ShapeDtypeStruct((width, 32, 128), F32),
-            jax.ShapeDtypeStruct((2, 32 * width + 8, 128), F32),
+            jax.ShapeDtypeStruct((32 * width + 8, 128), F32),
+            jax.ShapeDtypeStruct((32 * width + 8, 128), F32),
             jax.ShapeDtypeStruct(water_depth.shape, F32),
             jax.ShapeDtypeStruct((2, 8, 128), F32),
         ],
@@ -306,15 +315,15 @@
         ],
         compiler_params=pltpu.CompilerParams(vmem_limit_bytes=VMEM_LIMIT),
         name="surface",
-    )(place, soil, got, up, down, water_depth, after)
-
-
-def sweep_kernel(place_ref, depth_ref, bed_ref, rough_ref, got_ref, up_ref, down_ref,
+    )(soil, got, up, down, water_depth, after)
+
+
+def sweep_kernel(place, depth_ref, bed_ref, rough_ref, got_ref, up_ref, down_ref,
                  source_ref, low_ref, high_ref, back_ref, after_ref,
                  out_ref, depth_ext, bed_ext, rough_ext, source_ext, turn):
-    gx, gy = place_ref[1], place_ref[2]
-    left_at, right_at = jnp.maximum(gy - 1, 0), jnp.minimum(gy + 1, place_ref[4] - 1)
-    rows_total, cols_total = place_ref[5], place_ref[6]
+    _, gx, gy = position(place[1])
+    left_at, right_at = jnp.maximum(gy - 1, 0), jnp.minimum(gy + 1, place[1] - 1)
+    rows_total, cols_total = depth_ref.shape[0] * place[0], depth_ref.shape[1] * place[1]
     shape = depth_ext.shape
     halo = 40 * got_ref.shape[0]
     edge = 32 * got_ref.shape[0]
@@ -391,14 +400,14 @@
 def sweeps(place, water_depth, *rest):
     shape = (144, 512)
     return pl.pallas_call(
-        sweep_kernel,
-        in_specs=[SMEM] + [VMEM] * 10 + [ANY],
+        functools.partial(sweep_kernel, place),
+        in_specs=[VMEM] * 10 + [ANY],
         out_specs=VMEM,
         out_shape=jax.ShapeDtypeStruct(water_depth.shape, F32),
         scratch_shapes=[pltpu.VMEM(shape, F32)] * 4 + [pltpu.VMEM((128, 128), F32)],
         compiler_params=pltpu.CompilerParams(vmem_limit_bytes=VMEM_LIMIT),
         name="sweeps",
-    )(place, water_depth, *rest)
+    )(water_depth, *rest)
 
 
 def halo_tile(soil_ref, classes, source, slot, table, turned, cond):
@@ -412,15 +421,15 @@
         write_faces(turned, cond, half, slot, table)
 
 
-def inner_tile(soil_ref, meta_ref, head_ref, slot, table, turned, cond, base_sc, factor_sc, top_ref):
+def inner_tile(soil_ref, class_ref, level_ref, head_ref, slot, table, turned, cond, base_sc, factor_sc, top_ref):
     open_i = iota((8, 8, 128), 1) < 7
     nothing = jnp.zeros((1, 8, 128), F32)
     for half in range(TILE // 128):
         lanes = slice(128 * half, 128 * half + 128)
         at = 2 * (slot - 1) + half
         turned[half] = head_ref[lanes, :].T
-        soil = soil_rows(soil_ref, meta_ref[0:1, lanes])
-        width = cell_width(meta_ref[1:2, lanes])
+        soil = soil_rows(soil_ref, class_ref[:, lanes])
+        width = cell_width(level_ref[:, lanes])
         half_over = 0.5 / width
         scaled = SUB_STEP / width
 
@@ -494,10 +503,13 @@
         out_ref[128 * part : 128 * part + 128, :] = base_sc[2 * (slot - 1) + part].T
 
 
-def cells_kernel(part, inner, place_ref, soil_ref, meta_ref, head_ref, edge_ref, own_ref, near_ref, after_ref,
-                 out_ref, top_ref, table, turned, cond, base_sc, factor_sc):
+def cells_kernel(part, inner, width, has_edge, chained, *refs):
+    soil_ref, class_ref, level_ref, head_ref, own_ref, near_ref, after_ref = refs[:7]
+    edge_ref = refs[7] if has_edge else None
+    out_ref, top_ref, table, turned, cond, base_sc, factor_sc = refs[7 + has_edge + chained :]
     step = pl.program_id(0)
     last = inner + 1
+    own, _, _ = position(width)
     blocks = inner * TILE
 
     def at_edge():
@@ -511,24 +523,23 @@
     def beside():
         halo_tile(
             soil_ref,
-            lambda lanes: meta_ref[0:1, lanes],
+            lambda lanes: class_ref[:, lanes],
             lambda lanes: head_ref[lanes, :],
             step, table, turned, cond,
         )
 
     def within():
         inner_tile(
-            soil_ref, meta_ref, head_ref, step, table, turned, cond, base_sc, factor_sc, top_ref
+            soil_ref, class_ref, level_ref, head_ref, step, table, turned, cond, base_sc, factor_sc, top_ref
         )
 
     def faces():
         slot = step - 2
-        first_row = (2 * place_ref[0] + part) * blocks + (slot - 2) * TILE
-        face_tile(
-            first_row, own_ref[1:2, :], near_ref, slot, table, base_sc, factor_sc, out_ref
-        )
-
-    first, final = (at_edge, beside) if part == 0 else (beside, at_edge)
+        first_row = (PARTS * own + part) * blocks + (slot - 2) * TILE
+        face_tile(first_row, own_ref[...], near_ref, slot, table, base_sc, factor_sc, out_ref)
+
+    first = at_edge if part == 0 else beside
+    final = at_edge if part == PARTS - 1 else beside
 
     @pl.when(step == 0)
     def _():
@@ -538,10 +549,11 @@
     def _():
         within()
 
-    @pl.when((step >= 3) & (step < last))
-    def _():
-        faces()
-        within()
+    if last > 3:
+        @pl.when((step >= 3) & (step < last))
+        def _():
+            faces()
+            within()
 
     @pl.when(step == last)
     def _():
@@ -553,32 +565,29 @@
         faces()
 
 
-def cells(place, soil, meta, near, pressure, edge, after, part, head):
-    inner = pressure.shape[0] // TILE // 2
-    tiles = 2 * inner
-    kernel = functools.partial(cells_kernel, part, inner)
-    kernel_in = kernel
+def cells(shape, soil, kinds, near, pressure, edge, after, part, head):
+    inner = pressure.shape[0] // TILE // PARTS
+    tiles = PARTS * inner
+    low = part * inner
+    extra = [value for value in (edge, head) if value is not None]
+    extra_specs = [] if edge is None else [pl.BlockSpec(edge.shape, lambda t: (0, 0))]
     aliases = {}
-    extra, extra_specs = [], []
     if head is not None:
-        def kernel_in(*refs):
-            kernel(*refs[:8], *refs[9:])
-
-        aliases = {8: 0}
-        extra, extra_specs = [head], [ANY]
-    low = part * inner
+        aliases = {7 + len(extra_specs): 0}
+        extra_specs = extra_specs + [ANY]
     seen = lambda t: jnp.clip(t + low - 1, max(low - 1, 0), min(low + inner, tiles - 1))
     done = lambda t: jnp.clip(t + low - 3, low, low + inner - 1)
     return pl.pallas_call(
-        kernel_in,
+        functools.partial(
+            cells_kernel, part, inner, shape[1], int(edge is not None), int(head is not None)
+        ),
         grid=(inner + 3,),
         in_specs=[
             SMEM,
-            SMEM,
-            pl.BlockSpec((meta.shape[0], TILE), lambda t: (0, seen(t))),
+            pl.BlockSpec((1, TILE), lambda t: (0, seen(t))),
+            pl.BlockSpec((1, TILE), lambda t: (0, seen(t))),
             pl.BlockSpec((TILE, 512), lambda t: (seen(t), 0)),
-            pl.BlockSpec(edge.shape, lambda t: (0, 0)),
-            pl.BlockSpec((meta.shape[0], TILE), lambda t: (0, done(t))),
+            pl.BlockSpec((1, TILE), lambda t: (0, done(t))),
             pl.BlockSpec((near.shape[0], TILE), lambda t: (0, done(t))),
             ANY,
         ]
@@ -606,7 +615,7 @@
             transcendentals=inner * TILE * 512 * 8,
         ),
         name="cells",
-    )(place, soil, meta, pressure, edge, meta, near, after, *extra)
+    )(soil, *kinds, pressure, kinds[1], near, after, *extra)
 
 
 def top_kernel(got_ref, match_ref, factor_ref, head_ref, out_ref, packed, turned):
@@ -641,18 +650,13 @@
     blocks = head.shape[0]
     part = 2 * TILE
     steps = blocks // part
-    half = steps // 2
-
-    def kernel(got_ref, match_ref, first_ref, second_ref, head_ref, out_ref, packed, turned):
-        step = pl.program_id(0)
-
-        @pl.when(step < half)
-        def _():
-            top_kernel(got_ref, match_ref, first_ref, head_ref, out_ref, packed, turned)
-
-        @pl.when(step >= half)
-        def _():
-            top_kernel(got_ref, match_ref, second_ref, head_ref, out_ref, packed, turned)
+
+    def kernel(got_ref, match_ref, *refs):
+        head_ref, out_ref, packed, turned = refs[steps:]
+        for number in range(steps):
+            @pl.when(pl.program_id(0) == number)
+            def _():
+                top_kernel(got_ref, match_ref, refs[number], head_ref, out_ref, packed, turned)
 
     return pl.pallas_call(
         kernel,
@@ -660,13 +664,12 @@
         in_specs=[
             pl.BlockSpec(got.shape, lambda t: (0, 0, 0)),
             pl.BlockSpec((match.shape[0], part), lambda t: (0, t)),
-            pl.BlockSpec((part // 128, 64, 128), lambda t: (jnp.minimum(t, half - 1), 0, 0)),
-            pl.BlockSpec((part // 128, 64, 128), lambda t: (jnp.maximum(t - half, 0), 0, 0)),
-            pl.BlockSpec((part, 128), lambda t: (t, 3)),
-        ],
+        ]
+        + [pl.BlockSpec(factors[0].shape, lambda t: (0, 0, 0))] * steps
+        + [pl.BlockSpec((part, 128), lambda t: (t, 3))],
         out_specs=pl.BlockSpec((part, 128), lambda t: (t, 3)),
         out_shape=jax.ShapeDtypeStruct(head.shape, F32),
-        input_output_aliases={4: 0},
+        input_output_aliases={2 + steps: 0},
         scratch_shapes=[
             pltpu.VMEM((128, got.shape[0] * 128), BF16),
             pltpu.VMEM((part // 128, 128, 128), F32),
@@ -674,63 +677,6 @@
         compiler_params=pltpu.CompilerParams(vmem_limit_bytes=VMEM_LIMIT),
         name="top",
     )(got, match, *factors, head)
-
-
-def forward_kernel(place_ref, got_ref, rows_ref, after_ref, up_ref, down_ref):
-    gy, width = place_ref[2], got_ref.shape[0]
-    west = jnp.maximum(gy - 1, 0)
-    east = jnp.minimum(gy + 1, width - 1)
-    base = 40 * width
-    for number, ref in ((1, up_ref), (0, down_ref)):
-        for source in range(width):
-            ref[40 * source : 40 * source + 40, :] = got_ref[source, 32:72, :]
-        ref[base : base + 24, :] = rows_ref[number]
-        ref[base + 24 : base + 40, :] = got_ref[west, 72:88, :]
-        ref[base + 40 : base + 56, :] = got_ref[east, 72:88, :]
-
-
-def forward(place, got, rows, after):
-    width = got.shape[0]
-    shape = jax.ShapeDtypeStruct((40 * width + 56, 128), F32)
-    return pl.pallas_call(
-        forward_kernel,
-        in_specs=[SMEM, VMEM, VMEM, ANY],
-        out_specs=[VMEM, VMEM],
-        out_shape=[shape, shape],
-        compiler_params=pltpu.CompilerParams(vmem_limit_bytes=VMEM_LIMIT),
-        name="forward",
-    )(place, got, rows, after)
-
-
-def backward_kernel(place_ref, stay_ref, low_ref, high_ref, cols_ref, after_ref, send_ref):
-    gy, width = place_ref[2], stay_ref.shape[0]
-    base = 32 * width
-    sides = []
-    for kind in range(2):
-        lines = slice(base + 2 * kind, base + 2 * kind + 2)
-        sides.append(
-            jnp.concatenate(
-                [cols_ref[kind, 0:2, :], low_ref[lines, :], high_ref[lines, :], jnp.zeros((2, 128), F32)],
-                axis=0,
-            )
-        )
-    for number in range(width):
-        rows = slice(32 * number, 32 * number + 32)
-        send_ref[number, 0:32, :] = stay_ref[number]
-        send_ref[number, 32:64, :] = jnp.where(number >= gy, high_ref[rows, :], low_ref[rows, :])
-        send_ref[number, 64:72, :] = jnp.where(number == gy + 1, sides[1], sides[0])
-
-
-def backward(place, stay, low, high, cols, after):
-    width = stay.shape[0]
-    return pl.pallas_call(
-        backward_kernel,
-        in_specs=[SMEM, VMEM, VMEM, VMEM, VMEM, ANY],
-        out_specs=VMEM,
-        out_shape=jax.ShapeDtypeStruct((width, 72, 128), F32),
-        compiler_params=pltpu.CompilerParams(vmem_limit_bytes=VMEM_LIMIT),
-        name="backward",
-    )(place, stay, low, high, cols, after)
 
 
 def shifted(value, axis, steps, wrap=True):
@@ -744,13 +690,11 @@
     blocks = pressure.shape[0]
     rows, cols = water_depth.shape
     patches = rows // 8 * (cols // 8)
-    along, width = lax.axis_size("gx"), lax.axis_size("gy")
-    gx, gy = lax.axis_index("gx"), lax.axis_index("gy")
-    place = jnp.stack(
-        [gx * width + gy, gx, gy]
-        + [jnp.int32(v) for v in (along * width, width, rows * along, cols * width, 0)]
-    ).astype(I32)
-    meta = jnp.stack([soil_class, levels, patch_of_block])
+    shape = (lax.axis_size("gx"), lax.axis_size("gy"))
+    width = shape[1]
+    gy = lax.axis_index("gy")
+    kinds = [value.reshape(1, blocks) for value in (soil_class, levels)]
+    patch = patch_of_block.reshape(1, blocks)
     near = jnp.concatenate([neighbors.T, neighbor_levels.T], axis=0)
 
     def edge(part):
@@ -761,26 +705,50 @@
     high_edge = shifted(edge(slice(0, HB)), ("gx", "gy"), -1, wrap=False)
 
     send, slot, edge_rows, match = route(
-        place, meta, pressure, water_depth, bed_height, roughness, width
+        shape, kinds + [patch], pressure, water_depth, bed_height, roughness
     )
     got = lax.all_to_all(send, "gy", 0, 0)
-    up, down = forward(place, got, edge_rows, slot)
+    head, top_1 = cells(shape, soil_params, kinds, near, pressure, None, slot, 1, None)
+    got, top_1 = lax.optimization_barrier((got, top_1))
+    halos = got[:, 72:88]
+    west = lax.dynamic_index_in_dim(halos, jnp.maximum(gy - 1, 0), 0, keepdims=False)
+    east = lax.dynamic_index_in_dim(halos, jnp.minimum(gy + 1, width - 1), 0, keepdims=False)
+    moving = got[:, 32:72].reshape(40 * width, 128)
+    up = jnp.concatenate([moving, edge_rows[1], west, east], axis=0)
+    down = jnp.concatenate([moving, edge_rows[0], west, east], axis=0)
     from_low = shifted(up, "gx", 1)
     from_high = shifted(down, "gx", -1)
-    head, first = cells(place, soil_params, meta, near, pressure, low_edge, up, 0, None)
-    stay, back, tile, edge_cols = surface(
-        place, soil_params, got, from_low, from_high, water_depth, patches, first
+    head, top_2 = cells(shape, soil_params, kinds, near, pressure, None, up, 2, head)
+    stay, back_high, back_low, tile, edge_cols = surface(
+        shape, soil_params, got, from_low, from_high, water_depth, patches, top_2
     )
-    back_high = shifted(back[0], "gx", -1)
-    back_low = shifted(back[1], "gx", 1)
-    head, second = cells(place, soil_params, meta, near, pressure, high_edge, stay, 1, head)
-    reply = backward(place, stay, back_low, back_high, edge_cols, second)
+    back_high = shifted(back_high, "gx", -1)
+    back_low = shifted(back_low, "gx", 1)
+    head, top_0 = cells(shape, soil_params, kinds, near, pressure, low_edge, stay, 0, head)
+    back_low, back_high, top_0 = lax.optimization_barrier((back_low, back_high, top_0))
+    number = jnp.arange(width, dtype=I32)[:, None, None]
+    answers = 32 * width
+    moved = jnp.where(
+        number >= gy,
+        back_high[:answers].reshape(width, 32, 128),
+        back_low[:answers].reshape(width, 32, 128),
+    )
+
+    def side(kind):
+        lines = slice(answers + 2 * kind, answers + 2 * kind + 2)
+        return jnp.concatenate(
+            [edge_cols[kind, 0:2], back_low[lines], back_high[lines], jnp.zeros((2, 128), F32)], axis=0
+        )
+
+    sides = jnp.where(number == gy + 1, side(1)[None], side(0)[None])
+    reply = jnp.concatenate([stay, moved, sides], axis=1)
     returned = lax.all_to_all(reply, "gy", 0, 0)
+    head, top_3 = cells(shape, soil_params, kinds, near, pressure, high_edge, reply, 3, head)
     new_depth = sweeps(
-        place, water_depth, bed_height, roughness, got, from_low, from_high, tile,
+        shape, water_depth, bed_height, roughness, got, from_low, from_high, tile,
         back_low, back_high, returned, head,
     )
-    new_pressure = top(returned, match, (first, second), head)
+    new_pressure = top(returned, match, (top_0, top_1, top_2, top_3), head)
     return new_pressure, new_depth
 
 

time: 99.8 us -> 91.2 us (0.914)
  blocking collectives: 13.1 us -> 0 us
  starting transfers between devices: 21.6 us -> 28.9 us
  waiting for transfers between devices: 5.08 us -> 0.02 us
  Pallas kernels: 49 us -> 53 us
  local copies, waits for them, and re-layouts: 6.72 us -> 5.19 us
    all_to_all x1 -> x0, blocking collectives: 13.1 us -> none  [per_device(): returned = lax.all_to_all(reply, 'gy', 0, 0)]
    all_to_all x0 -> x1, starting transfers between devices: none -> 6.4 us  [per_device(): returned = lax.all_to_all(reply, 'gy', 0, 0)]
    all_to_all x1, waiting for transfers between devices: 5.06 us -> 0.01 us  [per_device(): got = lax.all_to_all(send, 'gy', 0, 0)]
    pallas_call x7, Pallas kernels: 43.6 us -> 47.8 us  [the longest x4 32.5 us: cells(): pl.pallas_call(functools.partial(cells_kernel, part, inner, shape[1], int...]
    all_to_all x1, starting transfers between devices: 4.28 us -> 5.97 us  [per_device(): got = lax.all_to_all(send, 'gy', 0, 0)]
    another operation x1 -> x0, other arithmetic: 1.35 us -> none  [per_device(): meta = jnp.stack([soil_class, levels, patch_of_block])]
    unnamed x18 -> x26, local copies, waits for them, and re-layouts: 3.79 us -> 3.1 us
  transfers between devices with their start and end apart: 7 -> 8, of which waited for: 1 -> 0; matrix products, arithmetic and copies ran while one was open for 4% -> 5% of each run, Pallas kernels for 38% -> 41%
where the time goes in v3:
time: 91.2 us; the launch traced here: 90.5 us
  Pallas kernels  53 us (58%)
  starting transfers between devices  28.9 us (32%)
  local copies, waits for them, and re-layouts  5.19 us (6%)
  other arithmetic  2.48 us (3%)
  between operations  0.93 us (1%)
    pallas_call x4, Pallas kernels, cells(): pl.pallas_call(functools.partial(cells_kernel, part, inner, shape[1], int...  32.5 us
    ppermute x6, starting transfers between devices, shifted(): return lax.ppermute(value, axis, pairs)  16.5 us
    pallas_call x1, Pallas kernels, route(): pl.pallas_call(functools.partial(route_kernel, shape), grid=(width,), in_...  6.57 us
    all_to_all x1, starting transfers between devices, per_device(): returned = lax.all_to_all(reply, 'gy', 0, 0)  6.4 us
    all_to_all x1, starting transfers between devices, per_device(): got = lax.all_to_all(send, 'gy', 0, 0)  5.97 us
    pallas_call x1, Pallas kernels, top(): pl.pallas_call(kernel, grid=(steps,), in_specs=[pl.BlockSpec(got.shape, l...  5.27 us
    pallas_call x1, Pallas kernels, surface(): pl.pallas_call(functools.partial(surface_kernel, shape), in_specs=[SMEM,...  4.88 us
    pallas_call x1, Pallas kernels, sweeps(): pl.pallas_call(functools.partial(sweep_kernel, place), in_specs=[VMEM] *...  3.81 us
  transfers between devices with their start and end apart: 8, of which 0 were waited for; matrix products, arithmetic and copies ran while one was open for 5% of the time, Pallas kernels for 41%

profile of v3, /device:TPU:1, one launch (start us, length us, event | category | flops | bytes accessed | tf_op | source)
XLA Modules:
  0.0 90.5 jit_solution(1217101215905890511)
XLA Ops:
  0.6 0.0 copy-start.10
  0.6 0.0 copy-start.11
  0.7 6.6 %route.1 = (f32[8,88,128]{2,1,0:T(8,128)}, s32[1,2048]{1,0:T(1,128)}, f32[2,24,128]{2,1,0:T(8,128)}, bf16[1024,2048]{1,0:T(8,128)(2,1)}) custom-call(s32[1,2048]{1,0:T(1,128)} %bitcast.34, s32[1,2048]{1,0:T(1,128)} %bitcast.25, s32[1,2048]{1,0:T(1,128)} %bitcast.41, f32[2048,512]{1,0:T(8,128)} %refs_3_.7, f32[128,256]{1,0:T(8,128)} %depth_ref.5, ...), custom_call_target="tpu_custom_call" | custom-call | tf_op jit(solution)/shard_map/route/pallas_call | solution.py:180
  7.2 6.0 %all-to-all-start = ((f32[8,88,128]{2,1,0:T(8,128)}), f32[8,88,128]{2,1,0:T(8,128)S(1)}, u32[]{:S(2)}, u32[]{:S(2)}) async-start(f32[8,88,128]{2,1,0:T(8,128)} %get-tuple-element.24), calls=%async_computation | async-start | bytes 720896 | tf_op jit(solution)/shard_map/all_to_all | solution.py:710
  13.2 1.3 %fusion = (f32[256,512]{1,0:T(8,128)S(1)}, f32[256,512]{1,0:T(8,128)S(1)}) fusion(f32[2048,512]{1,0:T(8,128)} %refs_3_.7), kind=kLoop, calls=%fused_computation.25 | loop fusion | bytes 2097152 | tf_op jit(solution)/shard_map/slice | solution.py:702
  14.5 0.7 slice_convert_fusion
  15.2 3.5 %collective-permute-start.4 = (f32[264,512]{1,0:T(8,128)S(1)}, f32[264,512]{1,0:T(8,128)S(1)}, u32[]{:S(2)}, u32[]{:S(2)}) collective-permute-start(f32[264,512]{1,0:T(8,128)S(1)} %select_maximum_fusion.1), channel_id=1, source_target_pairs={{0,1},{1,2},{2,3},{3,4},{4,5},{5,6},{6,7},{7,8},{8,9},{9,10},{10,1... | collective-permute-start | bytes 1622024 | tf_op jit(solution)/shard_map/ppermute | solution.py:685
  18.8 1.9 %collective-permute-start.5 = (f32[264,512]{1,0:T(8,128)S(1)}, f32[264,512]{1,0:T(8,128)S(1)}, u32[]{:S(2)}, u32[]{:S(2)}) collective-permute-start(f32[264,512]{1,0:T(8,128)S(1)} %select_maximum_fusion), channel_id=1, source_target_pairs={{1,0},{2,1},{3,2},{4,3},{5,4},{6,5},{7,6},{8,7},{9,8},{10,9},{11,1... | collective-permute-start | bytes 1622024 | tf_op jit(solution)/shard_map/ppermute | solution.py:685
  20.8 0.0 copy-done.10
  20.8 0.0 copy-done.11
  20.8 0.7 pad_add_fusion.refs_5_
  21.5 0.1 pad.21.clone
  21.5 8.0 %cells.4 = (f32[2048,512]{1,0:T(8,128)}, f32[4,64,128]{2,1,0:T(8,128)}) custom-call(f32[5,12]{1,0:T(8,128)} %refs_0_.7, s32[1,2048]{1,0:T(1,128)} %bitcast.35, s32[1,2048]{1,0:T(1,128)} %bitcast.26, f32[2048,512]{1,0:T(8,128)} %refs_3_.7, s32[1,2048]{1,0:T(1,128)} %bitcast.27, s32[12,2048]{1,0:T(8,128)} %pad_add_fusion.refs_5_, ...), custom_call_target="tpu_custom_call" | custom-call | flops 1207959552 | bytes 4194304 | tf_op jit(solution)/shard_map/cells/pallas_call | solution.py:580
  29.5 0.0 copy-done.12
  29.6 0.0 all-to-all-done.got_ref
  29.6 0.0 copy-start
  29.7 0.0 copy-start.2
  29.7 1.3 %collective-permute-start = (f32[376,128]{1,0:T(8,128)S(1)}, f32[376,128]{1,0:T(8,128)S(1)}, u32[]{:S(2)}, u32[]{:S(2)}) collective-permute-start(f32[376,128]{1,0:T(8,128)S(1)} %get-tuple-element.49.refs_6_), channel_id=1, source_target_pairs={{0,8},{8,16},{16,24},{24,32},{32,40},{40,48},{48,56},{56,64},{64,7... | collective-permute-start | bytes 577544 | tf_op jit(solution)/shard_map/ppermute | solution.py:685
  31.0 5.0 %collective-permute-start.1 = (f32[376,128]{1,0:T(8,128)S(1)}, f32[376,128]{1,0:T(8,128)S(1)}, u32[]{:S(2)}, u32[]{:S(2)}) collective-permute-start(f32[376,128]{1,0:T(8,128)S(1)} %get-tuple-element.48), channel_id=1, source_target_pairs={{0,120},{8,0},{16,8},{24,16},{32,24},{40,32},{48,40},{56,48},{64,5... | collective-permute-start | bytes 577544 | tf_op jit(solution)/shard_map/ppermute | solution.py:685
  36.0 0.0 copy-done.2
  36.0 8.0 %cells.5 = (f32[2048,512]{1,0:T(8,128)}, f32[4,64,128]{2,1,0:T(8,128)}) custom-call(f32[5,12]{1,0:T(8,128)} %refs_0_.7, s32[1,2048]{1,0:T(1,128)} %bitcast.36, s32[1,2048]{1,0:T(1,128)} %bitcast.28, f32[2048,512]{1,0:T(8,128)} %refs_3_.7, s32[1,2048]{1,0:T(1,128)} %bitcast.29, s32[12,2048]{1,0:T(8,128)} %pad_add_fusion.refs_5_, ...), custom_call_target="tpu_custom_call", output_to_operand_aliasing={{0}: (7, {})} | custom-call | flops 1207959552 | bytes 4194304 | tf_op jit(solution)/shard_map/cells/pallas_call | solution.py:580
  44.0 0.0 copy-done
  44.0 0.0 collective-permute-done.up_ref
  44.0 0.0 collective-permute-done.1.down_ref
  44.0 0.0 copy-start.4
  44.0 0.7 copy-done.3
  44.7 0.1 copy-done.4
  44.7 4.9 %surface.1 = (f32[8,32,128]{2,1,0:T(8,128)}, f32[264,128]{1,0:T(8,128)}, f32[264,128]{1,0:T(8,128)}, f32[128,256]{1,0:T(8,128)}, f32[2,8,128]{2,1,0:T(8,128)}) custom-call(f32[5,12]{1,0:T(8,128)} %refs_0_.7, f32[8,88,128]{2,1,0:T(8,128)} %copy-done, f32[376,128]{1,0:T(8,128)} %copy-done.3, f32[376,128]{1,0:T(8,128)} %copy-done.4, f32[128,256]{1,0:T(8,128)} %depth_ref.5, ...), custom_call_target="tpu_custom_call" | custom-call | tf_op jit(solution)/shard_map/surface/pallas_call | solution.py:300
  49.6 0.0 collective-permute-start.2
  49.6 4.8 %collective-permute-start.3 = (f32[264,128]{1,0:T(8,128)}, f32[264,128]{1,0:T(8,128)S(1)}, u32[]{:S(2)}, u32[]{:S(2)}) collective-permute-start(f32[264,128]{1,0:T(8,128)} %get-tuple-element.33), channel_id=1, source_target_pairs={{0,120},{8,0},{16,8},{24,16},{32,24},{40,32},{48,40},{56,48},{64,5... | collective-permute-start | bytes 405512 | tf_op jit(solution)/shard_map/ppermute | solution.py:685
  54.4 0.7 slice_bitcast_fusion.3
  55.1 0.0 collective-permute-done.4.refs_7_
  55.1 0.8 copy-done.6
  55.9 8.2 %cells.6 = (f32[2048,512]{1,0:T(8,128)}, f32[4,64,128]{2,1,0:T(8,128)}) custom-call(f32[5,12]{1,0:T(8,128)} %refs_0_.7, s32[1,2048]{1,0:T(1,128)} %bitcast.37, s32[1,2048]{1,0:T(1,128)} %bitcast.30, f32[2048,512]{1,0:T(8,128)} %refs_3_.7, s32[1,2048]{1,0:T(1,128)} %bitcast.31, s32[12,2048]{1,0:T(8,128)} %pad_add_fusion.refs_5_, ...), custom_call_target="tpu_custom_call", output_to_operand_aliasing={{0}: (8, {})} | custom-call | flops 1207959552 | bytes 4194304 | tf_op jit(solution)/shard_map/cells/pallas_call | solution.py:580
  64.1 0.0 collective-permute-done.2.low_ref
  64.2 0.0 collective-permute-done.3.high_ref
  64.2 0.1 maximum_maximum_fusion
  64.3 0.1 broadcast_select_fusion.1
  64.4 0.1 broadcast_select_fusion
  64.5 0.8 pad_maximum_fusion.refs_6_
  65.2 6.4 %all-to-all-start.1 = ((f32[8,72,128]{2,1,0:T(8,128)}), f32[8,72,128]{2,1,0:T(8,128)S(1)}, u32[]{:S(2)}, u32[]{:S(2)}) async-start(f32[8,72,128]{2,1,0:T(8,128)} %pad_maximum_fusion.refs_6_), calls=%async_computation.1 | async-start | bytes 589824 | tf_op jit(solution)/shard_map/all_to_all | solution.py:745
  71.6 0.0 collective-permute-done.5.refs_7_
  71.6 0.8 copy-done.5
  72.4 8.2 %cells.7 = (f32[2048,512]{1,0:T(8,128)}, f32[4,64,128]{2,1,0:T(8,128)}) custom-call(f32[5,12]{1,0:T(8,128)} %refs_0_.7, s32[1,2048]{1,0:T(1,128)} %bitcast.38, s32[1,2048]{1,0:T(1,128)} %bitcast.32, f32[2048,512]{1,0:T(8,128)} %refs_3_.7, s32[1,2048]{1,0:T(1,128)} %bitcast.33, s32[12,2048]{1,0:T(8,128)} %pad_add_fusion.refs_5_, ...), custom_call_target="tpu_custom_call", output_to_operand_aliasing={{0}: (8, {})} | custom-call | flops 1207959552 | bytes 4194304 | tf_op jit(solution)/shard_map/cells/pallas_call | solution.py:580
  80.7 0.0 all-to-all-done.1.got_ref.back_ref
  80.7 0.7 copy-done.1
  81.4 3.8 %sweeps.1 = f32[128,256]{1,0:T(8,128)} custom-call(f32[128,256]{1,0:T(8,128)} %depth_ref.5, f32[128,256]{1,0:T(8,128)} %bed_ref.3, f32[128,256]{1,0:T(8,128)} %rough_ref.3, f32[8,88,128]{2,1,0:T(8,128)} %copy-done, f32[376,128]{1,0:T(8,128)} %copy-done.3, f32[376,128]{1,0:T(8,128)} %copy-done.4, f32[128,256]{1,0:T(8,128)} %get-tuple-element.45.source_ref, ...), custom_call_target="tpu_custom_call" | custom-call | tf_op jit(solution)/shard_map/sweeps/pallas_call | solution.py:402
  85.3 5.3 %top.1 = f32[2048,512]{1,0:T(8,128)} custom-call(f32[8,72,128]{2,1,0:T(8,128)} %copy-done.1, bf16[1024,2048]{1,0:T(8,128)(2,1)} %get-tuple-element.39.match_ref, f32[4,64,128]{2,1,0:T(8,128)} %get-tuple-element.40.refs_0_, f32[4,64,128]{2,1,0:T(8,128)} %get-tuple-element.41.refs_1_, ...), custom_call_target="tpu_custom_call", output_to_operand_aliasing={{}: (6, {})} | custom-call | tf_op jit(solution)/shard_map/top/pallas_call | solution.py:661
  (24 shorter events, 0.2 us)
Async XLA Ops:
  0.6 20.1 %copy-start.10 = (s32[2048,6]{0,1:T(8,128)S(1)}, s32[2048,6]{0,1:T(8,128)}, u32[]{:S(2)}) copy-start(s32[2048,6]{0,1:T(8,128)} %param.14) | copy-start | bytes 147460
  0.6 20.1 %copy-start.11 = (s32[2048,6]{0,1:T(8,128)S(1)}, s32[2048,6]{0,1:T(8,128)}, u32[]{:S(2)}) copy-start(s32[2048,6]{0,1:T(8,128)} %param.13) | copy-start | bytes 147460
  7.2 22.3 %all-to-all-start = ((f32[8,88,128]{2,1,0:T(8,128)}), f32[8,88,128]{2,1,0:T(8,128)S(1)}, u32[]{:S(2)}, u32[]{:S(2)}) async-start(f32[8,88,128]{2,1,0:T(8,128)} %get-tuple-element.24), calls=%async_computation | async-start | bytes 720896 | tf_op jit(solution)/shard_map/all_to_all | solution.py:710
  13.2 16.3 %copy-start.12 = (f32[2,24,128]{2,1,0:T(8,128)S(1)}, f32[2,24,128]{2,1,0:T(8,128)}, u32[]{:S(2)}) copy-start(f32[2,24,128]{2,1,0:T(8,128)} %get-tuple-element.28) | copy-start | bytes 73732
  15.2 39.8 %collective-permute-start.4 = (f32[264,512]{1,0:T(8,128)S(1)}, f32[264,512]{1,0:T(8,128)S(1)}, u32[]{:S(2)}, u32[]{:S(2)}) collective-permute-start(f32[264,512]{1,0:T(8,128)S(1)} %select_maximum_fusion.1), channel_id=1, source_target_pairs={{0,1},{1,2},{2,3},{3,4},{4,5},{5,6},{6,7},{7,8},{8,9},{9,10},{10,1... | collective-permute-start | bytes 1622024 | tf_op jit(solution)/shard_map/ppermute | solution.py:685
  18.8 52.8 %collective-permute-start.5 = (f32[264,512]{1,0:T(8,128)S(1)}, f32[264,512]{1,0:T(8,128)S(1)}, u32[]{:S(2)}, u32[]{:S(2)}) collective-permute-start(f32[264,512]{1,0:T(8,128)S(1)} %select_maximum_fusion), channel_id=1, source_target_pairs={{1,0},{2,1},{3,2},{4,3},{5,4},{6,5},{7,6},{8,7},{9,8},{10,9},{11,1... | collective-permute-start | bytes 1622024 | tf_op jit(solution)/shard_map/ppermute | solution.py:685
  29.6 14.4 %copy-start = (f32[8,88,128]{2,1,0:T(8,128)}, f32[8,88,128]{2,1,0:T(8,128)S(1)}, u32[]{:S(2)}) copy-start(f32[8,88,128]{2,1,0:T(8,128)S(1)} %all-to-all-done.got_ref) | copy-start | bytes 1081348
  29.7 6.3 %copy-start.2 = (f32[376,128]{1,0:T(8,128)}, f32[376,128]{1,0:T(8,128)S(1)}, u32[]{:S(2)}) copy-start(f32[376,128]{1,0:T(8,128)S(1)} %get-tuple-element.49.refs_6_) | copy-start | bytes 577540
  29.7 14.3 %collective-permute-start = (f32[376,128]{1,0:T(8,128)S(1)}, f32[376,128]{1,0:T(8,128)S(1)}, u32[]{:S(2)}, u32[]{:S(2)}) collective-permute-start(f32[376,128]{1,0:T(8,128)S(1)} %get-tuple-element.49.refs_6_), channel_id=1, source_target_pairs={{0,8},{8,16},{16,24},{24,32},{32,40},{40,48},{48,56},{56,64},{64,7... | collective-permute-start | bytes 577544 | tf_op jit(solution)/shard_map/ppermute | solution.py:685
  31.0 13.0 %collective-permute-start.1 = (f32[376,128]{1,0:T(8,128)S(1)}, f32[376,128]{1,0:T(8,128)S(1)}, u32[]{:S(2)}, u32[]{:S(2)}) collective-permute-start(f32[376,128]{1,0:T(8,128)S(1)} %get-tuple-element.48), channel_id=1, source_target_pairs={{0,120},{8,0},{16,8},{24,16},{32,24},{40,32},{48,40},{56,48},{64,5... | collective-permute-start | bytes 577544 | tf_op jit(solution)/shard_map/ppermute | solution.py:685
  44.0 0.7 copy-start.3
  44.0 0.7 copy-start.4
  49.6 14.5 %collective-permute-start.2 = (f32[264,128]{1,0:T(8,128)}, f32[264,128]{1,0:T(8,128)S(1)}, u32[]{:S(2)}, u32[]{:S(2)}) collective-permute-start(f32[264,128]{1,0:T(8,128)} %get-tuple-element.32), channel_id=1, source_target_pairs={{0,8},{8,16},{16,24},{24,32},{32,40},{40,48},{48,56},{56,64},{64,7... | collective-permute-start | bytes 405512 | tf_op jit(solution)/shard_map/ppermute | solution.py:685
  49.6 14.5 %collective-permute-start.3 = (f32[264,128]{1,0:T(8,128)}, f32[264,128]{1,0:T(8,128)S(1)}, u32[]{:S(2)}, u32[]{:S(2)}) collective-permute-start(f32[264,128]{1,0:T(8,128)} %get-tuple-element.33), channel_id=1, source_target_pairs={{0,120},{8,0},{16,8},{24,16},{32,24},{40,32},{48,40},{56,48},{64,5... | collective-permute-start | bytes 405512 | tf_op jit(solution)/shard_map/ppermute | solution.py:685
  55.1 0.8 copy-start.6
  55.9 8.6 %copy-start.9 = (f32[8,32,128]{2,1,0:T(8,128)S(1)}, f32[8,32,128]{2,1,0:T(8,128)}, u32[]{:S(2)}) copy-start(f32[8,32,128]{2,1,0:T(8,128)} %get-tuple-element.31.refs_6_) | copy-start | bytes 393220
  64.1 16.5 %copy-start.7 = (f32[264,128]{1,0:T(8,128)}, f32[264,128]{1,0:T(8,128)S(1)}, u32[]{:S(2)}) copy-start(f32[264,128]{1,0:T(8,128)S(1)} %collective-permute-done.2.low_ref) | copy-start | bytes 405508
  64.2 16.5 %copy-start.8 = (f32[264,128]{1,0:T(8,128)}, f32[264,128]{1,0:T(8,128)S(1)}, u32[]{:S(2)}) copy-start(f32[264,128]{1,0:T(8,128)S(1)} %collective-permute-done.3.high_ref) | copy-start | bytes 405508
  65.2 15.5 %all-to-all-start.1 = ((f32[8,72,128]{2,1,0:T(8,128)}), f32[8,72,128]{2,1,0:T(8,128)S(1)}, u32[]{:S(2)}, u32[]{:S(2)}) async-start(f32[8,72,128]{2,1,0:T(8,128)} %pad_maximum_fusion.refs_6_), calls=%async_computation.1 | async-start | bytes 589824 | tf_op jit(solution)/shard_map/all_to_all | solution.py:745
  71.6 0.8 copy-start.5
  80.7 0.7 copy-start.1

commit v4 on v3

--- a/solution.py
+++ b/solution.py
@@ -13,7 +13,7 @@
 
 HB = 256
 TILE = 256
-PARTS = 4
+PARTS = ((0, 3), (3, 2), (5, 3))
 SLOTS = 64
 GROUPS = 16
 STORAGE = 0.05
@@ -97,28 +97,23 @@
 
 
 def route_kernel(shape, class_ref, level_ref, patch_ref, top_ref, depth_ref, bed_ref, rough_ref,
-                 send_ref, slot_ref, rows_ref, match_ref, turned, packed, edges):
-    number = pl.program_id(0)
+                 send_ref, slot_ref, rows_ref, turned, packed, edges):
     own, _, gy = position(shape[1])
-
-    @pl.when(number == 0)
-    def _():
-        route_once(own, gy, shape, class_ref, level_ref, patch_ref, top_ref, depth_ref, bed_ref, rough_ref,
-                   slot_ref, rows_ref, turned, packed, edges)
-
+    route_once(own, gy, shape, class_ref, level_ref, patch_ref, top_ref, depth_ref, bed_ref, rough_ref,
+               slot_ref, rows_ref, turned, packed, edges)
     blocks = patch_ref.shape[1]
     low_lane = iota((32, 128), 1) < 64
-    wanted = as_bf16(iota((128, blocks), 0) + 128 * number == slot_ref[...])
-    match_ref[...] = wanted
-    out = lax.dot_general(packed[...], wanted, (((1,), (1,)), ((), ())), preferred_element_type=F32)
-    first = out[0:32] + out[64:96]
-    second = out[32:64] + out[96:128]
-    send_ref[0, 0:32, :] = jnp.where(low_lane, first, pltpu.roll(second, 64, 1))
-    send_ref[0, 32:64, :] = jnp.where(low_lane, pltpu.roll(first, 64, 1), second)
-    label = out[130:131] * (out[128:129] + 256.0 * out[129:130] + 1.0) - 1.0
-    row = iota((8, 128), 0)
-    send_ref[0, 64:72, :] = jnp.where(row == 0, label, jnp.where(row == 1, out[131:132], out[132:133]))
-    send_ref[0, 72:88, :] = jnp.where(number == gy + 1, edges[1], edges[0])
+    for number in range(send_ref.shape[0]):
+        wanted = as_bf16(iota((128, blocks), 0) == slot_ref[...] - 128 * number)
+        out = lax.dot_general(packed[...], wanted, (((1,), (1,)), ((), ())), preferred_element_type=F32)
+        first = out[0:32] + out[64:96]
+        second = out[32:64] + out[96:128]
+        send_ref[number, 0:32, :] = jnp.where(low_lane, first, pltpu.roll(second, 64, 1))
+        send_ref[number, 32:64, :] = jnp.where(low_lane, pltpu.roll(first, 64, 1), second)
+        label = out[130:131] * (out[128:129] + 256.0 * out[129:130] + 1.0) - 1.0
+        row = iota((8, 128), 0)
+        send_ref[number, 64:72, :] = jnp.where(row == 0, label, jnp.where(row == 1, out[131:132], out[132:133]))
+        send_ref[number, 72:88, :] = jnp.where(number == gy + 1, edges[1], edges[0])
 
 
 def route_once(own, gy, shape, class_ref, level_ref, patch_ref, top_ref, depth_ref, bed_ref, rough_ref,
@@ -179,7 +174,7 @@
     row = pl.BlockSpec((1, blocks), lambda t: (0, 0))
     return pl.pallas_call(
         functools.partial(route_kernel, shape),
-        grid=(width,),
+        grid=(1,),
         in_specs=[
             row,
             row,
@@ -190,16 +185,14 @@
             pl.BlockSpec(water_depth.shape, lambda t: (0, 0)),
         ],
         out_specs=[
-            pl.BlockSpec((1, 88, 128), lambda t: (t, 0, 0)),
+            pl.BlockSpec((width, 88, 128), lambda t: (0, 0, 0)),
             pl.BlockSpec((1, blocks), lambda t: (0, 0)),
             pl.BlockSpec((2, 24, 128), lambda t: (0, 0, 0)),
-            pl.BlockSpec((128, blocks), lambda t: (t, 0)),
         ],
         out_shape=[
             jax.ShapeDtypeStruct((width, 88, 128), F32),
             jax.ShapeDtypeStruct((1, blocks), I32),
             jax.ShapeDtypeStruct((2, 24, 128), F32),
-            jax.ShapeDtypeStruct((128 * width, blocks), BF16),
         ],
         scratch_shapes=[
             pltpu.VMEM((blocks // 128, 128, 128), F32),
@@ -319,8 +312,12 @@
 
 
 def sweep_kernel(place, depth_ref, bed_ref, rough_ref, got_ref, up_ref, down_ref,
-                 source_ref, low_ref, high_ref, back_ref, after_ref,
-                 out_ref, depth_ext, bed_ext, rough_ext, source_ext, turn):
+                 source_ref, low_ref, high_ref, back_ref, slot_ref, factor_0, factor_1, factor_2, head_ref,
+                 out_ref, new_ref, depth_ext, bed_ext, rough_ext, source_ext, turn, slab, packed, turned, loaded, stored):
+    blocks = slab.shape[0]
+    top_lanes = pl.ds(384, 128)
+    load = pltpu.make_async_copy(head_ref.at[:, top_lanes], slab, loaded)
+    load.start()
     _, gx, gy = position(place[1])
     left_at, right_at = jnp.maximum(gy - 1, 0), jnp.minimum(gy + 1, place[1] - 1)
     rows_total, cols_total = depth_ref.shape[0] * place[0], depth_ref.shape[1] * place[1]
@@ -395,18 +392,64 @@
             net = net + flux - pltpu.roll(flux, 1, axis)
         head = head + SURF_STEP * net
     out_ref[...] = head[8:136, 128:384]
-
-
-def sweeps(place, water_depth, *rest):
+    low_lane = iota((32, 128), 1) < 64
+    slots = packed.shape[1]
+    for number in range(slots // 128):
+        lanes = slice(128 * number, 128 * number + 128)
+        stay, moved = back_ref[number, 0:32, :], back_ref[number, 32:64, :]
+        high, low = split(jnp.where(low_lane, stay, pltpu.roll(moved, 64, 1)))
+        packed[0:32, lanes] = high
+        packed[64:96, lanes] = low
+        high, low = split(jnp.where(low_lane, pltpu.roll(stay, 64, 1), moved))
+        packed[32:64, lanes] = high
+        packed[96:128, lanes] = low
+    load.wait()
+    factors = [(ref, at) for ref in (factor_0, factor_1, factor_2) for at in range(ref.shape[0])]
+    turned[:, 0:64, :] = jnp.zeros((TILE // 128, 64, 128), F32)
+    stores = []
+    for tile in range(blocks // TILE):
+        wanted = as_bf16(iota((slots, TILE), 0) == slot_ref[:, TILE * tile : TILE * tile + TILE])
+        flux = jnp.dot(packed[...], wanted, preferred_element_type=F32)
+        flux = flux[0:64] + flux[64:128]
+        for half in range(TILE // 128):
+            for i in range(8):
+                turned[half, pl.ds(64 + i, 8, stride=8), :] = flux[8 * i : 8 * i + 8, 128 * half : 128 * half + 128]
+            ref, at = factors[tile * (TILE // 128) + half]
+            turned[half, 64:128, :] = turned[half, 64:128, :] * ref[at]
+            rows = slice(TILE * tile + 128 * half, TILE * tile + 128 * half + 128)
+            slab[rows, :] = slab[rows, :] + turned[half].T
+        rows = pl.ds(TILE * tile, TILE)
+        store = pltpu.make_async_copy(slab.at[rows, :], new_ref.at[rows, top_lanes], stored.at[tile])
+        store.start()
+        stores.append(store)
+    for store in stores:
+        store.wait()
+
+
+def finish(place, water_depth, *rest):
     shape = (144, 512)
+    head = rest[-1]
+    blocks = head.shape[0]
     return pl.pallas_call(
         functools.partial(sweep_kernel, place),
-        in_specs=[VMEM] * 10 + [ANY],
-        out_specs=VMEM,
-        out_shape=jax.ShapeDtypeStruct(water_depth.shape, F32),
-        scratch_shapes=[pltpu.VMEM(shape, F32)] * 4 + [pltpu.VMEM((128, 128), F32)],
+        in_specs=[VMEM] * 14 + [ANY],
+        out_specs=[VMEM, ANY],
+        out_shape=[
+            jax.ShapeDtypeStruct(water_depth.shape, F32),
+            jax.ShapeDtypeStruct(head.shape, F32),
+        ],
+        input_output_aliases={14: 1},
+        scratch_shapes=[pltpu.VMEM(shape, F32)] * 4
+        + [
+            pltpu.VMEM((128, 128), F32),
+            pltpu.VMEM((blocks, 128), F32),
+            pltpu.VMEM((128, place[1] * 128), BF16),
+            pltpu.VMEM((TILE // 128, 128, 128), F32),
+            pltpu.SemaphoreType.DMA,
+            pltpu.SemaphoreType.DMA((blocks // TILE,)),
+        ],
         compiler_params=pltpu.CompilerParams(vmem_limit_bytes=VMEM_LIMIT),
-        name="sweeps",
+        name="finish",
     )(water_depth, *rest)
 
 
@@ -503,14 +546,13 @@
         out_ref[128 * part : 128 * part + 128, :] = base_sc[2 * (slot - 1) + part].T
 
 
-def cells_kernel(part, inner, width, has_edge, chained, *refs):
+def cells_kernel(low, inner, tiles, width, has_edge, chained, *refs):
     soil_ref, class_ref, level_ref, head_ref, own_ref, near_ref, after_ref = refs[:7]
     edge_ref = refs[7] if has_edge else None
     out_ref, top_ref, table, turned, cond, base_sc, factor_sc = refs[7 + has_edge + chained :]
     step = pl.program_id(0)
     last = inner + 1
     own, _, _ = position(width)
-    blocks = inner * TILE
 
     def at_edge():
         halo_tile(
@@ -535,11 +577,11 @@
 
     def faces():
         slot = step - 2
-        first_row = (PARTS * own + part) * blocks + (slot - 2) * TILE
+        first_row = own * tiles * TILE + (low + slot - 2) * TILE
         face_tile(first_row, own_ref[...], near_ref, slot, table, base_sc, factor_sc, out_ref)
 
-    first = at_edge if part == 0 else beside
-    final = at_edge if part == PARTS - 1 else beside
+    first = at_edge if low == 0 else beside
+    final = at_edge if low + inner == tiles else beside
 
     @pl.when(step == 0)
     def _():
@@ -566,9 +608,8 @@
 
 
 def cells(shape, soil, kinds, near, pressure, edge, after, part, head):
-    inner = pressure.shape[0] // TILE // PARTS
-    tiles = PARTS * inner
-    low = part * inner
+    tiles = pressure.shape[0] // TILE
+    low, inner = PARTS[part]
     extra = [value for value in (edge, head) if value is not None]
     extra_specs = [] if edge is None else [pl.BlockSpec(edge.shape, lambda t: (0, 0))]
     aliases = {}
@@ -579,7 +620,7 @@
     done = lambda t: jnp.clip(t + low - 3, low, low + inner - 1)
     return pl.pallas_call(
         functools.partial(
-            cells_kernel, part, inner, shape[1], int(edge is not None), int(head is not None)
+            cells_kernel, low, inner, tiles, shape[1], int(edge is not None), int(head is not None)
         ),
         grid=(inner + 3,),
         in_specs=[
@@ -618,67 +659,6 @@
     )(soil, *kinds, pressure, kinds[1], near, after, *extra)
 
 
-def top_kernel(got_ref, match_ref, factor_ref, head_ref, out_ref, packed, turned):
-    low_lane = iota((32, 128), 1) < 64
-    width = got_ref.shape[0]
-
-    @pl.when(pl.program_id(0) == 0)
-    def _():
-        for number in range(width):
-            lanes = slice(128 * number, 128 * number + 128)
-            stay, moved = got_ref[number, 0:32, :], got_ref[number, 32:64, :]
-            high, low = split(jnp.where(low_lane, stay, pltpu.roll(moved, 64, 1)))
-            packed[0:32, lanes] = high
-            packed[64:96, lanes] = low
-            high, low = split(jnp.where(low_lane, pltpu.roll(stay, 64, 1), moved))
-            packed[32:64, lanes] = high
-            packed[96:128, lanes] = low
-
-    blocks = match_ref.shape[1]
-    flux = jnp.dot(packed[...], match_ref[...], preferred_element_type=F32)
-    flux = flux[0:64] + flux[64:128]
-    for part in range(blocks // 128):
-        lanes = slice(128 * part, 128 * part + 128)
-        turned[part, 0:64, :] = jnp.zeros((64, 128), F32)
-        for i in range(8):
-            turned[part, pl.ds(64 + i, 8, stride=8), :] = flux[8 * i : 8 * i + 8, lanes]
-        turned[part, 64:128, :] = turned[part, 64:128, :] * factor_ref[part]
-        out_ref[lanes, :] = head_ref[lanes, :] + turned[part].T
-
-
-def top(got, match, factors, head):
-    blocks = head.shape[0]
-    part = 2 * TILE
-    steps = blocks // part
-
-    def kernel(got_ref, match_ref, *refs):
-        head_ref, out_ref, packed, turned = refs[steps:]
-        for number in range(steps):
-            @pl.when(pl.program_id(0) == number)
-            def _():
-                top_kernel(got_ref, match_ref, refs[number], head_ref, out_ref, packed, turned)
-
-    return pl.pallas_call(
-        kernel,
-        grid=(steps,),
-        in_specs=[
-            pl.BlockSpec(got.shape, lambda t: (0, 0, 0)),
-            pl.BlockSpec((match.shape[0], part), lambda t: (0, t)),
-        ]
-        + [pl.BlockSpec(factors[0].shape, lambda t: (0, 0, 0))] * steps
-        + [pl.BlockSpec((part, 128), lambda t: (t, 3))],
-        out_specs=pl.BlockSpec((part, 128), lambda t: (t, 3)),
-        out_shape=jax.ShapeDtypeStruct(head.shape, F32),
-        input_output_aliases={2 + steps: 0},
-        scratch_shapes=[
-            pltpu.VMEM((128, got.shape[0] * 128), BF16),
-            pltpu.VMEM((part // 128, 128, 128), F32),
-        ],
-        compiler_params=pltpu.CompilerParams(vmem_limit_bytes=VMEM_LIMIT),
-        name="top",
-    )(got, match, *factors, head)
-
-
 def shifted(value, axis, steps, wrap=True):
     count = lax.axis_size(axis)
     pairs = [(i, (i + steps) % count) for i in range(count) if wrap or 0 <= i + steps < count]
@@ -697,19 +677,18 @@
     patch = patch_of_block.reshape(1, blocks)
     near = jnp.concatenate([neighbors.T, neighbor_levels.T], axis=0)
 
+    send, slot, edge_rows = route(
+        shape, kinds + [patch], pressure, water_depth, bed_height, roughness
+    )
+    later, class_later, send = lax.optimization_barrier((pressure, soil_class, send))
+
     def edge(part):
-        classes = jnp.pad(soil_class[part].astype(F32)[None], ((0, 7), (0, 512 - HB)))
-        return jnp.concatenate([pressure[part], classes], axis=0)
+        classes = jnp.pad(class_later[part].astype(F32)[None], ((0, 7), (0, 512 - HB)))
+        return jnp.concatenate([later[part], classes], axis=0)
 
     low_edge = shifted(edge(slice(blocks - HB, blocks)), ("gx", "gy"), 1, wrap=False)
     high_edge = shifted(edge(slice(0, HB)), ("gx", "gy"), -1, wrap=False)
-
-    send, slot, edge_rows, match = route(
-        shape, kinds + [patch], pressure, water_depth, bed_height, roughness
-    )
     got = lax.all_to_all(send, "gy", 0, 0)
-    head, top_1 = cells(shape, soil_params, kinds, near, pressure, None, slot, 1, None)
-    got, top_1 = lax.optimization_barrier((got, top_1))
     halos = got[:, 72:88]
     west = lax.dynamic_index_in_dim(halos, jnp.maximum(gy - 1, 0), 0, keepdims=False)
     east = lax.dynamic_index_in_dim(halos, jnp.minimum(gy + 1, width - 1), 0, keepdims=False)
@@ -718,9 +697,9 @@
     down = jnp.concatenate([moving, edge_rows[0], west, east], axis=0)
     from_low = shifted(up, "gx", 1)
     from_high = shifted(down, "gx", -1)
-    head, top_2 = cells(shape, soil_params, kinds, near, pressure, None, up, 2, head)
+    head, top_1 = cells(shape, soil_params, kinds, near, pressure, None, up, 1, None)
     stay, back_high, back_low, tile, edge_cols = surface(
-        shape, soil_params, got, from_low, from_high, water_depth, patches, top_2
+        shape, soil_params, got, from_low, from_high, water_depth, patches, top_1
     )
     back_high = shifted(back_high, "gx", -1)
     back_low = shifted(back_low, "gx", 1)
@@ -743,12 +722,11 @@
     sides = jnp.where(number == gy + 1, side(1)[None], side(0)[None])
     reply = jnp.concatenate([stay, moved, sides], axis=1)
     returned = lax.all_to_all(reply, "gy", 0, 0)
-    head, top_3 = cells(shape, soil_params, kinds, near, pressure, high_edge, reply, 3, head)
-    new_depth = sweeps(
+    head, top_2 = cells(shape, soil_params, kinds, near, pressure, high_edge, reply, 2, head)
+    new_depth, new_pressure = finish(
         shape, water_depth, bed_height, roughness, got, from_low, from_high, tile,
-        back_low, back_high, returned, head,
+        back_low, back_high, returned, slot, top_0, top_1, top_2, head,
     )
-    new_pressure = top(returned, match, (top_0, top_1, top_2, top_3), head)
     return new_pressure, new_depth
 
 

time: 91.2 us -> 81 us (0.89)
  Pallas kernels: 53 us -> 42.8 us
    pallas_call x7 -> x5, Pallas kernels: 48.1 us -> 37.9 us  [the longest x3 28.3 us: cells(): pl.pallas_call(functools.partial(cells_kernel, low, inner, tiles, shape[1...]
  transfers between devices with their start and end apart: 8 -> 8, of which waited for: 0 -> 0; matrix products, arithmetic and copies ran while one was open for 5% -> 6% of each run, Pallas kernels for 41% -> 41%
where the time goes in v4:
time: 81 us; the launch traced here: 80.3 us
  Pallas kernels  42.8 us (53%)
  starting transfers between devices  28.8 us (36%)
  local copies, waits for them, and re-layouts  5.13 us (6%)
  other arithmetic  2.46 us (3%)
  between operations  1.08 us (1%)
    pallas_call x3, Pallas kernels, cells(): pl.pallas_call(functools.partial(cells_kernel, low, inner, tiles, shape[1...  28.3 us
    ppermute x6, starting transfers between devices, shifted(): return lax.ppermute(value, axis, pairs)  16.3 us
    all_to_all x1, starting transfers between devices, per_device(): returned = lax.all_to_all(reply, 'gy', 0, 0)  6.4 us
    all_to_all x1, starting transfers between devices, per_device(): got = lax.all_to_all(send, 'gy', 0, 0)  6.1 us
    pallas_call x1, Pallas kernels, finish(): pl.pallas_call(functools.partial(sweep_kernel, place), in_specs=[VMEM] *...  5.75 us
    pallas_call x1, Pallas kernels, surface(): pl.pallas_call(functools.partial(surface_kernel, shape), in_specs=[SMEM,...  4.85 us
    pallas_call x1, Pallas kernels, route(): pl.pallas_call(functools.partial(route_kernel, shape), grid=(1,), in_spec...  3.91 us
    unnamed x26, local copies, waits for them, and re-layouts  3.04 us
  transfers between devices with their start and end apart: 8, of which 0 were waited for; matrix products, arithmetic and copies ran while one was open for 6% of the time, Pallas kernels for 41%

profile of v4, /device:TPU:1, one launch (start us, length us, event | category | flops | bytes accessed | tf_op | source)
XLA Modules:
  0.0 80.3 jit_solution(3433563012675921934)
XLA Ops:
  0.6 0.0 copy-start.10
  0.6 0.0 copy-start.11
  0.7 3.9 %route.1 = (f32[8,88,128]{2,1,0:T(8,128)}, s32[1,2048]{1,0:T(1,128)}, f32[2,24,128]{2,1,0:T(8,128)}) custom-call(s32[1,2048]{1,0:T(1,128)} %bitcast.32, s32[1,2048]{1,0:T(1,128)} %bitcast.25, s32[1,2048]{1,0:T(1,128)} %bitcast.38, f32[2048,512]{1,0:T(8,128)} %refs_3_.5, f32[128,256]{1,0:T(8,128)} %depth_ref.5, f32[128,256]{1,0:T(8,128)} %bed_ref.3, ...), custom_call_target="tpu_custom_call" | custom-call | tf_op jit(solution)/shard_map/route/pallas_call | solution.py:175
  4.6 6.1 %all-to-all-start = ((f32[8,88,128]{2,1,0:T(8,128)}), f32[8,88,128]{2,1,0:T(8,128)S(1)}, u32[]{:S(2)}, u32[]{:S(2)}) async-start(f32[8,88,128]{2,1,0:T(8,128)} %get-tuple-element.25), calls=%async_computation | async-start | bytes 720896 | tf_op jit(solution)/shard_map/all_to_all | solution.py:691
  10.7 1.3 %fusion = (f32[256,512]{1,0:T(8,128)S(1)}, f32[256,512]{1,0:T(8,128)S(1)}) fusion(f32[2048,512]{1,0:T(8,128)} %refs_3_.5), kind=kLoop, calls=%fused_computation.25 | loop fusion | bytes 2097152 | tf_op jit(solution)/shard_map/slice | solution.py:687
  11.9 0.7 slice_convert_fusion
  12.7 3.5 %collective-permute-start.4 = (f32[264,512]{1,0:T(8,128)S(1)}, f32[264,512]{1,0:T(8,128)S(1)}, u32[]{:S(2)}, u32[]{:S(2)}) collective-permute-start(f32[264,512]{1,0:T(8,128)S(1)} %select_maximum_fusion.1), channel_id=1, source_target_pairs={{0,1},{1,2},{2,3},{3,4},{4,5},{5,6},{6,7},{7,8},{8,9},{9,10},{10,1... | collective-permute-start | bytes 1622024 | tf_op jit(solution)/shard_map/ppermute | solution.py:665
  16.3 1.9 %collective-permute-start.5 = (f32[264,512]{1,0:T(8,128)S(1)}, f32[264,512]{1,0:T(8,128)S(1)}, u32[]{:S(2)}, u32[]{:S(2)}) collective-permute-start(f32[264,512]{1,0:T(8,128)S(1)} %select_maximum_fusion), channel_id=1, source_target_pairs={{1,0},{2,1},{3,2},{4,3},{5,4},{6,5},{7,6},{8,7},{9,8},{10,9},{11,1... | collective-permute-start | bytes 1622024 | tf_op jit(solution)/shard_map/ppermute | solution.py:665
  18.2 0.0 copy-done.12
  18.3 0.1 pad.21.clone
  18.3 0.0 copy-done.10
  18.3 0.0 copy-done.11
  18.3 0.7 pad_add_fusion.refs_5_
  19.0 0.0 all-to-all-done.got_ref
  19.1 0.0 copy-start.4
  19.1 1.3 %collective-permute-start = (f32[376,128]{1,0:T(8,128)S(1)}, f32[376,128]{1,0:T(8,128)S(1)}, u32[]{:S(2)}, u32[]{:S(2)}) collective-permute-start(f32[376,128]{1,0:T(8,128)S(1)} %get-tuple-element.49.refs_6_), channel_id=1, source_target_pairs={{0,8},{8,16},{16,24},{24,32},{32,40},{40,48},{48,56},{56,64},{64,7... | collective-permute-start | bytes 577544 | tf_op jit(solution)/shard_map/ppermute | solution.py:665
  20.4 4.8 %collective-permute-start.1 = (f32[376,128]{1,0:T(8,128)S(1)}, f32[376,128]{1,0:T(8,128)S(1)}, u32[]{:S(2)}, u32[]{:S(2)}) collective-permute-start(f32[376,128]{1,0:T(8,128)S(1)} %get-tuple-element.48), channel_id=1, source_target_pairs={{0,120},{8,0},{16,8},{24,16},{32,24},{40,32},{48,40},{56,48},{64,5... | collective-permute-start | bytes 577544 | tf_op jit(solution)/shard_map/ppermute | solution.py:665
  25.2 0.0 copy-done.4
  25.2 8.0 %cells.3 = (f32[2048,512]{1,0:T(8,128)}, f32[4,64,128]{2,1,0:T(8,128)}) custom-call(f32[5,12]{1,0:T(8,128)} %refs_0_.5, s32[1,2048]{1,0:T(1,128)} %bitcast.33, s32[1,2048]{1,0:T(1,128)} %bitcast.26, f32[2048,512]{1,0:T(8,128)} %refs_3_.5, s32[1,2048]{1,0:T(1,128)} %bitcast.27, s32[12,2048]{1,0:T(8,128)} %pad_add_fusion.refs_5_, f32[376,128]{1,0:T(8,128)} %copy-done.4), custom_call_target="tpu_custom_call" | custom-call | flops 1207959552 | bytes 4194304 | tf_op jit(solution)/shard_map/cells/pallas_call | solution.py:621
  33.2 0.0 collective-permute-done.up_ref
  33.2 0.0 copy-start.2
  33.3 0.0 collective-permute-done.1.down_ref
  33.3 0.6 copy-done.2
  33.9 0.0 copy-done.3
  34.0 4.9 %surface.1 = (f32[8,32,128]{2,1,0:T(8,128)}, f32[264,128]{1,0:T(8,128)}, f32[264,128]{1,0:T(8,128)}, f32[128,256]{1,0:T(8,128)}, f32[2,8,128]{2,1,0:T(8,128)}) custom-call(f32[5,12]{1,0:T(8,128)} %refs_0_.5, f32[8,88,128]{2,1,0:T(8,128)} %copy-done, f32[376,128]{1,0:T(8,128)} %copy-done.2, f32[376,128]{1,0:T(8,128)} %copy-done.3, f32[128,256]{1,0:T(8,128)} %depth_ref.5, ...), custom_call_target="tpu_custom_call" | custom-call | tf_op jit(solution)/shard_map/surface/pallas_call | solution.py:293
  38.8 0.0 collective-permute-start.2
  38.8 4.8 %collective-permute-start.3 = (f32[264,128]{1,0:T(8,128)}, f32[264,128]{1,0:T(8,128)S(1)}, u32[]{:S(2)}, u32[]{:S(2)}) collective-permute-start(f32[264,128]{1,0:T(8,128)} %get-tuple-element.30), channel_id=1, source_target_pairs={{0,120},{8,0},{16,8},{24,16},{32,24},{40,32},{48,40},{56,48},{64,5... | collective-permute-start | bytes 405512 | tf_op jit(solution)/shard_map/ppermute | solution.py:665
  43.6 0.7 slice_bitcast_fusion.3
  44.3 0.0 collective-permute-done.4.refs_7_
  44.3 0.8 copy-done.6
  45.1 10.1 %cells.4 = (f32[2048,512]{1,0:T(8,128)}, f32[6,64,128]{2,1,0:T(8,128)}) custom-call(f32[5,12]{1,0:T(8,128)} %refs_0_.5, s32[1,2048]{1,0:T(1,128)} %bitcast.34, s32[1,2048]{1,0:T(1,128)} %bitcast.28, f32[2048,512]{1,0:T(8,128)} %refs_3_.5, s32[1,2048]{1,0:T(1,128)} %bitcast.29, s32[12,2048]{1,0:T(8,128)} %pad_add_fusion.refs_5_, ...), custom_call_target="tpu_custom_call", output_to_operand_aliasing={{0}: (8, {})} | custom-call | flops 1811939328 | bytes 6291456 | tf_op jit(solution)/shard_map/cells/pallas_call | solution.py:621
  55.2 0.0 collective-permute-done.2.low_ref
  55.3 0.0 collective-permute-done.3.high_ref
  55.3 0.0 copy-start.8
  55.3 0.1 maximum_maximum_fusion
  55.4 0.1 broadcast_select_fusion.1
  55.5 0.1 broadcast_select_fusion
  55.6 0.0 copy-done.9
  55.6 0.7 pad_maximum_fusion.refs_6_
  56.3 6.4 %all-to-all-start.1 = ((f32[8,72,128]{2,1,0:T(8,128)}), f32[8,72,128]{2,1,0:T(8,128)S(1)}, u32[]{:S(2)}, u32[]{:S(2)}) async-start(f32[8,72,128]{2,1,0:T(8,128)} %pad_maximum_fusion.refs_6_), calls=%async_computation.1 | async-start | bytes 589824 | tf_op jit(solution)/shard_map/all_to_all | solution.py:724
  62.7 0.0 collective-permute-done.5.refs_7_
  62.7 0.8 copy-done.5
  63.5 10.1 %cells.5 = (f32[2048,512]{1,0:T(8,128)}, f32[6,64,128]{2,1,0:T(8,128)}) custom-call(f32[5,12]{1,0:T(8,128)} %refs_0_.5, s32[1,2048]{1,0:T(1,128)} %bitcast.35, s32[1,2048]{1,0:T(1,128)} %bitcast.30, f32[2048,512]{1,0:T(8,128)} %refs_3_.5, s32[1,2048]{1,0:T(1,128)} %bitcast.31, s32[12,2048]{1,0:T(8,128)} %pad_add_fusion.refs_5_, ...), custom_call_target="tpu_custom_call", output_to_operand_aliasing={{0}: (8, {})} | custom-call | flops 1811939328 | bytes 6291456 | tf_op jit(solution)/shard_map/cells/pallas_call | solution.py:621
  73.6 0.0 copy-done.7
  73.6 0.0 copy-done.8
  73.6 0.0 all-to-all-done.1.back_ref
  73.7 0.7 copy-done.1
  74.4 5.8 %finish.1 = (f32[128,256]{1,0:T(8,128)}, f32[2048,512]{1,0:T(8,128)}) custom-call(f32[128,256]{1,0:T(8,128)} %depth_ref.5, f32[128,256]{1,0:T(8,128)} %bed_ref.3, f32[128,256]{1,0:T(8,128)} %rough_ref.3, f32[8,88,128]{2,1,0:T(8,128)} %copy-done, f32[376,128]{1,0:T(8,128)} %copy-done.2, f32[376,128]{1,0:T(8,128)} %copy-done.3, ...), custom_call_target="tpu_custom_call", output_to_operand_aliasing={{1}: (14, {})} | custom-call | tf_op jit(solution)/shard_map/finish/pallas_call | solution.py:433
  (22 shorter events, 0.2 us)
Async XLA Ops:
  0.6 17.7 %copy-start.10 = (s32[2048,6]{0,1:T(8,128)S(1)}, s32[2048,6]{0,1:T(8,128)}, u32[]{:S(2)}) copy-start(s32[2048,6]{0,1:T(8,128)} %param.14) | copy-start | bytes 147460
  0.6 17.7 %copy-start.11 = (s32[2048,6]{0,1:T(8,128)S(1)}, s32[2048,6]{0,1:T(8,128)}, u32[]{:S(2)}) copy-start(s32[2048,6]{0,1:T(8,128)} %param.13) | copy-start | bytes 147460
  4.6 13.7 %copy-start.12 = (f32[2,24,128]{2,1,0:T(8,128)S(1)}, f32[2,24,128]{2,1,0:T(8,128)}, u32[]{:S(2)}) copy-start(f32[2,24,128]{2,1,0:T(8,128)} %get-tuple-element.26) | copy-start | bytes 73732
  4.6 14.5 %all-to-all-start = ((f32[8,88,128]{2,1,0:T(8,128)}), f32[8,88,128]{2,1,0:T(8,128)S(1)}, u32[]{:S(2)}, u32[]{:S(2)}) async-start(f32[8,88,128]{2,1,0:T(8,128)} %get-tuple-element.25), calls=%async_computation | async-start | bytes 720896 | tf_op jit(solution)/shard_map/all_to_all | solution.py:691
  12.7 31.6 %collective-permute-start.4 = (f32[264,512]{1,0:T(8,128)S(1)}, f32[264,512]{1,0:T(8,128)S(1)}, u32[]{:S(2)}, u32[]{:S(2)}) collective-permute-start(f32[264,512]{1,0:T(8,128)S(1)} %select_maximum_fusion.1), channel_id=1, source_target_pairs={{0,1},{1,2},{2,3},{3,4},{4,5},{5,6},{6,7},{7,8},{8,9},{9,10},{10,1... | collective-permute-start | bytes 1622024 | tf_op jit(solution)/shard_map/ppermute | solution.py:665
  16.3 46.4 %collective-permute-start.5 = (f32[264,512]{1,0:T(8,128)S(1)}, f32[264,512]{1,0:T(8,128)S(1)}, u32[]{:S(2)}, u32[]{:S(2)}) collective-permute-start(f32[264,512]{1,0:T(8,128)S(1)} %select_maximum_fusion), channel_id=1, source_target_pairs={{1,0},{2,1},{3,2},{4,3},{5,4},{6,5},{7,6},{8,7},{9,8},{10,9},{11,1... | collective-permute-start | bytes 1622024 | tf_op jit(solution)/shard_map/ppermute | solution.py:665
  19.0 14.3 %copy-start = (f32[8,88,128]{2,1,0:T(8,128)}, f32[8,88,128]{2,1,0:T(8,128)S(1)}, u32[]{:S(2)}) copy-start(f32[8,88,128]{2,1,0:T(8,128)S(1)} %all-to-all-done.got_ref) | copy-start | bytes 1081348
  19.1 6.1 %copy-start.4 = (f32[376,128]{1,0:T(8,128)}, f32[376,128]{1,0:T(8,128)S(1)}, u32[]{:S(2)}) copy-start(f32[376,128]{1,0:T(8,128)S(1)} %get-tuple-element.49.refs_6_) | copy-start | bytes 577540
  19.1 14.1 %collective-permute-start = (f32[376,128]{1,0:T(8,128)S(1)}, f32[376,128]{1,0:T(8,128)S(1)}, u32[]{:S(2)}, u32[]{:S(2)}) collective-permute-start(f32[376,128]{1,0:T(8,128)S(1)} %get-tuple-element.49.refs_6_), channel_id=1, source_target_pairs={{0,8},{8,16},{16,24},{24,32},{32,40},{40,48},{48,56},{56,64},{64,7... | collective-permute-start | bytes 577544 | tf_op jit(solution)/shard_map/ppermute | solution.py:665
  20.4 12.9 %collective-permute-start.1 = (f32[376,128]{1,0:T(8,128)S(1)}, f32[376,128]{1,0:T(8,128)S(1)}, u32[]{:S(2)}, u32[]{:S(2)}) collective-permute-start(f32[376,128]{1,0:T(8,128)S(1)} %get-tuple-element.48), channel_id=1, source_target_pairs={{0,120},{8,0},{16,8},{24,16},{32,24},{40,32},{48,40},{56,48},{64,5... | collective-permute-start | bytes 577544 | tf_op jit(solution)/shard_map/ppermute | solution.py:665
  33.2 0.7 copy-start.2
  33.3 0.7 copy-start.3
  38.8 16.4 %collective-permute-start.2 = (f32[264,128]{1,0:T(8,128)}, f32[264,128]{1,0:T(8,128)S(1)}, u32[]{:S(2)}, u32[]{:S(2)}) collective-permute-start(f32[264,128]{1,0:T(8,128)} %get-tuple-element.29), channel_id=1, source_target_pairs={{0,8},{8,16},{16,24},{24,32},{32,40},{40,48},{48,56},{56,64},{64,7... | collective-permute-start | bytes 405512 | tf_op jit(solution)/shard_map/ppermute | solution.py:665
  38.8 16.4 %collective-permute-start.3 = (f32[264,128]{1,0:T(8,128)}, f32[264,128]{1,0:T(8,128)S(1)}, u32[]{:S(2)}, u32[]{:S(2)}) collective-permute-start(f32[264,128]{1,0:T(8,128)} %get-tuple-element.30), channel_id=1, source_target_pairs={{0,120},{8,0},{16,8},{24,16},{32,24},{40,32},{48,40},{56,48},{64,5... | collective-permute-start | bytes 405512 | tf_op jit(solution)/shard_map/ppermute | solution.py:665
  44.3 0.8 copy-start.6
  45.1 10.5 %copy-start.9 = (f32[8,32,128]{2,1,0:T(8,128)S(1)}, f32[8,32,128]{2,1,0:T(8,128)}, u32[]{:S(2)}) copy-start(f32[8,32,128]{2,1,0:T(8,128)} %get-tuple-element.31.refs_6_) | copy-start | bytes 393220
  55.3 18.4 %copy-start.7 = (f32[264,128]{1,0:T(8,128)}, f32[264,128]{1,0:T(8,128)S(1)}, u32[]{:S(2)}) copy-start(f32[264,128]{1,0:T(8,128)S(1)} %collective-permute-done.2.low_ref) | copy-start | bytes 405508
  55.3 18.4 %copy-start.8 = (f32[264,128]{1,0:T(8,128)}, f32[264,128]{1,0:T(8,128)S(1)}, u32[]{:S(2)}) copy-start(f32[264,128]{1,0:T(8,128)S(1)} %collective-permute-done.3.high_ref) | copy-start | bytes 405508
  56.3 17.3 %all-to-all-start.1 = ((f32[8,72,128]{2,1,0:T(8,128)}), f32[8,72,128]{2,1,0:T(8,128)S(1)}, u32[]{:S(2)}, u32[]{:S(2)}) async-start(f32[8,72,128]{2,1,0:T(8,128)} %pad_maximum_fusion.refs_6_), calls=%async_computation.1 | async-start | bytes 589824 | tf_op jit(solution)/shard_map/all_to_all | solution.py:724
  62.7 0.8 copy-start.5
  73.7 0.7 copy-start.1

commit v5 on v4

--- a/solution.py
+++ b/solution.py
@@ -10,6 +10,7 @@
 F32 = jnp.float32
 BF16 = jnp.bfloat16
 I32 = jnp.int32
+I16 = jnp.int16
 
 HB = 256
 TILE = 256
@@ -86,14 +87,11 @@
     return ref[half, start : start + 64, :]
 
 
-def write_faces(head_ref, cond_ref, half, slot, table):
-    lanes = pl.ds(pl.multiple_of(slot * TILE, TILE) + 128 * half, 128)
-    for face in range(6):
-        head_high, head_low = split(face_rows(head_ref, half, face))
-        cond_high, cond_low = split(face_rows(cond_ref, half, face))
-        for part, value in enumerate((head_high, head_low, cond_high, cond_low)):
-            row = 256 * face + 64 * part
-            table[row : row + 64, lanes] = value
+def write_face(head, conductivity, half, face, slot, table):
+    lanes = slice(slot * TILE + 128 * half, slot * TILE + 128 * half + 128)
+    for part, value in enumerate(split(head) + split(conductivity)):
+        row = 256 * face + 64 * part
+        table[row : row + 64, lanes] = value
 
 
 def route_kernel(shape, class_ref, level_ref, patch_ref, top_ref, depth_ref, bed_ref, rough_ref,
@@ -453,28 +451,40 @@
     )(water_depth, *rest)
 
 
-def halo_tile(soil_ref, classes, source, slot, table, turned, cond):
-    for half in range(TILE // 128):
+def halo_pieces(soil_ref, classes, source, slot, table, turned):
+    pieces = []
+
+    def turn(half):
         lanes = slice(128 * half, 128 * half + 128)
         turned[half] = source(lanes).T
         soil = soil_rows(soil_ref, classes(lanes))
-        for k in range(8):
-            rows = slice(64 * k, 64 * k + 64)
-            cond[half, rows, :] = curve(turned[half, rows, :], soil)[0]
-        write_faces(turned, cond, half, slot, table)
-
-
-def inner_tile(soil_ref, class_ref, level_ref, head_ref, slot, table, turned, cond, base_sc, factor_sc, top_ref):
+        for face in range(6):
+            late.append(functools.partial(part, half, face, soil))
+
+    def part(half, face, soil):
+        head = face_rows(turned, half, face)
+        write_face(head, curve(head, soil)[0], half, face, slot, table)
+
+    late = []
+    for half in range(TILE // 128):
+        turn(half)
+    return pieces, late
+
+
+def inner_pieces(soil_ref, classes, levels, source, slot, table, turned, cond, base_sc, factor_sc, top_ref):
     open_i = iota((8, 8, 128), 1) < 7
     nothing = jnp.zeros((1, 8, 128), F32)
-    for half in range(TILE // 128):
+    pieces, late = [], []
+
+    def one(half):
         lanes = slice(128 * half, 128 * half + 128)
         at = 2 * (slot - 1) + half
-        turned[half] = head_ref[lanes, :].T
-        soil = soil_rows(soil_ref, class_ref[:, lanes])
-        width = cell_width(level_ref[:, lanes])
+        turned[half] = source(lanes).T
+        soil = soil_rows(soil_ref, classes(lanes))
+        width = cell_width(levels(lanes))
         half_over = 0.5 / width
         scaled = SUB_STEP / width
+        state = {"below": None}
 
         def conduct(k):
             rows = slice(64 * k, 64 * k + 64)
@@ -483,13 +493,9 @@
             factor = scaled * base / (soil[4] * ratio + STORAGE * base)
             factor_sc[at, rows, :] = factor
             if k == 7:
-                top_ref[half] = factor
-
-        conduct(0)
-        below = None
-        for k in range(8):
-            if k < 7:
-                conduct(k + 1)
+                top_ref[at] = factor
+
+        def flow(k):
             rows = slice(64 * k, 64 * k + 64)
             head = turned[half, rows, :].reshape(8, 8, 128)
             cnd = cond[half, rows, :].reshape(8, 8, 128)
@@ -504,139 +510,182 @@
                 cnd_up = cond[half, above, :].reshape(8, 8, 128)
                 flux = (cnd + cnd_up) * ((head_up - head) * half_over + 0.5)
                 inflow = inflow + flux
-            if below is not None:
-                inflow = inflow - below
-            below = flux
+            if state["below"] is not None:
+                inflow = inflow - state["below"]
+            state["below"] = flux
             base_sc[at, rows, :] = (
                 turned[half, rows, :] + factor_sc[at, rows, :] * inflow.reshape(64, 128)
             )
-        write_faces(turned, cond, half, slot, table)
-
-
-def face_tile(first_row, levels, near_ref, slot, table, base_sc, factor_sc, out_ref):
+
+        pieces.append(functools.partial(conduct, 0))
+        for k in range(8):
+            if k < 7:
+                pieces.append(functools.partial(conduct, k + 1))
+            pieces.append(functools.partial(flow, k))
+        for face in range(6):
+            late.append(
+                lambda face=face: write_face(
+                    face_rows(turned, half, face), face_rows(cond, half, face), half, face, slot, table
+                )
+            )
+
+    for half in range(TILE // 128):
+        one(half)
+    return pieces, late
+
+
+def face_pieces(first_row, levels, near, slot, table, total, factor, out):
+    halves = TILE // 128
+    first = halves * (slot - 1)
     width = cell_width(levels)
-    window = pl.ds(pl.multiple_of((slot - 1) * TILE, TILE), 3 * TILE)
-    own = pl.ds(pl.multiple_of(slot * TILE, TILE), TILE)
-    for face in range(6):
-        neighbor = near_ref[face : face + 1, :]
-        far_width = cell_width(near_ref[6 + face : 7 + face, :])
+    window = slice((slot - 1) * TILE, (slot + 2) * TILE)
+    own = slice(slot * TILE, (slot + 1) * TILE)
+
+    def one(face):
+        neighbor = near(face)
+        far_width = cell_width(near(6 + face))
         over_gap = 2.0 / (width + far_width)
         half = jnp.where(neighbor >= 0, 0.5, 0.0)
-        chosen = as_bf16(iota((3 * TILE, TILE), 0) == neighbor - first_row)
+        row = jnp.where(neighbor >= 0, neighbor - first_row, -1)
+        chosen = jnp.where(
+            iota((3 * TILE, TILE), 0).astype(I16) == row.astype(I16), jnp.ones((), BF16), jnp.zeros((), BF16)
+        )
         there = 256 * OPPOSITE[face]
         far = jnp.dot(table[there : there + 256, window], chosen, preferred_element_type=F32)
-        near = table[256 * face : 256 * face + 256, own].astype(F32)
-        head_diff = (far[0:64] - near[0:64]) + (far[64:128] - near[64:128])
-        conds = (far[128:192] + near[128:192]) + (far[192:256] + near[192:256])
+        here = table[256 * face : 256 * face + 256, own].astype(F32)
+        head_diff = (far[0:64] - here[0:64]) + (far[64:128] - here[64:128])
+        conds = (far[128:192] + here[128:192]) + (far[192:256] + here[192:256])
         flux = conds * half * (head_diff * over_gap + GRAVITY[face])
-        for part in range(TILE // 128):
-            at = 2 * (slot - 1) + part
+        for part in range(halves):
+            at = first + part
             added = flux[:, 128 * part : 128 * part + 128]
             if face < 2:
                 rows = pl.ds(7 * face, 64, stride=8)
-                base_sc[at, rows, :] += factor_sc[at, rows, :] * added
+                total[at, rows, :] += factor[at, rows, :] * added
             elif face < 4:
                 for k in range(8):
                     rows = slice(64 * k + 56 * (face - 2), 64 * k + 56 * (face - 2) + 8)
-                    base_sc[at, rows, :] += factor_sc[at, rows, :] * added[8 * k : 8 * k + 8]
+                    total[at, rows, :] += factor[at, rows, :] * added[8 * k : 8 * k + 8]
             else:
                 rows = slice(448 * (face - 4), 448 * (face - 4) + 64)
-                base_sc[at, rows, :] += factor_sc[at, rows, :] * added
-    for part in range(TILE // 128):
-        out_ref[128 * part : 128 * part + 128, :] = base_sc[2 * (slot - 1) + part].T
+                total[at, rows, :] += factor[at, rows, :] * added
+
+    def write():
+        out([total[first + part].T for part in range(halves)])
+
+    return [functools.partial(one, face) for face in range(6)] + [write]
+
+
+def run_mixed(faces, pieces, late):
+    done = 0
+    for number, face in enumerate(faces):
+        face()
+        upto = -(-len(pieces) * (number + 1) // len(faces))
+        for piece in pieces[done:upto]:
+            piece()
+        done = upto
+    for piece in pieces[done:] + late:
+        piece()
 
 
 def cells_kernel(low, inner, tiles, width, has_edge, chained, *refs):
-    soil_ref, class_ref, level_ref, head_ref, own_ref, near_ref, after_ref = refs[:7]
-    edge_ref = refs[7] if has_edge else None
-    out_ref, top_ref, table, turned, cond, base_sc, factor_sc = refs[7 + has_edge + chained :]
-    step = pl.program_id(0)
-    last = inner + 1
+    soil_ref, class_any, level_any, near_any, pressure_ref, after_ref = refs[:6]
+    edge_ref = refs[6] if has_edge else None
+    (
+        out_ref, top_any, table, turned, cond, base_sc, factor_sc, inbox, outbox, edge,
+        class_ref, level_ref, near_ref, top_ref, arrived, stored, small,
+    ) = refs[6 + has_edge + chained :]
     own, _, _ = position(width)
-
-    def at_edge():
-        halo_tile(
+    loads, stores = [], []
+    for number, (source, kept) in enumerate(((class_any, class_ref), (level_any, level_ref), (near_any, near_ref))):
+        smalls = pltpu.make_async_copy(source, kept, small.at[number])
+        smalls.start()
+        loads.append(smalls)
+    small_loads, loads = loads, []
+    for slot in range(inner + 2):
+        tile = low + slot - 1
+        if 0 <= tile < tiles:
+            rows = pl.ds(tile * TILE, TILE)
+            load = pltpu.make_async_copy(pressure_ref.at[rows, :], inbox.at[slot], arrived.at[slot])
+        else:
+            load = pltpu.make_async_copy(edge_ref, edge, arrived.at[slot])
+        load.start()
+        loads.append(load)
+    for load in small_loads:
+        load.wait()
+
+    def tile_lanes(ref, slot):
+        start = (low + slot - 1) * TILE
+        return lambda lanes: ref[:, start + lanes.start : start + lanes.stop]
+
+    def around(slot):
+        loads[slot].wait()
+        if 0 <= low + slot - 1 < tiles:
+            return halo_pieces(
+                soil_ref, tile_lanes(class_ref, slot), lambda lanes: inbox[slot, lanes, :], slot, table,
+                turned.at[slot % 2],
+            )
+        return halo_pieces(
             soil_ref,
-            lambda lanes: edge_ref[HB : HB + 8, lanes][0:1, :].astype(I32),
-            lambda lanes: edge_ref[lanes, :],
-            step, table, turned, cond,
-        )
-
-    def beside():
-        halo_tile(
-            soil_ref,
-            lambda lanes: class_ref[:, lanes],
-            lambda lanes: head_ref[lanes, :],
-            step, table, turned, cond,
-        )
-
-    def within():
-        inner_tile(
-            soil_ref, class_ref, level_ref, head_ref, step, table, turned, cond, base_sc, factor_sc, top_ref
-        )
-
-    def faces():
-        slot = step - 2
+            lambda lanes: edge[HB : HB + 8, lanes][0:1, :].astype(I32),
+            lambda lanes: edge[lanes, :],
+            slot, table, turned.at[slot % 2],
+        )
+
+    def within(slot):
+        loads[slot].wait()
+        return inner_pieces(
+            soil_ref, tile_lanes(class_ref, slot), tile_lanes(level_ref, slot),
+            lambda lanes: inbox[slot, lanes, :],
+            slot, table, turned.at[slot % 2], cond.at[slot % 2], base_sc, factor_sc, top_ref,
+        )
+
+    def faces(slot):
         first_row = own * tiles * TILE + (low + slot - 2) * TILE
-        face_tile(first_row, own_ref[...], near_ref, slot, table, base_sc, factor_sc, out_ref)
-
-    first = at_edge if low == 0 else beside
-    final = at_edge if low + inner == tiles else beside
-
-    @pl.when(step == 0)
-    def _():
-        first()
-
-    @pl.when((step > 0) & (step < 3))
-    def _():
-        within()
-
-    if last > 3:
-        @pl.when((step >= 3) & (step < last))
-        def _():
-            faces()
-            within()
-
-    @pl.when(step == last)
-    def _():
-        faces()
-        final()
-
-    @pl.when(step == last + 1)
-    def _():
-        faces()
+        start = (low + slot - 1) * TILE
+
+        def near(row):
+            return near_ref[row : row + 1, start : start + TILE]
+
+        def out(halves):
+            for number, value in enumerate(halves):
+                outbox[slot - 1, 128 * number : 128 * number + 128, :] = value
+            store = pltpu.make_async_copy(
+                outbox.at[slot - 1], out_ref.at[pl.ds(start, TILE), :], stored.at[slot - 1]
+            )
+            store.start()
+            stores.append(store)
+
+        return face_pieces(
+            first_row, level_ref[:, start : start + TILE], near, slot, table, base_sc, factor_sc, out
+        )
+
+    for step in range(inner + 3):
+        if step == inner + 2:
+            store = pltpu.make_async_copy(top_ref, top_any, small.at[3])
+            store.start()
+            stores.append(store)
+        work = [], []
+        if step in (0, inner + 1):
+            work = around(step)
+        elif step <= inner:
+            work = within(step)
+        run_mixed(faces(step - 2) if step >= 3 else [], *work)
+    for store in stores:
+        store.wait()
 
 
 def cells(shape, soil, kinds, near, pressure, edge, after, part, head):
     tiles = pressure.shape[0] // TILE
     low, inner = PARTS[part]
     extra = [value for value in (edge, head) if value is not None]
-    extra_specs = [] if edge is None else [pl.BlockSpec(edge.shape, lambda t: (0, 0))]
-    aliases = {}
-    if head is not None:
-        aliases = {7 + len(extra_specs): 0}
-        extra_specs = extra_specs + [ANY]
-    seen = lambda t: jnp.clip(t + low - 1, max(low - 1, 0), min(low + inner, tiles - 1))
-    done = lambda t: jnp.clip(t + low - 3, low, low + inner - 1)
+    aliases = {} if head is None else {5 + len(extra): 0}
     return pl.pallas_call(
         functools.partial(
             cells_kernel, low, inner, tiles, shape[1], int(edge is not None), int(head is not None)
         ),
-        grid=(inner + 3,),
-        in_specs=[
-            SMEM,
-            pl.BlockSpec((1, TILE), lambda t: (0, seen(t))),
-            pl.BlockSpec((1, TILE), lambda t: (0, seen(t))),
-            pl.BlockSpec((TILE, 512), lambda t: (seen(t), 0)),
-            pl.BlockSpec((1, TILE), lambda t: (0, done(t))),
-            pl.BlockSpec((near.shape[0], TILE), lambda t: (0, done(t))),
-            ANY,
-        ]
-        + extra_specs,
-        out_specs=[
-            pl.BlockSpec((TILE, 512), lambda t: (done(t), 0)),
-            pl.BlockSpec((TILE // 128, 64, 128), lambda t: (jnp.clip(t - 1, 0, inner - 1), 0, 0)),
-        ],
+        in_specs=[SMEM] + [ANY] * (5 + len(extra)),
+        out_specs=[ANY, ANY],
         out_shape=[
             jax.ShapeDtypeStruct(pressure.shape, F32),
             jax.ShapeDtypeStruct((2 * inner, 64, 128), F32),
@@ -644,10 +693,20 @@
         input_output_aliases=aliases,
         scratch_shapes=[
             pltpu.VMEM((1536, (inner + 2) * TILE), BF16),
-            pltpu.VMEM((TILE // 128, 512, 128), F32),
-            pltpu.VMEM((TILE // 128, 512, 128), F32),
+            pltpu.VMEM((2, TILE // 128, 512, 128), F32),
+            pltpu.VMEM((2, TILE // 128, 512, 128), F32),
             pltpu.VMEM((2 * inner, 512, 128), F32),
             pltpu.VMEM((2 * inner, 512, 128), F32),
+            pltpu.VMEM((inner + 2, TILE, 512), F32),
+            pltpu.VMEM((inner, TILE, 512), F32),
+            pltpu.VMEM((HB + 8, 512), F32),
+            pltpu.VMEM(kinds[0].shape, I32),
+            pltpu.VMEM(kinds[1].shape, I32),
+            pltpu.VMEM(near.shape, I32),
+            pltpu.VMEM((2 * inner, 64, 128), F32),
+            pltpu.SemaphoreType.DMA((inner + 2,)),
+            pltpu.SemaphoreType.DMA((inner,)),
+            pltpu.SemaphoreType.DMA((4,)),
         ],
         compiler_params=pltpu.CompilerParams(vmem_limit_bytes=VMEM_LIMIT),
         cost_estimate=pl.CostEstimate(
@@ -656,7 +715,7 @@
             transcendentals=inner * TILE * 512 * 8,
         ),
         name="cells",
-    )(soil, *kinds, pressure, kinds[1], near, after, *extra)
+    )(soil, *kinds, near, pressure, after, *extra)
 
 
 def shifted(value, axis, steps, wrap=True):

time: 81 us -> 79.5 us (0.981)
  Pallas kernels: 42.8 us -> 41.2 us
    pallas_call x3, Pallas kernels: 28.3 us -> 26.7 us  [cells(): pl.pallas_call(functools.partial(cells_kernel, low, inner, tiles, shape[1...]
  transfers between devices with their start and end apart: 8 -> 8, of which waited for: 0 -> 0; matrix products, arithmetic and copies ran while one was open for 6% -> 6% of each run, Pallas kernels for 41% -> 40%
where the time goes in v5:
time: 79.5 us; the launch traced here: 78.7 us
  Pallas kernels  41.2 us (52%)
  starting transfers between devices  28.8 us (36%)
  local copies, waits for them, and re-layouts  5.13 us (6%)
  other arithmetic  2.46 us (3%)
  between operations  1.11 us (1%)
    pallas_call x3, Pallas kernels, cells(): pl.pallas_call(functools.partial(cells_kernel, low, inner, tiles, shape[1...  26.7 us
    ppermute x6, starting transfers between devices, shifted(): return lax.ppermute(value, axis, pairs)  16.3 us
    all_to_all x1, starting transfers between devices, per_device(): returned = lax.all_to_all(reply, 'gy', 0, 0)  6.38 us
    all_to_all x1, starting transfers between devices, per_device(): got = lax.all_to_all(send, 'gy', 0, 0)  6.1 us
    pallas_call x1, Pallas kernels, finish(): pl.pallas_call(functools.partial(sweep_kernel, place), in_specs=[VMEM] *...  5.75 us
    pallas_call x1, Pallas kernels, surface(): pl.pallas_call(functools.partial(surface_kernel, shape), in_specs=[SMEM,...  4.86 us
    pallas_call x1, Pallas kernels, route(): pl.pallas_call(functools.partial(route_kernel, shape), grid=(1,), in_spec...  3.91 us
    unnamed x26, local copies, waits for them, and re-layouts  3.04 us
  transfers between devices with their start and end apart: 8, of which 0 were waited for; matrix products, arithmetic and copies ran while one was open for 6% of the time, Pallas kernels for 40%

profile of v5, /device:TPU:1, one launch (start us, length us, event | category | flops | bytes accessed | tf_op | source)
XLA Modules:
  0.0 78.7 jit_solution(14276098038136227825)
XLA Ops:
  0.6 0.0 copy-start.10
  0.6 0.0 copy-start.11
  0.7 3.9 %route.1 = (f32[8,88,128]{2,1,0:T(8,128)}, s32[1,2048]{1,0:T(1,128)}, f32[2,24,128]{2,1,0:T(8,128)}) custom-call(s32[1,2048]{1,0:T(1,128)} %bitcast.25, s32[1,2048]{1,0:T(1,128)} %bitcast.29, s32[1,2048]{1,0:T(1,128)} %bitcast.35, f32[2048,512]{1,0:T(8,128)} %refs_4_.5, f32[128,256]{1,0:T(8,128)} %depth_ref.5, f32[128,256]{1,0:T(8,128)} %bed_ref.3, ...), custom_call_target="tpu_custom_call" | custom-call | tf_op jit(solution)/shard_map/route/pallas_call | solution.py:173
  4.6 6.1 %all-to-all-start = ((f32[8,88,128]{2,1,0:T(8,128)}), f32[8,88,128]{2,1,0:T(8,128)S(1)}, u32[]{:S(2)}, u32[]{:S(2)}) async-start(f32[8,88,128]{2,1,0:T(8,128)} %get-tuple-element.25), calls=%async_computation | async-start | bytes 720896 | tf_op jit(solution)/shard_map/all_to_all | solution.py:750
  10.7 1.3 %fusion = (f32[256,512]{1,0:T(8,128)S(1)}, f32[256,512]{1,0:T(8,128)S(1)}) fusion(f32[2048,512]{1,0:T(8,128)} %refs_4_.5), kind=kLoop, calls=%fused_computation.25 | loop fusion | bytes 2097152 | tf_op jit(solution)/shard_map/slice | solution.py:746
  11.9 0.7 slice_convert_fusion
  12.7 3.5 %collective-permute-start.4 = (f32[264,512]{1,0:T(8,128)S(1)}, f32[264,512]{1,0:T(8,128)S(1)}, u32[]{:S(2)}, u32[]{:S(2)}) collective-permute-start(f32[264,512]{1,0:T(8,128)S(1)} %select_maximum_fusion.1), channel_id=1, source_target_pairs={{0,1},{1,2},{2,3},{3,4},{4,5},{5,6},{6,7},{7,8},{8,9},{9,10},{10,1... | collective-permute-start | bytes 1622024 | tf_op jit(solution)/shard_map/ppermute | solution.py:724
  16.3 1.9 %collective-permute-start.5 = (f32[264,512]{1,0:T(8,128)S(1)}, f32[264,512]{1,0:T(8,128)S(1)}, u32[]{:S(2)}, u32[]{:S(2)}) collective-permute-start(f32[264,512]{1,0:T(8,128)S(1)} %select_maximum_fusion), channel_id=1, source_target_pairs={{1,0},{2,1},{3,2},{4,3},{5,4},{6,5},{7,6},{8,7},{9,8},{10,9},{11,1... | collective-permute-start | bytes 1622024 | tf_op jit(solution)/shard_map/ppermute | solution.py:724
  18.2 0.0 copy-done.12
  18.3 0.1 pad.21.clone
  18.3 0.0 copy-done.10
  18.3 0.0 copy-done.11
  18.3 0.7 pad_add_fusion.refs_3_
  19.0 0.0 all-to-all-done.got_ref
  19.1 0.0 copy-start.4
  19.1 1.3 %collective-permute-start = (f32[376,128]{1,0:T(8,128)S(1)}, f32[376,128]{1,0:T(8,128)S(1)}, u32[]{:S(2)}, u32[]{:S(2)}) collective-permute-start(f32[376,128]{1,0:T(8,128)S(1)} %get-tuple-element.49.refs_5_), channel_id=1, source_target_pairs={{0,8},{8,16},{16,24},{24,32},{32,40},{40,48},{48,56},{56,64},{64,7... | collective-permute-start | bytes 577544 | tf_op jit(solution)/shard_map/ppermute | solution.py:724
  20.4 4.8 %collective-permute-start.1 = (f32[376,128]{1,0:T(8,128)S(1)}, f32[376,128]{1,0:T(8,128)S(1)}, u32[]{:S(2)}, u32[]{:S(2)}) collective-permute-start(f32[376,128]{1,0:T(8,128)S(1)} %get-tuple-element.48), channel_id=1, source_target_pairs={{0,120},{8,0},{16,8},{24,16},{32,24},{40,32},{48,40},{56,48},{64,5... | collective-permute-start | bytes 577544 | tf_op jit(solution)/shard_map/ppermute | solution.py:724
  25.2 0.0 copy-done.4
  25.2 7.6 %cells.3 = (f32[2048,512]{1,0:T(8,128)}, f32[4,64,128]{2,1,0:T(8,128)}) custom-call(f32[5,12]{1,0:T(8,128)} %refs_0_.5, s32[1,2048]{1,0:T(1,128)} %bitcast.26, s32[1,2048]{1,0:T(1,128)} %bitcast.30, s32[12,2048]{1,0:T(8,128)} %pad_add_fusion.refs_3_, f32[2048,512]{1,0:T(8,128)} %refs_4_.5, f32[376,128]{1,0:T(8,128)} %copy-done.4), custom_call_target="tpu_custom_call" | custom-call | flops 1207959552 | bytes 4194304 | tf_op jit(solution)/shard_map/cells/pallas_call | solution.py:683
  32.8 0.0 collective-permute-done.up_ref
  32.9 0.0 copy-start.2
  32.9 0.0 collective-permute-done.1.down_ref
  32.9 0.0 copy-start.3
  32.9 0.0 copy-done
  32.9 0.6 copy-done.2
  33.5 0.0 copy-done.3
  33.6 4.9 %surface.1 = (f32[8,32,128]{2,1,0:T(8,128)}, f32[264,128]{1,0:T(8,128)}, f32[264,128]{1,0:T(8,128)}, f32[128,256]{1,0:T(8,128)}, f32[2,8,128]{2,1,0:T(8,128)}) custom-call(f32[5,12]{1,0:T(8,128)} %refs_0_.5, f32[8,88,128]{2,1,0:T(8,128)} %copy-done, f32[376,128]{1,0:T(8,128)} %copy-done.2, f32[376,128]{1,0:T(8,128)} %copy-done.3, f32[128,256]{1,0:T(8,128)} %depth_ref.5, ...), custom_call_target="tpu_custom_call" | custom-call | tf_op jit(solution)/shard_map/surface/pallas_call | solution.py:291
  38.5 0.0 collective-permute-start.2
  38.5 4.8 %collective-permute-start.3 = (f32[264,128]{1,0:T(8,128)}, f32[264,128]{1,0:T(8,128)S(1)}, u32[]{:S(2)}, u32[]{:S(2)}) collective-permute-start(f32[264,128]{1,0:T(8,128)} %get-tuple-element.30), channel_id=1, source_target_pairs={{0,120},{8,0},{16,8},{24,16},{32,24},{40,32},{48,40},{56,48},{64,5... | collective-permute-start | bytes 405512 | tf_op jit(solution)/shard_map/ppermute | solution.py:724
  43.2 0.7 slice_bitcast_fusion.3
  43.9 0.0 collective-permute-done.4.refs_6_
  43.9 0.8 %copy-done.6 = f32[264,512]{1,0:T(8,128)} copy-done((f32[264,512]{1,0:T(8,128)}, f32[264,512]{1,0:T(8,128)S(1)}, u32[]{:S(2)}) %copy-start.6) | copy-done | bytes 540696
  44.7 9.6 %cells.4 = (f32[2048,512]{1,0:T(8,128)}, f32[6,64,128]{2,1,0:T(8,128)}) custom-call(f32[5,12]{1,0:T(8,128)} %refs_0_.5, s32[1,2048]{1,0:T(1,128)} %bitcast.27, s32[1,2048]{1,0:T(1,128)} %bitcast.31, s32[12,2048]{1,0:T(8,128)} %pad_add_fusion.refs_3_, f32[2048,512]{1,0:T(8,128)} %refs_4_.5, ...), custom_call_target="tpu_custom_call", output_to_operand_aliasing={{0}: (7, {})} | custom-call | flops 1811939328 | bytes 6291456 | tf_op jit(solution)/shard_map/cells/pallas_call | solution.py:683
  54.3 0.0 collective-permute-done.2.low_ref
  54.3 0.0 copy-start.7
  54.3 0.0 collective-permute-done.3.high_ref
  54.4 0.0 copy-start.8
  54.4 0.1 maximum_maximum_fusion
  54.5 0.1 broadcast_select_fusion.1
  54.6 0.1 broadcast_select_fusion
  54.7 0.7 pad_maximum_fusion.refs_5_
  55.4 6.4 %all-to-all-start.1 = ((f32[8,72,128]{2,1,0:T(8,128)}), f32[8,72,128]{2,1,0:T(8,128)S(1)}, u32[]{:S(2)}, u32[]{:S(2)}) async-start(f32[8,72,128]{2,1,0:T(8,128)} %pad_maximum_fusion.refs_5_), calls=%async_computation.1 | async-start | bytes 589824 | tf_op jit(solution)/shard_map/all_to_all | solution.py:783
  61.8 0.0 collective-permute-done.5.refs_6_
  61.8 0.8 %copy-done.5 = f32[264,512]{1,0:T(8,128)} copy-done((f32[264,512]{1,0:T(8,128)}, f32[264,512]{1,0:T(8,128)S(1)}, u32[]{:S(2)}) %copy-start.5) | copy-done | bytes 540696
  62.6 9.5 %cells.5 = (f32[2048,512]{1,0:T(8,128)}, f32[6,64,128]{2,1,0:T(8,128)}) custom-call(f32[5,12]{1,0:T(8,128)} %refs_0_.5, s32[1,2048]{1,0:T(1,128)} %bitcast.28, s32[1,2048]{1,0:T(1,128)} %bitcast.32, s32[12,2048]{1,0:T(8,128)} %pad_add_fusion.refs_3_, f32[2048,512]{1,0:T(8,128)} %refs_4_.5, ...), custom_call_target="tpu_custom_call", output_to_operand_aliasing={{0}: (7, {})} | custom-call | flops 1811939328 | bytes 6291456 | tf_op jit(solution)/shard_map/cells/pallas_call | solution.py:683
  72.1 0.0 all-to-all-done.1.back_ref
  72.1 0.7 copy-done.1
  72.8 5.8 %finish.1 = (f32[128,256]{1,0:T(8,128)}, f32[2048,512]{1,0:T(8,128)}) custom-call(f32[128,256]{1,0:T(8,128)} %depth_ref.5, f32[128,256]{1,0:T(8,128)} %bed_ref.3, f32[128,256]{1,0:T(8,128)} %rough_ref.3, f32[8,88,128]{2,1,0:T(8,128)} %copy-done, f32[376,128]{1,0:T(8,128)} %copy-done.2, f32[376,128]{1,0:T(8,128)} %copy-done.3, ...), custom_call_target="tpu_custom_call", output_to_operand_aliasing={{1}: (14, {})} | custom-call | tf_op jit(solution)/shard_map/finish/pallas_call | solution.py:431
  (22 shorter events, 0.2 us)
Async XLA Ops:
  0.6 17.7 %copy-start.10 = (s32[2048,6]{0,1:T(8,128)S(1)}, s32[2048,6]{0,1:T(8,128)}, u32[]{:S(2)}) copy-start(s32[2048,6]{0,1:T(8,128)} %param.14) | copy-start | bytes 147460
  0.6 17.7 %copy-start.11 = (s32[2048,6]{0,1:T(8,128)S(1)}, s32[2048,6]{0,1:T(8,128)}, u32[]{:S(2)}) copy-start(s32[2048,6]{0,1:T(8,128)} %param.13) | copy-start | bytes 147460
  4.6 13.7 %copy-start.12 = (f32[2,24,128]{2,1,0:T(8,128)S(1)}, f32[2,24,128]{2,1,0:T(8,128)}, u32[]{:S(2)}) copy-start(f32[2,24,128]{2,1,0:T(8,128)} %get-tuple-element.26) | copy-start | bytes 73732
  4.6 14.5 %all-to-all-start = ((f32[8,88,128]{2,1,0:T(8,128)}), f32[8,88,128]{2,1,0:T(8,128)S(1)}, u32[]{:S(2)}, u32[]{:S(2)}) async-start(f32[8,88,128]{2,1,0:T(8,128)} %get-tuple-element.25), calls=%async_computation | async-start | bytes 720896 | tf_op jit(solution)/shard_map/all_to_all | solution.py:750
  12.7 31.2 %collective-permute-start.4 = (f32[264,512]{1,0:T(8,128)S(1)}, f32[264,512]{1,0:T(8,128)S(1)}, u32[]{:S(2)}, u32[]{:S(2)}) collective-permute-start(f32[264,512]{1,0:T(8,128)S(1)} %select_maximum_fusion.1), channel_id=1, source_target_pairs={{0,1},{1,2},{2,3},{3,4},{4,5},{5,6},{6,7},{7,8},{8,9},{9,10},{10,1... | collective-permute-start | bytes 1622024 | tf_op jit(solution)/shard_map/ppermute | solution.py:724
  16.3 45.5 %collective-permute-start.5 = (f32[264,512]{1,0:T(8,128)S(1)}, f32[264,512]{1,0:T(8,128)S(1)}, u32[]{:S(2)}, u32[]{:S(2)}) collective-permute-start(f32[264,512]{1,0:T(8,128)S(1)} %select_maximum_fusion), channel_id=1, source_target_pairs={{1,0},{2,1},{3,2},{4,3},{5,4},{6,5},{7,6},{8,7},{9,8},{10,9},{11,1... | collective-permute-start | bytes 1622024 | tf_op jit(solution)/shard_map/ppermute | solution.py:724
  19.0 13.9 %copy-start = (f32[8,88,128]{2,1,0:T(8,128)}, f32[8,88,128]{2,1,0:T(8,128)S(1)}, u32[]{:S(2)}) copy-start(f32[8,88,128]{2,1,0:T(8,128)S(1)} %all-to-all-done.got_ref) | copy-start | bytes 1081348
  19.1 6.1 %copy-start.4 = (f32[376,128]{1,0:T(8,128)}, f32[376,128]{1,0:T(8,128)S(1)}, u32[]{:S(2)}) copy-start(f32[376,128]{1,0:T(8,128)S(1)} %get-tuple-element.49.refs_5_) | copy-start | bytes 577540
  19.1 13.7 %collective-permute-start = (f32[376,128]{1,0:T(8,128)S(1)}, f32[376,128]{1,0:T(8,128)S(1)}, u32[]{:S(2)}, u32[]{:S(2)}) collective-permute-start(f32[376,128]{1,0:T(8,128)S(1)} %get-tuple-element.49.refs_5_), channel_id=1, source_target_pairs={{0,8},{8,16},{16,24},{24,32},{32,40},{40,48},{48,56},{56,64},{64,7... | collective-permute-start | bytes 577544 | tf_op jit(solution)/shard_map/ppermute | solution.py:724
  20.4 12.5 %collective-permute-start.1 = (f32[376,128]{1,0:T(8,128)S(1)}, f32[376,128]{1,0:T(8,128)S(1)}, u32[]{:S(2)}, u32[]{:S(2)}) collective-permute-start(f32[376,128]{1,0:T(8,128)S(1)} %get-tuple-element.48), channel_id=1, source_target_pairs={{0,120},{8,0},{16,8},{24,16},{32,24},{40,32},{48,40},{56,48},{64,5... | collective-permute-start | bytes 577544 | tf_op jit(solution)/shard_map/ppermute | solution.py:724
  32.9 0.7 copy-start.2
  32.9 0.7 copy-start.3
  38.5 15.9 %collective-permute-start.2 = (f32[264,128]{1,0:T(8,128)}, f32[264,128]{1,0:T(8,128)S(1)}, u32[]{:S(2)}, u32[]{:S(2)}) collective-permute-start(f32[264,128]{1,0:T(8,128)} %get-tuple-element.29), channel_id=1, source_target_pairs={{0,8},{8,16},{16,24},{24,32},{32,40},{40,48},{48,56},{56,64},{64,7... | collective-permute-start | bytes 405512 | tf_op jit(solution)/shard_map/ppermute | solution.py:724
  38.5 15.9 %collective-permute-start.3 = (f32[264,128]{1,0:T(8,128)}, f32[264,128]{1,0:T(8,128)S(1)}, u32[]{:S(2)}, u32[]{:S(2)}) collective-permute-start(f32[264,128]{1,0:T(8,128)} %get-tuple-element.30), channel_id=1, source_target_pairs={{0,120},{8,0},{16,8},{24,16},{32,24},{40,32},{48,40},{56,48},{64,5... | collective-permute-start | bytes 405512 | tf_op jit(solution)/shard_map/ppermute | solution.py:724
  43.9 0.8 %copy-start.6 = (f32[264,512]{1,0:T(8,128)}, f32[264,512]{1,0:T(8,128)S(1)}, u32[]{:S(2)}) copy-start(f32[264,512]{1,0:T(8,128)S(1)} %collective-permute-done.4.refs_6_) | copy-start | bytes 1622020
  44.7 9.9 %copy-start.9 = (f32[8,32,128]{2,1,0:T(8,128)S(1)}, f32[8,32,128]{2,1,0:T(8,128)}, u32[]{:S(2)}) copy-start(f32[8,32,128]{2,1,0:T(8,128)} %get-tuple-element.31.refs_5_) | copy-start | bytes 393220
  54.3 17.7 %copy-start.7 = (f32[264,128]{1,0:T(8,128)}, f32[264,128]{1,0:T(8,128)S(1)}, u32[]{:S(2)}) copy-start(f32[264,128]{1,0:T(8,128)S(1)} %collective-permute-done.2.low_ref) | copy-start | bytes 405508
  54.4 17.7 %copy-start.8 = (f32[264,128]{1,0:T(8,128)}, f32[264,128]{1,0:T(8,128)S(1)}, u32[]{:S(2)}) copy-start(f32[264,128]{1,0:T(8,128)S(1)} %collective-permute-done.3.high_ref) | copy-start | bytes 405508
  55.4 16.7 %all-to-all-start.1 = ((f32[8,72,128]{2,1,0:T(8,128)}), f32[8,72,128]{2,1,0:T(8,128)S(1)}, u32[]{:S(2)}, u32[]{:S(2)}) async-start(f32[8,72,128]{2,1,0:T(8,128)} %pad_maximum_fusion.refs_5_), calls=%async_computation.1 | async-start | bytes 589824 | tf_op jit(solution)/shard_map/all_to_all | solution.py:783
  61.8 0.8 %copy-start.5 = (f32[264,512]{1,0:T(8,128)}, f32[264,512]{1,0:T(8,128)S(1)}, u32[]{:S(2)}) copy-start(f32[264,512]{1,0:T(8,128)S(1)} %collective-permute-done.5.refs_6_) | copy-start | bytes 1622020
  72.1 0.7 copy-start.1

commit v6 on v5

--- a/solution.py
+++ b/solution.py
@@ -24,10 +24,12 @@
 OPPOSITE = (1, 0, 3, 2, 5, 4)
 GRAVITY = (0.0, 0.0, 0.0, 0.0, -1.0, 1.0)
 VMEM_LIMIT = 60 * 1024 * 1024
+VMEM_SHARE = 32 * 1024 * 1024
 
 VMEM = pl.BlockSpec(memory_space=pltpu.VMEM)
 SMEM = pl.BlockSpec(memory_space=pltpu.SMEM)
 ANY = pl.BlockSpec(memory_space=pl.ANY)
+HBM = pl.BlockSpec(memory_space=pltpu.HBM)
 
 
 def position(width):
@@ -304,7 +306,7 @@
             pltpu.VMEM((1, width * 128), I32),
             pltpu.VMEM((patches, width * 128), BF16),
         ],
-        compiler_params=pltpu.CompilerParams(vmem_limit_bytes=VMEM_LIMIT),
+        compiler_params=pltpu.CompilerParams(vmem_limit_bytes=VMEM_SHARE),
         name="surface",
     )(soil, got, up, down, water_depth, after)
 
@@ -430,11 +432,11 @@
     blocks = head.shape[0]
     return pl.pallas_call(
         functools.partial(sweep_kernel, place),
-        in_specs=[VMEM] * 14 + [ANY],
-        out_specs=[VMEM, ANY],
+        in_specs=[VMEM] * 14 + [HBM],
+        out_specs=[VMEM, HBM],
         out_shape=[
             jax.ShapeDtypeStruct(water_depth.shape, F32),
-            jax.ShapeDtypeStruct(head.shape, F32),
+            pltpu.HBM(head.shape, F32),
         ],
         input_output_aliases={14: 1},
         scratch_shapes=[pltpu.VMEM(shape, F32)] * 4
@@ -446,7 +448,7 @@
             pltpu.SemaphoreType.DMA,
             pltpu.SemaphoreType.DMA((blocks // TILE,)),
         ],
-        compiler_params=pltpu.CompilerParams(vmem_limit_bytes=VMEM_LIMIT),
+        compiler_params=pltpu.CompilerParams(vmem_limit_bytes=VMEM_SHARE),
         name="finish",
     )(water_depth, *rest)
 
@@ -684,10 +686,10 @@
         functools.partial(
             cells_kernel, low, inner, tiles, shape[1], int(edge is not None), int(head is not None)
         ),
-        in_specs=[SMEM] + [ANY] * (5 + len(extra)),
-        out_specs=[ANY, ANY],
+        in_specs=[SMEM, ANY, ANY, ANY, HBM, ANY] + [ANY] * (edge is not None) + [HBM] * (head is not None),
+        out_specs=[HBM, ANY],
         out_shape=[
-            jax.ShapeDtypeStruct(pressure.shape, F32),
+            pltpu.HBM(pressure.shape, F32),
             jax.ShapeDtypeStruct((2 * inner, 64, 128), F32),
         ],
         input_output_aliases=aliases,
@@ -708,7 +710,7 @@
             pltpu.SemaphoreType.DMA((inner,)),
             pltpu.SemaphoreType.DMA((4,)),
         ],
-        compiler_params=pltpu.CompilerParams(vmem_limit_bytes=VMEM_LIMIT),
+        compiler_params=pltpu.CompilerParams(vmem_limit_bytes=VMEM_SHARE),
         cost_estimate=pl.CostEstimate(
             flops=inner * 6 * 2 * 256 * 256 * 768,
             bytes_accessed=inner * TILE * 512 * 16,

time: 79.5 us -> 75.3 us (0.947)
  Pallas kernels: 41.2 us -> 36.3 us
    pallas_call x3, Pallas kernels: 26.7 us -> 24.6 us  [cells(): pl.pallas_call(functools.partial(cells_kernel, low, inner, tiles, shape[1...]
    concatenate x2, other arithmetic: 0.07 us -> 1.68 us  [edge(): return jnp.concatenate([later[part], classes], axis=0)]
    pallas_call x1, Pallas kernels: 5.75 us -> 4.16 us  [finish(): pl.pallas_call(functools.partial(sweep_kernel, place), in_specs=[VMEM] *...]
    unnamed x26, local copies, waits for them, and re-layouts: 3.04 us -> 4.41 us
    pallas_call x1, Pallas kernels: 4.86 us -> 3.62 us  [surface(): pl.pallas_call(functools.partial(surface_kernel, shape), in_specs=[SMEM,...]
  transfers between devices with their start and end apart: 8 -> 8, of which waited for: 0 -> 0; matrix products, arithmetic and copies ran while one was open for 6% -> 5% of each run, Pallas kernels for 40% -> 38%
where the time goes in v6:
time: 75.3 us; the launch traced here: 74.8 us
  Pallas kernels  36.3 us (48%)
  starting transfers between devices  28.9 us (38%)
  local copies, waits for them, and re-layouts  5.82 us (8%)
  other arithmetic  2.71 us (4%)
  between operations  1.13 us (2%)
    pallas_call x3, Pallas kernels, cells(): pl.pallas_call(functools.partial(cells_kernel, low, inner, tiles, shape[1...  24.6 us
    ppermute x6, starting transfers between devices, shifted(): return lax.ppermute(value, axis, pairs)  16.4 us
    all_to_all x1, starting transfers between devices, per_device(): returned = lax.all_to_all(reply, 'gy', 0, 0)  6.37 us
    all_to_all x1, starting transfers between devices, per_device(): got = lax.all_to_all(send, 'gy', 0, 0)  6.11 us
    unnamed x26, local copies, waits for them, and re-layouts  4.41 us
    pallas_call x1, Pallas kernels, finish(): pl.pallas_call(functools.partial(sweep_kernel, place), in_specs=[VMEM] *...  4.16 us
    pallas_call x1, Pallas kernels, route(): pl.pallas_call(functools.partial(route_kernel, shape), grid=(1,), in_spec...  3.92 us
    pallas_call x1, Pallas kernels, surface(): pl.pallas_call(functools.partial(surface_kernel, shape), in_specs=[SMEM,...  3.62 us
  transfers between devices with their start and end apart: 8, of which 0 were waited for; matrix products, arithmetic and copies ran while one was open for 5% of the time, Pallas kernels for 38%

profile of v6, /device:TPU:1, one launch (start us, length us, event | category | flops | bytes accessed | tf_op | source)
XLA Modules:
  0.0 74.8 jit_solution(1813365059784575258)
XLA Ops:
  0.6 0.0 copy-start.6
  0.6 0.0 copy-start.10
  0.7 0.0 copy-start.11
  0.7 3.9 %route.1 = (f32[8,88,128]{2,1,0:T(8,128)}, s32[1,2048]{1,0:T(1,128)}, f32[2,24,128]{2,1,0:T(8,128)}) custom-call(s32[1,2048]{1,0:T(1,128)} %bitcast.22, s32[1,2048]{1,0:T(1,128)} %bitcast.26, s32[1,2048]{1,0:T(1,128)} %bitcast.35, f32[2048,512]{1,0:T(8,128)} %refs_4_.5, f32[128,256]{1,0:T(8,128)} %depth_ref.5, f32[128,256]{1,0:T(8,128)} %bed_ref.3, ...), custom_call_target="tpu_custom_call" | custom-call | tf_op jit(solution)/shard_map/route/pallas_call | solution.py:175
  4.6 6.1 %all-to-all-start = ((f32[8,88,128]{2,1,0:T(8,128)}), f32[8,88,128]{2,1,0:T(8,128)S(1)}, u32[]{:S(2)}, u32[]{:S(2)}) async-start(f32[8,88,128]{2,1,0:T(8,128)} %get-tuple-element.25), calls=%async_computation | async-start | bytes 720896 | tf_op jit(solution)/shard_map/all_to_all | solution.py:752
  10.7 1.3 %fusion = (f32[256,512]{1,0:T(8,128)S(1)}, f32[256,512]{1,0:T(8,128)S(1)}) fusion(f32[2048,512]{1,0:T(8,128)} %refs_4_.5), kind=kLoop, calls=%fused_computation.25 | loop fusion | bytes 2097152 | tf_op jit(solution)/shard_map/slice | solution.py:748
  12.0 0.0 copy-done.6
  12.0 0.0 copy-start.3
  12.0 0.8 %select_maximum_fusion.1 = f32[264,512]{1,0:T(8,128)} fusion(f32[1,256]{1,0:T(1,128)S(1)} %bitcast.37, f32[256,512]{1,0:T(8,128)S(1)} %get-tuple-element.47), kind=kLoop, calls=%fused_computation.1 | loop fusion | flops 405504 | bytes 1065984 | tf_op jit(solution)/shard_map/concatenate | solution.py:748
  12.8 3.5 %collective-permute-start.4 = (f32[264,512]{1,0:T(8,128)}, f32[264,512]{1,0:T(8,128)S(1)}, u32[]{:S(2)}, u32[]{:S(2)}) collective-permute-start(f32[264,512]{1,0:T(8,128)} %select_maximum_fusion.1), channel_id=1, source_target_pairs={{0,1},{1,2},{2,3},{3,4},{4,5},{5,6},{6,7},{7,8},{8,9},{9,10},{10,1... | collective-permute-start | bytes 1622024 | tf_op jit(solution)/shard_map/ppermute | solution.py:726
  16.4 0.8 %select_maximum_fusion = f32[264,512]{1,0:T(8,128)} fusion(f32[1,256]{1,0:T(1,128)S(1)} %bitcast.36, f32[256,512]{1,0:T(8,128)S(1)} %get-tuple-element.46), kind=kLoop, calls=%fused_computation | loop fusion | flops 405504 | bytes 1065984 | tf_op jit(solution)/shard_map/concatenate | solution.py:748
  17.2 1.9 %collective-permute-start.5 = (f32[264,512]{1,0:T(8,128)}, f32[264,512]{1,0:T(8,128)S(1)}, u32[]{:S(2)}, u32[]{:S(2)}) collective-permute-start(f32[264,512]{1,0:T(8,128)} %select_maximum_fusion), channel_id=1, source_target_pairs={{1,0},{2,1},{3,2},{4,3},{5,4},{6,5},{7,6},{8,7},{9,8},{10,9},{11,1... | collective-permute-start | bytes 1622024 | tf_op jit(solution)/shard_map/ppermute | solution.py:726
  19.1 0.0 copy-done.12
  19.2 0.1 pad.21.clone
  19.3 0.0 copy-done.10
  19.3 0.0 copy-done.11
  19.3 0.0 all-to-all-done.got_ref
  19.4 1.3 %collective-permute-start = (f32[376,128]{1,0:T(8,128)S(1)}, f32[376,128]{1,0:T(8,128)S(1)}, u32[]{:S(2)}, u32[]{:S(2)}) collective-permute-start(f32[376,128]{1,0:T(8,128)S(1)} %get-tuple-element.49.refs_5_), channel_id=1, source_target_pairs={{0,8},{8,16},{16,24},{24,32},{32,40},{40,48},{48,56},{56,64},{64,7... | collective-permute-start | bytes 577544 | tf_op jit(solution)/shard_map/ppermute | solution.py:726
  20.7 4.8 %collective-permute-start.1 = (f32[376,128]{1,0:T(8,128)S(1)}, f32[376,128]{1,0:T(8,128)S(1)}, u32[]{:S(2)}, u32[]{:S(2)}) collective-permute-start(f32[376,128]{1,0:T(8,128)S(1)} %get-tuple-element.48), channel_id=1, source_target_pairs={{0,120},{8,0},{16,8},{24,16},{32,24},{40,32},{48,40},{56,48},{64,5... | collective-permute-start | bytes 577544 | tf_op jit(solution)/shard_map/ppermute | solution.py:726
  25.5 0.0 copy-done.7
  25.5 0.0 copy-done.8
  25.5 0.0 copy-start
  25.5 2.2 %copy-done = f32[2048,512]{1,0:T(8,128)S(1)} copy-done((f32[2048,512]{1,0:T(8,128)S(1)}, f32[2048,512]{1,0:T(8,128)}, u32[]{:S(2)}) %copy-start) | copy-done | bytes 4194328
  27.7 6.9 %cells.3 = (f32[2048,512]{1,0:T(8,128)}, f32[4,64,128]{2,1,0:T(8,128)S(1)}) custom-call(f32[5,12]{1,0:T(8,128)S(1)} %copy-done.8, s32[1,2048]{1,0:T(1,128)S(1)} %bitcast.23, s32[1,2048]{1,0:T(1,128)S(1)} %bitcast.27, s32[12,2048]{1,0:T(8,128)S(1)} %pad_add_fusion.refs_3_, f32[2048,512]{1,0:T(8,128)S(1)} %copy-done, f32[376,128]{1,0:T(8,128)S(1)} %get-tuple-element.49.refs_5_), custom_call_target="tpu_custom_call" | custom-call | flops 1207959552 | bytes 4194304 | tf_op jit(solution)/shard_map/cells/pallas_call | solution.py:685
  34.6 0.0 collective-permute-done.up_ref
  34.7 0.0 collective-permute-done.1.down_ref
  34.7 0.0 copy-done.3
  34.7 3.6 %surface.1 = (f32[8,32,128]{2,1,0:T(8,128)S(1)}, f32[264,128]{1,0:T(8,128)S(1)}, f32[264,128]{1,0:T(8,128)S(1)}, f32[128,256]{1,0:T(8,128)S(1)}, f32[2,8,128]{2,1,0:T(8,128)S(1)}) custom-call(f32[5,12]{1,0:T(8,128)S(1)} %copy-done.8, f32[8,88,128]{2,1,0:T(8,128)S(1)} %all-to-all-done.got_ref, f32[376,128]{1,0:T(8,128)S(1)} %collective-permute-done.up_ref, ...), custom_call_target="tpu_custom_call" | custom-call | tf_op jit(solution)/shard_map/surface/pallas_call | solution.py:293
  38.3 0.1 collective-permute-start.2
  38.4 4.8 %collective-permute-start.3 = (f32[264,128]{1,0:T(8,128)S(1)}, f32[264,128]{1,0:T(8,128)S(1)}, u32[]{:S(2)}, u32[]{:S(2)}) collective-permute-start(f32[264,128]{1,0:T(8,128)S(1)} %get-tuple-element.30), channel_id=1, source_target_pairs={{0,120},{8,0},{16,8},{24,16},{32,24},{40,32},{48,40},{56,48},{64,5... | collective-permute-start | bytes 405512 | tf_op jit(solution)/shard_map/ppermute | solution.py:726
  43.2 0.0 collective-permute-done.4.refs_6_
  43.2 0.0 copy-done.1
  43.2 8.8 %cells.4 = (f32[2048,512]{1,0:T(8,128)}, f32[6,64,128]{2,1,0:T(8,128)S(1)}) custom-call(f32[5,12]{1,0:T(8,128)S(1)} %copy-done.8, s32[1,2048]{1,0:T(1,128)S(1)} %bitcast.24, s32[1,2048]{1,0:T(1,128)S(1)} %bitcast.28, s32[12,2048]{1,0:T(8,128)S(1)} %pad_add_fusion.refs_3_, f32[2048,512]{1,0:T(8,128)S(1)} %copy-done.1, ...), custom_call_target="tpu_custom_call", output_to_operand_aliasing={{0}: (7, {})} | custom-call | flops 1811939328 | bytes 6291456 | tf_op jit(solution)/shard_map/cells/pallas_call | solution.py:685
  52.0 0.0 collective-permute-done.2.low_ref
  52.0 0.0 collective-permute-done.3.high_ref
  52.0 0.1 maximum_maximum_fusion
  52.1 0.1 broadcast_select_fusion.1
  52.2 0.1 broadcast_select_fusion
  52.3 0.7 pad_maximum_fusion.refs_5_
  53.0 6.4 %all-to-all-start.1 = ((f32[8,72,128]{2,1,0:T(8,128)}), f32[8,72,128]{2,1,0:T(8,128)S(1)}, u32[]{:S(2)}, u32[]{:S(2)}) async-start(f32[8,72,128]{2,1,0:T(8,128)} %pad_maximum_fusion.refs_5_), calls=%async_computation.1 | async-start | bytes 589824 | tf_op jit(solution)/shard_map/all_to_all | solution.py:785
  59.4 0.0 collective-permute-done.5.refs_6_
  59.4 2.2 %copy-done.2 = f32[2048,512]{1,0:T(8,128)S(1)} copy-done((f32[2048,512]{1,0:T(8,128)S(1)}, f32[2048,512]{1,0:T(8,128)}, u32[]{:S(2)}) %copy-start.2) | copy-done | bytes 4194328
  61.6 8.8 %cells.5 = (f32[2048,512]{1,0:T(8,128)}, f32[6,64,128]{2,1,0:T(8,128)S(1)}) custom-call(f32[5,12]{1,0:T(8,128)S(1)} %copy-done.8, s32[1,2048]{1,0:T(1,128)S(1)} %bitcast.25, s32[1,2048]{1,0:T(1,128)S(1)} %bitcast.29, s32[12,2048]{1,0:T(8,128)S(1)} %pad_add_fusion.refs_3_, f32[2048,512]{1,0:T(8,128)S(1)} %copy-done.2, ...), custom_call_target="tpu_custom_call", output_to_operand_aliasing={{0}: (7, {})} | custom-call | flops 1811939328 | bytes 6291456 | tf_op jit(solution)/shard_map/cells/pallas_call | solution.py:685
  70.4 0.0 all-to-all-done.1.back_ref
  70.5 0.0 copy-done.4
  70.5 0.0 copy-done.5
  70.5 0.0 copy-done.9
  70.5 4.2 %finish.1 = (f32[128,256]{1,0:T(8,128)}, f32[2048,512]{1,0:T(8,128)}) custom-call(f32[128,256]{1,0:T(8,128)S(1)} %copy-done.3, f32[128,256]{1,0:T(8,128)S(1)} %copy-done.4, f32[128,256]{1,0:T(8,128)S(1)} %copy-done.5, f32[8,88,128]{2,1,0:T(8,128)S(1)} %all-to-all-done.got_ref, ...), custom_call_target="tpu_custom_call", output_to_operand_aliasing={{1}: (14, {})} | custom-call | tf_op jit(solution)/shard_map/finish/pallas_call | solution.py:433
  (22 shorter events, 0.1 us)
Async XLA Ops:
  0.6 11.3 %copy-start.6 = (s32[2048]{0:T(1024)S(1)}, s32[2048]{0:T(1024)}, u32[]{:S(2)}) copy-start(s32[2048]{0:T(1024)} %param.11) | copy-start | bytes 24580
  0.6 18.6 %copy-start.10 = (s32[2048,6]{0,1:T(8,128)S(1)}, s32[2048,6]{0,1:T(8,128)}, u32[]{:S(2)}) copy-start(s32[2048,6]{0,1:T(8,128)} %param.14) | copy-start | bytes 147460
  0.7 18.6 %copy-start.11 = (s32[2048,6]{0,1:T(8,128)S(1)}, s32[2048,6]{0,1:T(8,128)}, u32[]{:S(2)}) copy-start(s32[2048,6]{0,1:T(8,128)} %param.13) | copy-start | bytes 147460
  4.6 14.6 %copy-start.12 = (f32[2,24,128]{2,1,0:T(8,128)S(1)}, f32[2,24,128]{2,1,0:T(8,128)}, u32[]{:S(2)}) copy-start(f32[2,24,128]{2,1,0:T(8,128)} %get-tuple-element.26) | copy-start | bytes 73732
  4.6 20.9 %copy-start.7 = (s32[2048]{0:T(1024)S(1)}, s32[2048]{0:T(1024)}, u32[]{:S(2)}) copy-start(s32[2048]{0:T(1024)} %param.12) | copy-start | bytes 24580
  4.6 20.9 %copy-start.8 = (f32[5,12]{1,0:T(8,128)S(1)}, f32[5,12]{1,0:T(8,128)}, u32[]{:S(2)}) copy-start(f32[5,12]{1,0:T(8,128)} %refs_0_.5) | copy-start | bytes 724
  4.6 14.7 %all-to-all-start = ((f32[8,88,128]{2,1,0:T(8,128)}), f32[8,88,128]{2,1,0:T(8,128)S(1)}, u32[]{:S(2)}, u32[]{:S(2)}) async-start(f32[8,88,128]{2,1,0:T(8,128)} %get-tuple-element.25), calls=%async_computation | async-start | bytes 720896 | tf_op jit(solution)/shard_map/all_to_all | solution.py:752
  12.0 22.7 %copy-start.3 = (f32[128,256]{1,0:T(8,128)S(1)}, f32[128,256]{1,0:T(8,128)}, u32[]{:S(2)}) copy-start(f32[128,256]{1,0:T(8,128)} %depth_ref.5) | copy-start | bytes 393220
  12.8 30.3 %collective-permute-start.4 = (f32[264,512]{1,0:T(8,128)}, f32[264,512]{1,0:T(8,128)S(1)}, u32[]{:S(2)}, u32[]{:S(2)}) collective-permute-start(f32[264,512]{1,0:T(8,128)} %select_maximum_fusion.1), channel_id=1, source_target_pairs={{0,1},{1,2},{2,3},{3,4},{4,5},{5,6},{6,7},{7,8},{8,9},{9,10},{10,1... | collective-permute-start | bytes 1622024 | tf_op jit(solution)/shard_map/ppermute | solution.py:726
  17.2 42.2 %collective-permute-start.5 = (f32[264,512]{1,0:T(8,128)}, f32[264,512]{1,0:T(8,128)S(1)}, u32[]{:S(2)}, u32[]{:S(2)}) collective-permute-start(f32[264,512]{1,0:T(8,128)} %select_maximum_fusion), channel_id=1, source_target_pairs={{1,0},{2,1},{3,2},{4,3},{5,4},{6,5},{7,6},{8,7},{9,8},{10,9},{11,1... | collective-permute-start | bytes 1622024 | tf_op jit(solution)/shard_map/ppermute | solution.py:726
  19.4 15.2 %collective-permute-start = (f32[376,128]{1,0:T(8,128)S(1)}, f32[376,128]{1,0:T(8,128)S(1)}, u32[]{:S(2)}, u32[]{:S(2)}) collective-permute-start(f32[376,128]{1,0:T(8,128)S(1)} %get-tuple-element.49.refs_5_), channel_id=1, source_target_pairs={{0,8},{8,16},{16,24},{24,32},{32,40},{40,48},{48,56},{56,64},{64,7... | collective-permute-start | bytes 577544 | tf_op jit(solution)/shard_map/ppermute | solution.py:726
  20.7 14.0 %collective-permute-start.1 = (f32[376,128]{1,0:T(8,128)S(1)}, f32[376,128]{1,0:T(8,128)S(1)}, u32[]{:S(2)}, u32[]{:S(2)}) collective-permute-start(f32[376,128]{1,0:T(8,128)S(1)} %get-tuple-element.48), channel_id=1, source_target_pairs={{0,120},{8,0},{16,8},{24,16},{32,24},{40,32},{48,40},{56,48},{64,5... | collective-permute-start | bytes 577544 | tf_op jit(solution)/shard_map/ppermute | solution.py:726
  25.5 2.2 %copy-start = (f32[2048,512]{1,0:T(8,128)S(1)}, f32[2048,512]{1,0:T(8,128)}, u32[]{:S(2)}) copy-start(f32[2048,512]{1,0:T(8,128)} %refs_4_.5) | copy-start | bytes 12582916
  27.7 15.5 %copy-start.1 = (f32[2048,512]{1,0:T(8,128)S(1)}, f32[2048,512]{1,0:T(8,128)}, u32[]{:S(2)}) copy-start(f32[2048,512]{1,0:T(8,128)} %refs_4_.5) | copy-start | bytes 12582916
  38.3 13.7 %collective-permute-start.2 = (f32[264,128]{1,0:T(8,128)S(1)}, f32[264,128]{1,0:T(8,128)S(1)}, u32[]{:S(2)}, u32[]{:S(2)}) collective-permute-start(f32[264,128]{1,0:T(8,128)S(1)} %get-tuple-element.29), channel_id=1, source_target_pairs={{0,8},{8,16},{16,24},{24,32},{32,40},{40,48},{48,56},{56,64},{64,7... | collective-permute-start | bytes 405512 | tf_op jit(solution)/shard_map/ppermute | solution.py:726
  38.4 13.6 %collective-permute-start.3 = (f32[264,128]{1,0:T(8,128)S(1)}, f32[264,128]{1,0:T(8,128)S(1)}, u32[]{:S(2)}, u32[]{:S(2)}) collective-permute-start(f32[264,128]{1,0:T(8,128)S(1)} %get-tuple-element.30), channel_id=1, source_target_pairs={{0,120},{8,0},{16,8},{24,16},{32,24},{40,32},{48,40},{56,48},{64,5... | collective-permute-start | bytes 405512 | tf_op jit(solution)/shard_map/ppermute | solution.py:726
  53.0 17.4 %all-to-all-start.1 = ((f32[8,72,128]{2,1,0:T(8,128)}), f32[8,72,128]{2,1,0:T(8,128)S(1)}, u32[]{:S(2)}, u32[]{:S(2)}) async-start(f32[8,72,128]{2,1,0:T(8,128)} %pad_maximum_fusion.refs_5_), calls=%async_computation.1 | async-start | bytes 589824 | tf_op jit(solution)/shard_map/all_to_all | solution.py:785
  59.4 2.2 %copy-start.2 = (f32[2048,512]{1,0:T(8,128)S(1)}, f32[2048,512]{1,0:T(8,128)}, u32[]{:S(2)}) copy-start(f32[2048,512]{1,0:T(8,128)} %refs_4_.5) | copy-start | bytes 12582916
  61.6 8.8 %copy-start.4 = (f32[128,256]{1,0:T(8,128)S(1)}, f32[128,256]{1,0:T(8,128)}, u32[]{:S(2)}) copy-start(f32[128,256]{1,0:T(8,128)} %bed_ref.3) | copy-start | bytes 393220
  61.6 8.9 %copy-start.5 = (f32[128,256]{1,0:T(8,128)S(1)}, f32[128,256]{1,0:T(8,128)}, u32[]{:S(2)}) copy-start(f32[128,256]{1,0:T(8,128)} %rough_ref.3) | copy-start | bytes 393220
  61.6 8.9 %copy-start.9 = (s32[1,2048]{1,0:T(1,128)S(1)}, s32[1,2048]{1,0:T(1,128)}, u32[]{:S(2)}) copy-start(s32[1,2048]{1,0:T(1,128)} %get-tuple-element.39.slot_ref) | copy-start | bytes 24580

commit v7 on v6

--- a/solution.py
+++ b/solution.py
@@ -717,7 +717,7 @@
             transcendentals=inner * TILE * 512 * 8,
         ),
         name="cells",
-    )(soil, *kinds, near, pressure, after, *extra)
+    )(soil, *kinds, near, pltpu.with_memory_space_constraint(pressure, pltpu.HBM), after, *extra)
 
 
 def shifted(value, axis, steps, wrap=True):

time: 75.3 us -> 72.4 us (0.961)
  local copies, waits for them, and re-layouts: 5.82 us -> 1.45 us
  Pallas kernels: 36.3 us -> 38.5 us
  other arithmetic: 2.71 us -> 1.9 us
    unnamed x26 -> x20, local copies, waits for them, and re-layouts: 4.41 us -> 0.04 us
    pallas_call x3, Pallas kernels: 24.6 us -> 26.8 us  [cells(): pl.pallas_call(functools.partial(cells_kernel, low, inner, tiles, shape[1...]
    concatenate x2, other arithmetic: 1.68 us -> 0.87 us  [edge(): return jnp.concatenate([later[part], classes], axis=0)]
  transfers between devices with their start and end apart: 8 -> 8, of which waited for: 0 -> 0; matrix products, arithmetic and copies ran while one was open for 5% -> 5% of each run, Pallas kernels for 38% -> 42%
where the time goes in v7:
time: 72.4 us; the launch traced here: 71.9 us
  Pallas kernels  38.5 us (53%)
  starting transfers between devices  28.9 us (40%)
  other arithmetic  1.9 us (3%)
  local copies, waits for them, and re-layouts  1.45 us (2%)
  between operations  1.15 us (2%)
    pallas_call x3, Pallas kernels, cells(): pl.pallas_call(functools.partial(cells_kernel, low, inner, tiles, shape[1...  26.8 us
    ppermute x6, starting transfers between devices, shifted(): return lax.ppermute(value, axis, pairs)  16.4 us
    all_to_all x1, starting transfers between devices, per_device(): returned = lax.all_to_all(reply, 'gy', 0, 0)  6.37 us
    all_to_all x1, starting transfers between devices, per_device(): got = lax.all_to_all(send, 'gy', 0, 0)  6.11 us
    pallas_call x1, Pallas kernels, finish(): pl.pallas_call(functools.partial(sweep_kernel, place), in_specs=[VMEM] *...  4.16 us
    pallas_call x1, Pallas kernels, route(): pl.pallas_call(functools.partial(route_kernel, shape), grid=(1,), in_spec...  3.92 us
    pallas_call x1, Pallas kernels, surface(): pl.pallas_call(functools.partial(surface_kernel, shape), in_specs=[SMEM,...  3.62 us
  transfers between devices with their start and end apart: 8, of which 0 were waited for; matrix products, arithmetic and copies ran while one was open for 5% of the time, Pallas kernels for 42%

profile of v7, /device:TPU:1, one launch (start us, length us, event | category | flops | bytes accessed | tf_op | source)
XLA Modules:
  0.0 71.9 jit_solution(3519431784943199265)
XLA Ops:
  0.6 0.0 copy-start.3
  0.6 0.0 copy-start.7
  0.7 0.0 copy-start.8
  0.7 3.9 %route.1 = (f32[8,88,128]{2,1,0:T(8,128)}, s32[1,2048]{1,0:T(1,128)}, f32[2,24,128]{2,1,0:T(8,128)}) custom-call(s32[1,2048]{1,0:T(1,128)} %bitcast.22, s32[1,2048]{1,0:T(1,128)} %bitcast.26, s32[1,2048]{1,0:T(1,128)} %bitcast.35, f32[2048,512]{1,0:T(8,128)} %refs_4_.5, f32[128,256]{1,0:T(8,128)} %depth_ref.5, f32[128,256]{1,0:T(8,128)} %bed_ref.3, ...), custom_call_target="tpu_custom_call" | custom-call | tf_op jit(solution)/shard_map/route/pallas_call | solution.py:175
  4.6 0.0 copy-start.9
  4.6 0.0 copy-start.4
  4.6 0.0 copy-start.5
  4.6 6.1 %all-to-all-start = ((f32[8,88,128]{2,1,0:T(8,128)}), f32[8,88,128]{2,1,0:T(8,128)S(1)}, u32[]{:S(2)}, u32[]{:S(2)}) async-start(f32[8,88,128]{2,1,0:T(8,128)} %get-tuple-element.25), calls=%async_computation | async-start | bytes 720896 | tf_op jit(solution)/shard_map/all_to_all | solution.py:752
  10.7 1.3 %fusion = (f32[256,512]{1,0:T(8,128)S(1)}, f32[256,512]{1,0:T(8,128)S(1)}) fusion(f32[2048,512]{1,0:T(8,128)} %refs_4_.5), kind=kLoop, calls=%fused_computation.25 | loop fusion | bytes 2097152 | tf_op jit(solution)/shard_map/slice | solution.py:748
  12.0 0.0 copy-done.3
  12.0 0.0 copy-start
  12.0 0.8 %select_maximum_fusion.1 = f32[264,512]{1,0:T(8,128)} fusion(f32[1,256]{1,0:T(1,128)S(1)} %bitcast.37, f32[256,512]{1,0:T(8,128)S(1)} %get-tuple-element.47), kind=kLoop, calls=%fused_computation.1 | loop fusion | flops 405504 | bytes 1065984 | tf_op jit(solution)/shard_map/concatenate | solution.py:748
  12.8 3.5 %collective-permute-start.4 = (f32[264,512]{1,0:T(8,128)}, f32[264,512]{1,0:T(8,128)S(1)}, u32[]{:S(2)}, u32[]{:S(2)}) collective-permute-start(f32[264,512]{1,0:T(8,128)} %select_maximum_fusion.1), channel_id=1, source_target_pairs={{0,1},{1,2},{2,3},{3,4},{4,5},{5,6},{6,7},{7,8},{8,9},{9,10},{10,1... | collective-permute-start | bytes 1622024 | tf_op jit(solution)/shard_map/ppermute | solution.py:726
  16.4 1.9 %collective-permute-start.5 = (f32[264,512]{1,0:T(8,128)S(1)}, f32[264,512]{1,0:T(8,128)S(1)}, u32[]{:S(2)}, u32[]{:S(2)}) collective-permute-start(f32[264,512]{1,0:T(8,128)S(1)} %select_maximum_fusion), channel_id=1, source_target_pairs={{1,0},{2,1},{3,2},{4,3},{5,4},{6,5},{7,6},{8,7},{9,8},{10,9},{11,1... | collective-permute-start | bytes 1622024 | tf_op jit(solution)/shard_map/ppermute | solution.py:726
  18.4 0.0 copy-done.9
  18.4 0.1 pad.21.clone
  18.5 0.0 copy-done.7
  18.5 0.0 copy-done.8
  18.5 0.0 all-to-all-done.got_ref
  18.6 1.3 %collective-permute-start = (f32[376,128]{1,0:T(8,128)S(1)}, f32[376,128]{1,0:T(8,128)S(1)}, u32[]{:S(2)}, u32[]{:S(2)}) collective-permute-start(f32[376,128]{1,0:T(8,128)S(1)} %get-tuple-element.49.refs_5_), channel_id=1, source_target_pairs={{0,8},{8,16},{16,24},{24,32},{32,40},{40,48},{48,56},{56,64},{64,7... | collective-permute-start | bytes 577544 | tf_op jit(solution)/shard_map/ppermute | solution.py:726
  19.9 4.8 %collective-permute-start.1 = (f32[376,128]{1,0:T(8,128)S(1)}, f32[376,128]{1,0:T(8,128)S(1)}, u32[]{:S(2)}, u32[]{:S(2)}) collective-permute-start(f32[376,128]{1,0:T(8,128)S(1)} %get-tuple-element.48), channel_id=1, source_target_pairs={{0,120},{8,0},{16,8},{24,16},{32,24},{40,32},{48,40},{56,48},{64,5... | collective-permute-start | bytes 577544 | tf_op jit(solution)/shard_map/ppermute | solution.py:726
  24.7 0.0 copy-done.4
  24.7 0.0 copy-done.5
  24.7 7.8 %cells.3 = (f32[2048,512]{1,0:T(8,128)}, f32[4,64,128]{2,1,0:T(8,128)S(1)}) custom-call(f32[5,12]{1,0:T(8,128)S(1)} %copy-done.5, s32[1,2048]{1,0:T(1,128)S(1)} %bitcast.23, s32[1,2048]{1,0:T(1,128)S(1)} %bitcast.27, s32[12,2048]{1,0:T(8,128)S(1)} %pad_add_fusion.refs_3_, f32[2048,512]{1,0:T(8,128)} %refs_4_.5, f32[376,128]{1,0:T(8,128)S(1)} %get-tuple-element.49.refs_5_), custom_call_target="tpu_custom_call" | custom-call | flops 1207959552 | bytes 4194304 | tf_op jit(solution)/shard_map/cells/pallas_call | solution.py:685
  32.6 0.0 collective-permute-done.up_ref
  32.6 0.0 collective-permute-done.1.down_ref
  32.6 0.0 copy-done
  32.6 3.6 %surface.1 = (f32[8,32,128]{2,1,0:T(8,128)S(1)}, f32[264,128]{1,0:T(8,128)S(1)}, f32[264,128]{1,0:T(8,128)S(1)}, f32[128,256]{1,0:T(8,128)S(1)}, f32[2,8,128]{2,1,0:T(8,128)S(1)}) custom-call(f32[5,12]{1,0:T(8,128)S(1)} %copy-done.5, f32[8,88,128]{2,1,0:T(8,128)S(1)} %all-to-all-done.got_ref, f32[376,128]{1,0:T(8,128)S(1)} %collective-permute-done.up_ref, ...), custom_call_target="tpu_custom_call" | custom-call | tf_op jit(solution)/shard_map/surface/pallas_call | solution.py:293
  36.2 0.1 collective-permute-start.2
  36.3 4.8 %collective-permute-start.3 = (f32[264,128]{1,0:T(8,128)S(1)}, f32[264,128]{1,0:T(8,128)S(1)}, u32[]{:S(2)}, u32[]{:S(2)}) collective-permute-start(f32[264,128]{1,0:T(8,128)S(1)} %get-tuple-element.30), channel_id=1, source_target_pairs={{0,120},{8,0},{16,8},{24,16},{32,24},{40,32},{48,40},{56,48},{64,5... | collective-permute-start | bytes 405512 | tf_op jit(solution)/shard_map/ppermute | solution.py:726
  41.1 0.0 collective-permute-done.4.refs_6_
  41.1 9.3 %cells.4 = (f32[2048,512]{1,0:T(8,128)}, f32[6,64,128]{2,1,0:T(8,128)S(1)}) custom-call(f32[5,12]{1,0:T(8,128)S(1)} %copy-done.5, s32[1,2048]{1,0:T(1,128)S(1)} %bitcast.24, s32[1,2048]{1,0:T(1,128)S(1)} %bitcast.28, s32[12,2048]{1,0:T(8,128)S(1)} %pad_add_fusion.refs_3_, f32[2048,512]{1,0:T(8,128)} %refs_4_.5, ...), custom_call_target="tpu_custom_call", output_to_operand_aliasing={{0}: (7, {})} | custom-call | flops 1811939328 | bytes 6291456 | tf_op jit(solution)/shard_map/cells/pallas_call | solution.py:685
  50.4 0.0 collective-permute-done.2.low_ref
  50.4 0.0 collective-permute-done.3.high_ref
  50.4 0.1 maximum_maximum_fusion
  50.5 0.1 broadcast_select_fusion.1
  50.6 0.1 broadcast_select_fusion
  50.7 0.7 %pad_maximum_fusion.refs_5_ = f32[8,72,128]{2,1,0:T(8,128)} fusion(f32[8,8,128]{2,1,0:T(8,128)S(1)} %broadcast_select_fusion.1, f32[8,32,128]{2,1,0:T(8,128)S(1)} %broadcast_select_fusion, f32[8,32,128]{2,1,0:T(8,128)S(1)} %get-tuple-element.31.refs_5_), kind=kLoop, calls=%fused_computation.3 | loop fusion | flops 147456 | bytes 589824 | tf_op jit(solution)/shard_map/concatenate | solution.py:784
  51.4 6.4 %all-to-all-start.1 = ((f32[8,72,128]{2,1,0:T(8,128)}), f32[8,72,128]{2,1,0:T(8,128)S(1)}, u32[]{:S(2)}, u32[]{:S(2)}) async-start(f32[8,72,128]{2,1,0:T(8,128)} %pad_maximum_fusion.refs_5_), calls=%async_computation.1 | async-start | bytes 589824 | tf_op jit(solution)/shard_map/all_to_all | solution.py:785
  57.8 0.0 collective-permute-done.5.refs_6_
  57.8 0.0 copy-start.2
  57.8 0.0 copy-start.6
  57.8 9.7 %cells.5 = (f32[2048,512]{1,0:T(8,128)}, f32[6,64,128]{2,1,0:T(8,128)S(1)}) custom-call(f32[5,12]{1,0:T(8,128)S(1)} %copy-done.5, s32[1,2048]{1,0:T(1,128)S(1)} %bitcast.25, s32[1,2048]{1,0:T(1,128)S(1)} %bitcast.29, s32[12,2048]{1,0:T(8,128)S(1)} %pad_add_fusion.refs_3_, f32[2048,512]{1,0:T(8,128)} %refs_4_.5, ...), custom_call_target="tpu_custom_call", output_to_operand_aliasing={{0}: (7, {})} | custom-call | flops 1811939328 | bytes 6291456 | tf_op jit(solution)/shard_map/cells/pallas_call | solution.py:685
  67.5 0.0 all-to-all-done.1.back_ref
  67.5 0.0 copy-done.1
  67.5 0.0 copy-done.2
  67.5 0.0 copy-done.6
  67.5 4.2 %finish.1 = (f32[128,256]{1,0:T(8,128)}, f32[2048,512]{1,0:T(8,128)}) custom-call(f32[128,256]{1,0:T(8,128)S(1)} %copy-done, f32[128,256]{1,0:T(8,128)S(1)} %copy-done.1, f32[128,256]{1,0:T(8,128)S(1)} %copy-done.2, f32[8,88,128]{2,1,0:T(8,128)S(1)} %all-to-all-done.got_ref, ...), custom_call_target="tpu_custom_call", output_to_operand_aliasing={{1}: (14, {})} | custom-call | tf_op jit(solution)/shard_map/finish/pallas_call | solution.py:433
  (16 shorter events, 0.2 us)
Async XLA Ops:
  0.6 11.3 %copy-start.3 = (s32[2048]{0:T(1024)S(1)}, s32[2048]{0:T(1024)}, u32[]{:S(2)}) copy-start(s32[2048]{0:T(1024)} %param.11) | copy-start | bytes 24580
  0.6 17.8 %copy-start.7 = (s32[2048,6]{0,1:T(8,128)S(1)}, s32[2048,6]{0,1:T(8,128)}, u32[]{:S(2)}) copy-start(s32[2048,6]{0,1:T(8,128)} %param.14) | copy-start | bytes 147460
  0.7 17.8 %copy-start.8 = (s32[2048,6]{0,1:T(8,128)S(1)}, s32[2048,6]{0,1:T(8,128)}, u32[]{:S(2)}) copy-start(s32[2048,6]{0,1:T(8,128)} %param.13) | copy-start | bytes 147460
  4.6 13.8 %copy-start.9 = (f32[2,24,128]{2,1,0:T(8,128)S(1)}, f32[2,24,128]{2,1,0:T(8,128)}, u32[]{:S(2)}) copy-start(f32[2,24,128]{2,1,0:T(8,128)} %get-tuple-element.26) | copy-start | bytes 73732
  4.6 20.1 %copy-start.4 = (s32[2048]{0:T(1024)S(1)}, s32[2048]{0:T(1024)}, u32[]{:S(2)}) copy-start(s32[2048]{0:T(1024)} %param.12) | copy-start | bytes 24580
  4.6 20.1 %copy-start.5 = (f32[5,12]{1,0:T(8,128)S(1)}, f32[5,12]{1,0:T(8,128)}, u32[]{:S(2)}) copy-start(f32[5,12]{1,0:T(8,128)} %refs_0_.5) | copy-start | bytes 724
  4.6 13.9 %all-to-all-start = ((f32[8,88,128]{2,1,0:T(8,128)}), f32[8,88,128]{2,1,0:T(8,128)S(1)}, u32[]{:S(2)}, u32[]{:S(2)}) async-start(f32[8,88,128]{2,1,0:T(8,128)} %get-tuple-element.25), calls=%async_computation | async-start | bytes 720896 | tf_op jit(solution)/shard_map/all_to_all | solution.py:752
  12.0 20.6 %copy-start = (f32[128,256]{1,0:T(8,128)S(1)}, f32[128,256]{1,0:T(8,128)}, u32[]{:S(2)}) copy-start(f32[128,256]{1,0:T(8,128)} %depth_ref.5) | copy-start | bytes 393220
  12.8 28.2 %collective-permute-start.4 = (f32[264,512]{1,0:T(8,128)}, f32[264,512]{1,0:T(8,128)S(1)}, u32[]{:S(2)}, u32[]{:S(2)}) collective-permute-start(f32[264,512]{1,0:T(8,128)} %select_maximum_fusion.1), channel_id=1, source_target_pairs={{0,1},{1,2},{2,3},{3,4},{4,5},{5,6},{6,7},{7,8},{8,9},{9,10},{10,1... | collective-permute-start | bytes 1622024 | tf_op jit(solution)/shard_map/ppermute | solution.py:726
  16.4 41.4 %collective-permute-start.5 = (f32[264,512]{1,0:T(8,128)S(1)}, f32[264,512]{1,0:T(8,128)S(1)}, u32[]{:S(2)}, u32[]{:S(2)}) collective-permute-start(f32[264,512]{1,0:T(8,128)S(1)} %select_maximum_fusion), channel_id=1, source_target_pairs={{1,0},{2,1},{3,2},{4,3},{5,4},{6,5},{7,6},{8,7},{9,8},{10,9},{11,1... | collective-permute-start | bytes 1622024 | tf_op jit(solution)/shard_map/ppermute | solution.py:726
  18.6 13.9 %collective-permute-start = (f32[376,128]{1,0:T(8,128)S(1)}, f32[376,128]{1,0:T(8,128)S(1)}, u32[]{:S(2)}, u32[]{:S(2)}) collective-permute-start(f32[376,128]{1,0:T(8,128)S(1)} %get-tuple-element.49.refs_5_), channel_id=1, source_target_pairs={{0,8},{8,16},{16,24},{24,32},{32,40},{40,48},{48,56},{56,64},{64,7... | collective-permute-start | bytes 577544 | tf_op jit(solution)/shard_map/ppermute | solution.py:726
  19.9 12.7 %collective-permute-start.1 = (f32[376,128]{1,0:T(8,128)S(1)}, f32[376,128]{1,0:T(8,128)S(1)}, u32[]{:S(2)}, u32[]{:S(2)}) collective-permute-start(f32[376,128]{1,0:T(8,128)S(1)} %get-tuple-element.48), channel_id=1, source_target_pairs={{0,120},{8,0},{16,8},{24,16},{32,24},{40,32},{48,40},{56,48},{64,5... | collective-permute-start | bytes 577544 | tf_op jit(solution)/shard_map/ppermute | solution.py:726
  36.2 14.2 %collective-permute-start.2 = (f32[264,128]{1,0:T(8,128)S(1)}, f32[264,128]{1,0:T(8,128)S(1)}, u32[]{:S(2)}, u32[]{:S(2)}) collective-permute-start(f32[264,128]{1,0:T(8,128)S(1)} %get-tuple-element.29), channel_id=1, source_target_pairs={{0,8},{8,16},{16,24},{24,32},{32,40},{40,48},{48,56},{56,64},{64,7... | collective-permute-start | bytes 405512 | tf_op jit(solution)/shard_map/ppermute | solution.py:726
  36.3 14.1 %collective-permute-start.3 = (f32[264,128]{1,0:T(8,128)S(1)}, f32[264,128]{1,0:T(8,128)S(1)}, u32[]{:S(2)}, u32[]{:S(2)}) collective-permute-start(f32[264,128]{1,0:T(8,128)S(1)} %get-tuple-element.30), channel_id=1, source_target_pairs={{0,120},{8,0},{16,8},{24,16},{32,24},{40,32},{48,40},{56,48},{64,5... | collective-permute-start | bytes 405512 | tf_op jit(solution)/shard_map/ppermute | solution.py:726
  51.4 16.1 %all-to-all-start.1 = ((f32[8,72,128]{2,1,0:T(8,128)}), f32[8,72,128]{2,1,0:T(8,128)S(1)}, u32[]{:S(2)}, u32[]{:S(2)}) async-start(f32[8,72,128]{2,1,0:T(8,128)} %pad_maximum_fusion.refs_5_), calls=%async_computation.1 | async-start | bytes 589824 | tf_op jit(solution)/shard_map/all_to_all | solution.py:785
  57.8 9.7 %copy-start.1 = (f32[128,256]{1,0:T(8,128)S(1)}, f32[128,256]{1,0:T(8,128)}, u32[]{:S(2)}) copy-start(f32[128,256]{1,0:T(8,128)} %bed_ref.3) | copy-start | bytes 393220
  57.8 9.7 %copy-start.2 = (f32[128,256]{1,0:T(8,128)S(1)}, f32[128,256]{1,0:T(8,128)}, u32[]{:S(2)}) copy-start(f32[128,256]{1,0:T(8,128)} %rough_ref.3) | copy-start | bytes 393220
  57.8 9.7 %copy-start.6 = (s32[1,2048]{1,0:T(1,128)S(1)}, s32[1,2048]{1,0:T(1,128)}, u32[]{:S(2)}) copy-start(s32[1,2048]{1,0:T(1,128)} %get-tuple-element.39.slot_ref) | copy-start | bytes 24580

commit v8 on v7

--- a/solution.py
+++ b/solution.py
@@ -14,7 +14,7 @@
 
 HB = 256
 TILE = 256
-PARTS = ((0, 3), (3, 2), (5, 3))
+PARTS = ((0, 2), (2, 3), (5, 3))
 SLOTS = 64
 GROUPS = 16
 STORAGE = 0.05

time: 72.4 us -> 72.7 us (level)
  no operation moved by 1% of the time
where the time goes in v8:
time: 72.7 us; the launch traced here: 72.1 us
  Pallas kernels  38.4 us (53%)
  starting transfers between devices  29.2 us (40%)
  other arithmetic  1.9 us (3%)
  local copies, waits for them, and re-layouts  1.45 us (2%)
  between operations  1.14 us (2%)
    pallas_call x3, Pallas kernels, cells(): pl.pallas_call(functools.partial(cells_kernel, low, inner, tiles, shape[1...  26.8 us
    ppermute x6, starting transfers between devices, shifted(): return lax.ppermute(value, axis, pairs)  16.7 us
    all_to_all x1, starting transfers between devices, per_device(): returned = lax.all_to_all(reply, 'gy', 0, 0)  6.39 us
    all_to_all x1, starting transfers between devices, per_device(): got = lax.all_to_all(send, 'gy', 0, 0)  6.11 us
    pallas_call x1, Pallas kernels, finish(): pl.pallas_call(functools.partial(sweep_kernel, place), in_specs=[VMEM] *...  4.15 us
    pallas_call x1, Pallas kernels, route(): pl.pallas_call(functools.partial(route_kernel, shape), grid=(1,), in_spec...  3.92 us
    pallas_call x1, Pallas kernels, surface(): pl.pallas_call(functools.partial(surface_kernel, shape), in_specs=[SMEM,...  3.61 us
  transfers between devices with their start and end apart: 8, of which 0 were waited for; matrix products, arithmetic and copies ran while one was open for 5% of the time, Pallas kernels for 42%

profile of v8, /device:TPU:1, one launch (start us, length us, event | category | flops | bytes accessed | tf_op | source)
XLA Modules:
  0.0 72.1 jit_solution(18333627361009532072)
XLA Ops:
  0.6 0.0 copy-start.3
  0.6 0.0 copy-start.7
  0.7 0.0 copy-start.8
  0.7 3.9 %route.1 = (f32[8,88,128]{2,1,0:T(8,128)}, s32[1,2048]{1,0:T(1,128)}, f32[2,24,128]{2,1,0:T(8,128)}) custom-call(s32[1,2048]{1,0:T(1,128)} %bitcast.22, s32[1,2048]{1,0:T(1,128)} %bitcast.26, s32[1,2048]{1,0:T(1,128)} %bitcast.35, f32[2048,512]{1,0:T(8,128)} %refs_4_.5, f32[128,256]{1,0:T(8,128)} %depth_ref.5, f32[128,256]{1,0:T(8,128)} %bed_ref.3, ...), custom_call_target="tpu_custom_call" | custom-call | tf_op jit(solution)/shard_map/route/pallas_call | solution.py:175
  4.6 0.0 copy-start.9
  4.6 0.0 copy-start.4
  4.6 0.0 copy-start.5
  4.6 6.1 %all-to-all-start = ((f32[8,88,128]{2,1,0:T(8,128)}), f32[8,88,128]{2,1,0:T(8,128)S(1)}, u32[]{:S(2)}, u32[]{:S(2)}) async-start(f32[8,88,128]{2,1,0:T(8,128)} %get-tuple-element.25), calls=%async_computation | async-start | bytes 720896 | tf_op jit(solution)/shard_map/all_to_all | solution.py:752
  10.7 1.3 %fusion = (f32[256,512]{1,0:T(8,128)S(1)}, f32[256,512]{1,0:T(8,128)S(1)}) fusion(f32[2048,512]{1,0:T(8,128)} %refs_4_.5), kind=kLoop, calls=%fused_computation.25 | loop fusion | bytes 2097152 | tf_op jit(solution)/shard_map/slice | solution.py:748
  12.0 0.0 copy-done.3
  12.0 0.8 %select_maximum_fusion.1 = f32[264,512]{1,0:T(8,128)} fusion(f32[1,256]{1,0:T(1,128)S(1)} %bitcast.37, f32[256,512]{1,0:T(8,128)S(1)} %get-tuple-element.47), kind=kLoop, calls=%fused_computation.1 | loop fusion | flops 405504 | bytes 1065984 | tf_op jit(solution)/shard_map/concatenate | solution.py:748
  12.8 3.5 %collective-permute-start.4 = (f32[264,512]{1,0:T(8,128)}, f32[264,512]{1,0:T(8,128)S(1)}, u32[]{:S(2)}, u32[]{:S(2)}) collective-permute-start(f32[264,512]{1,0:T(8,128)} %select_maximum_fusion.1), channel_id=1, source_target_pairs={{0,1},{1,2},{2,3},{3,4},{4,5},{5,6},{6,7},{7,8},{8,9},{9,10},{10,1... | collective-permute-start | bytes 1622024 | tf_op jit(solution)/shard_map/ppermute | solution.py:726
  16.4 0.0 copy-start
  16.4 2.1 %collective-permute-start.5 = (f32[264,512]{1,0:T(8,128)S(1)}, f32[264,512]{1,0:T(8,128)S(1)}, u32[]{:S(2)}, u32[]{:S(2)}) collective-permute-start(f32[264,512]{1,0:T(8,128)S(1)} %select_maximum_fusion), channel_id=1, source_target_pairs={{1,0},{2,1},{3,2},{4,3},{5,4},{6,5},{7,6},{8,7},{9,8},{10,9},{11,1... | collective-permute-start | bytes 1622024 | tf_op jit(solution)/shard_map/ppermute | solution.py:726
  18.5 0.0 copy-done.9
  18.5 0.0 copy-done.7
  18.5 0.0 copy-done.8
  18.6 0.0 all-to-all-done.got_ref
  18.7 1.3 %collective-permute-start = (f32[376,128]{1,0:T(8,128)S(1)}, f32[376,128]{1,0:T(8,128)S(1)}, u32[]{:S(2)}, u32[]{:S(2)}) collective-permute-start(f32[376,128]{1,0:T(8,128)S(1)} %get-tuple-element.49.refs_5_), channel_id=1, source_target_pairs={{0,8},{8,16},{16,24},{24,32},{32,40},{40,48},{48,56},{56,64},{64,7... | collective-permute-start | bytes 577544 | tf_op jit(solution)/shard_map/ppermute | solution.py:726
  20.0 4.8 %collective-permute-start.1 = (f32[376,128]{1,0:T(8,128)S(1)}, f32[376,128]{1,0:T(8,128)S(1)}, u32[]{:S(2)}, u32[]{:S(2)}) collective-permute-start(f32[376,128]{1,0:T(8,128)S(1)} %get-tuple-element.48), channel_id=1, source_target_pairs={{0,120},{8,0},{16,8},{24,16},{32,24},{40,32},{48,40},{56,48},{64,5... | collective-permute-start | bytes 577544 | tf_op jit(solution)/shard_map/ppermute | solution.py:726
  24.8 0.1 pad.21.clone
  24.9 0.0 copy-done.4
  24.9 0.0 copy-done.5
  24.9 9.7 %cells.3 = (f32[2048,512]{1,0:T(8,128)}, f32[6,64,128]{2,1,0:T(8,128)S(1)}) custom-call(f32[5,12]{1,0:T(8,128)S(1)} %copy-done.5, s32[1,2048]{1,0:T(1,128)S(1)} %bitcast.23, s32[1,2048]{1,0:T(1,128)S(1)} %bitcast.27, s32[12,2048]{1,0:T(8,128)S(1)} %pad_add_fusion.refs_3_, f32[2048,512]{1,0:T(8,128)} %refs_4_.5, f32[376,128]{1,0:T(8,128)S(1)} %get-tuple-element.49.refs_5_), custom_call_target="tpu_custom_call" | custom-call | flops 1811939328 | bytes 6291456 | tf_op jit(solution)/shard_map/cells/pallas_call | solution.py:685
  34.5 0.0 collective-permute-done.up_ref
  34.5 0.0 collective-permute-done.1.down_ref
  34.6 0.0 copy-done
  34.6 3.6 %surface.1 = (f32[8,32,128]{2,1,0:T(8,128)S(1)}, f32[264,128]{1,0:T(8,128)S(1)}, f32[264,128]{1,0:T(8,128)S(1)}, f32[128,256]{1,0:T(8,128)S(1)}, f32[2,8,128]{2,1,0:T(8,128)S(1)}) custom-call(f32[5,12]{1,0:T(8,128)S(1)} %copy-done.5, f32[8,88,128]{2,1,0:T(8,128)S(1)} %all-to-all-done.got_ref, f32[376,128]{1,0:T(8,128)S(1)} %collective-permute-done.up_ref, ...), custom_call_target="tpu_custom_call" | custom-call | tf_op jit(solution)/shard_map/surface/pallas_call | solution.py:293
  38.2 0.3 collective-permute-start.2
  38.4 4.8 %collective-permute-start.3 = (f32[264,128]{1,0:T(8,128)S(1)}, f32[264,128]{1,0:T(8,128)S(1)}, u32[]{:S(2)}, u32[]{:S(2)}) collective-permute-start(f32[264,128]{1,0:T(8,128)S(1)} %get-tuple-element.30), channel_id=1, source_target_pairs={{0,120},{8,0},{16,8},{24,16},{32,24},{40,32},{48,40},{56,48},{64,5... | collective-permute-start | bytes 405512 | tf_op jit(solution)/shard_map/ppermute | solution.py:726
  43.2 0.0 collective-permute-done.4.refs_6_
  43.2 7.4 %cells.4 = (f32[2048,512]{1,0:T(8,128)}, f32[4,64,128]{2,1,0:T(8,128)S(1)}) custom-call(f32[5,12]{1,0:T(8,128)S(1)} %copy-done.5, s32[1,2048]{1,0:T(1,128)S(1)} %bitcast.24, s32[1,2048]{1,0:T(1,128)S(1)} %bitcast.28, s32[12,2048]{1,0:T(8,128)S(1)} %pad_add_fusion.refs_3_, f32[2048,512]{1,0:T(8,128)} %refs_4_.5, ...), custom_call_target="tpu_custom_call", output_to_operand_aliasing={{0}: (7, {})} | custom-call | flops 1207959552 | bytes 4194304 | tf_op jit(solution)/shard_map/cells/pallas_call | solution.py:685
  50.7 0.0 collective-permute-done.2.low_ref
  50.7 0.0 collective-permute-done.3.high_ref
  50.7 0.1 maximum_maximum_fusion
  50.8 0.1 broadcast_select_fusion.1
  50.9 0.1 broadcast_select_fusion
  51.0 0.7 %pad_maximum_fusion.refs_5_ = f32[8,72,128]{2,1,0:T(8,128)} fusion(f32[8,8,128]{2,1,0:T(8,128)S(1)} %broadcast_select_fusion.1, f32[8,32,128]{2,1,0:T(8,128)S(1)} %broadcast_select_fusion, f32[8,32,128]{2,1,0:T(8,128)S(1)} %get-tuple-element.31.refs_5_), kind=kLoop, calls=%fused_computation.3 | loop fusion | flops 147456 | bytes 589824 | tf_op jit(solution)/shard_map/concatenate | solution.py:784
  51.7 6.4 %all-to-all-start.1 = ((f32[8,72,128]{2,1,0:T(8,128)}), f32[8,72,128]{2,1,0:T(8,128)S(1)}, u32[]{:S(2)}, u32[]{:S(2)}) async-start(f32[8,72,128]{2,1,0:T(8,128)} %pad_maximum_fusion.refs_5_), calls=%async_computation.1 | async-start | bytes 589824 | tf_op jit(solution)/shard_map/all_to_all | solution.py:785
  58.1 0.0 collective-permute-done.5.refs_6_
  58.1 0.0 copy-start.2
  58.1 0.0 copy-start.6
  58.1 9.7 %cells.5 = (f32[2048,512]{1,0:T(8,128)}, f32[6,64,128]{2,1,0:T(8,128)S(1)}) custom-call(f32[5,12]{1,0:T(8,128)S(1)} %copy-done.5, s32[1,2048]{1,0:T(1,128)S(1)} %bitcast.25, s32[1,2048]{1,0:T(1,128)S(1)} %bitcast.29, s32[12,2048]{1,0:T(8,128)S(1)} %pad_add_fusion.refs_3_, f32[2048,512]{1,0:T(8,128)} %refs_4_.5, ...), custom_call_target="tpu_custom_call", output_to_operand_aliasing={{0}: (7, {})} | custom-call | flops 1811939328 | bytes 6291456 | tf_op jit(solution)/shard_map/cells/pallas_call | solution.py:685
  67.8 0.0 all-to-all-done.1.back_ref
  67.8 0.0 copy-done.1
  67.8 0.0 copy-done.2
  67.8 0.0 copy-done.6
  67.8 4.1 %finish.1 = (f32[128,256]{1,0:T(8,128)}, f32[2048,512]{1,0:T(8,128)}) custom-call(f32[128,256]{1,0:T(8,128)S(1)} %copy-done, f32[128,256]{1,0:T(8,128)S(1)} %copy-done.1, f32[128,256]{1,0:T(8,128)S(1)} %copy-done.2, f32[8,88,128]{2,1,0:T(8,128)S(1)} %all-to-all-done.got_ref, ...), custom_call_target="tpu_custom_call", output_to_operand_aliasing={{1}: (14, {})} | custom-call | tf_op jit(solution)/shard_map/finish/pallas_call | solution.py:433
  (16 shorter events, 0.2 us)
Async XLA Ops:
  0.6 11.3 %copy-start.3 = (s32[2048]{0:T(1024)S(1)}, s32[2048]{0:T(1024)}, u32[]{:S(2)}) copy-start(s32[2048]{0:T(1024)} %param.11) | copy-start | bytes 24580
  0.6 17.9 %copy-start.7 = (s32[2048,6]{0,1:T(8,128)S(1)}, s32[2048,6]{0,1:T(8,128)}, u32[]{:S(2)}) copy-start(s32[2048,6]{0,1:T(8,128)} %param.14) | copy-start | bytes 147460
  0.7 17.9 %copy-start.8 = (s32[2048,6]{0,1:T(8,128)S(1)}, s32[2048,6]{0,1:T(8,128)}, u32[]{:S(2)}) copy-start(s32[2048,6]{0,1:T(8,128)} %param.13) | copy-start | bytes 147460
  4.6 13.9 %copy-start.9 = (f32[2,24,128]{2,1,0:T(8,128)S(1)}, f32[2,24,128]{2,1,0:T(8,128)}, u32[]{:S(2)}) copy-start(f32[2,24,128]{2,1,0:T(8,128)} %get-tuple-element.26) | copy-start | bytes 73732
  4.6 20.3 %copy-start.4 = (s32[2048]{0:T(1024)S(1)}, s32[2048]{0:T(1024)}, u32[]{:S(2)}) copy-start(s32[2048]{0:T(1024)} %param.12) | copy-start | bytes 24580
  4.6 20.3 %copy-start.5 = (f32[5,12]{1,0:T(8,128)S(1)}, f32[5,12]{1,0:T(8,128)}, u32[]{:S(2)}) copy-start(f32[5,12]{1,0:T(8,128)} %refs_0_.5) | copy-start | bytes 724
  4.6 14.0 %all-to-all-start = ((f32[8,88,128]{2,1,0:T(8,128)}), f32[8,88,128]{2,1,0:T(8,128)S(1)}, u32[]{:S(2)}, u32[]{:S(2)}) async-start(f32[8,88,128]{2,1,0:T(8,128)} %get-tuple-element.25), calls=%async_computation | async-start | bytes 720896 | tf_op jit(solution)/shard_map/all_to_all | solution.py:752
  12.8 30.4 %collective-permute-start.4 = (f32[264,512]{1,0:T(8,128)}, f32[264,512]{1,0:T(8,128)S(1)}, u32[]{:S(2)}, u32[]{:S(2)}) collective-permute-start(f32[264,512]{1,0:T(8,128)} %select_maximum_fusion.1), channel_id=1, source_target_pairs={{0,1},{1,2},{2,3},{3,4},{4,5},{5,6},{6,7},{7,8},{8,9},{9,10},{10,1... | collective-permute-start | bytes 1622024 | tf_op jit(solution)/shard_map/ppermute | solution.py:726
  16.4 18.2 %copy-start = (f32[128,256]{1,0:T(8,128)S(1)}, f32[128,256]{1,0:T(8,128)}, u32[]{:S(2)}) copy-start(f32[128,256]{1,0:T(8,128)} %depth_ref.5) | copy-start | bytes 393220
  16.4 41.7 %collective-permute-start.5 = (f32[264,512]{1,0:T(8,128)S(1)}, f32[264,512]{1,0:T(8,128)S(1)}, u32[]{:S(2)}, u32[]{:S(2)}) collective-permute-start(f32[264,512]{1,0:T(8,128)S(1)} %select_maximum_fusion), channel_id=1, source_target_pairs={{1,0},{2,1},{3,2},{4,3},{5,4},{6,5},{7,6},{8,7},{9,8},{10,9},{11,1... | collective-permute-start | bytes 1622024 | tf_op jit(solution)/shard_map/ppermute | solution.py:726
  18.7 15.9 %collective-permute-start = (f32[376,128]{1,0:T(8,128)S(1)}, f32[376,128]{1,0:T(8,128)S(1)}, u32[]{:S(2)}, u32[]{:S(2)}) collective-permute-start(f32[376,128]{1,0:T(8,128)S(1)} %get-tuple-element.49.refs_5_), channel_id=1, source_target_pairs={{0,8},{8,16},{16,24},{24,32},{32,40},{40,48},{48,56},{56,64},{64,7... | collective-permute-start | bytes 577544 | tf_op jit(solution)/shard_map/ppermute | solution.py:726
  20.0 14.6 %collective-permute-start.1 = (f32[376,128]{1,0:T(8,128)S(1)}, f32[376,128]{1,0:T(8,128)S(1)}, u32[]{:S(2)}, u32[]{:S(2)}) collective-permute-start(f32[376,128]{1,0:T(8,128)S(1)} %get-tuple-element.48), channel_id=1, source_target_pairs={{0,120},{8,0},{16,8},{24,16},{32,24},{40,32},{48,40},{56,48},{64,5... | collective-permute-start | bytes 577544 | tf_op jit(solution)/shard_map/ppermute | solution.py:726
  38.2 12.5 %collective-permute-start.2 = (f32[264,128]{1,0:T(8,128)S(1)}, f32[264,128]{1,0:T(8,128)S(1)}, u32[]{:S(2)}, u32[]{:S(2)}) collective-permute-start(f32[264,128]{1,0:T(8,128)S(1)} %get-tuple-element.29), channel_id=1, source_target_pairs={{0,8},{8,16},{16,24},{24,32},{32,40},{40,48},{48,56},{56,64},{64,7... | collective-permute-start | bytes 405512 | tf_op jit(solution)/shard_map/ppermute | solution.py:726
  38.4 12.2 %collective-permute-start.3 = (f32[264,128]{1,0:T(8,128)S(1)}, f32[264,128]{1,0:T(8,128)S(1)}, u32[]{:S(2)}, u32[]{:S(2)}) collective-permute-start(f32[264,128]{1,0:T(8,128)S(1)} %get-tuple-element.30), channel_id=1, source_target_pairs={{0,120},{8,0},{16,8},{24,16},{32,24},{40,32},{48,40},{56,48},{64,5... | collective-permute-start | bytes 405512 | tf_op jit(solution)/shard_map/ppermute | solution.py:726
  51.7 16.1 %all-to-all-start.1 = ((f32[8,72,128]{2,1,0:T(8,128)}), f32[8,72,128]{2,1,0:T(8,128)S(1)}, u32[]{:S(2)}, u32[]{:S(2)}) async-start(f32[8,72,128]{2,1,0:T(8,128)} %pad_maximum_fusion.refs_5_), calls=%async_computation.1 | async-start | bytes 589824 | tf_op jit(solution)/shard_map/all_to_all | solution.py:785
  58.1 9.7 %copy-start.1 = (f32[128,256]{1,0:T(8,128)S(1)}, f32[128,256]{1,0:T(8,128)}, u32[]{:S(2)}) copy-start(f32[128,256]{1,0:T(8,128)} %bed_ref.3) | copy-start | bytes 393220
  58.1 9.7 %copy-start.2 = (f32[128,256]{1,0:T(8,128)S(1)}, f32[128,256]{1,0:T(8,128)}, u32[]{:S(2)}) copy-start(f32[128,256]{1,0:T(8,128)} %rough_ref.3) | copy-start | bytes 393220
  58.1 9.7 %copy-start.6 = (s32[1,2048]{1,0:T(1,128)S(1)}, s32[1,2048]{1,0:T(1,128)}, u32[]{:S(2)}) copy-start(s32[1,2048]{1,0:T(1,128)} %get-tuple-element.39.slot_ref) | copy-start | bytes 24580
